TPU v7x, 32 devices: a whole 2x2x4 slice. The times are simulated.
32 devices in a mesh: nodes: 8 (over z, y), hid: 4 (over x, core).
Axes of the slice: x: 2, y: 2, z: 4, core: 2. Of those that a mesh axis runs over, the one named last changes fastest.
Arguments:
- states: float32 [32768, 512], P(('nodes', 'hid')), may hold values from -6 to 6
- condition: float32 [16], replicated, may hold values from -4 to 4
- mod_w: bfloat16 [16, 2048], replicated, may hold values from -0.5 to 0.5
- w_query: bfloat16 [512, 512], replicated, may hold values from -0.25 to 0.25
- w_key: bfloat16 [512, 512], replicated, may hold values from -0.25 to 0.25
- w_value: bfloat16 [512, 512], replicated, may hold values from -0.25 to 0.25
- w_out: bfloat16 [512, 512], replicated, may hold values from -1 to 1
- w_gate: bfloat16 [512, 2048], P(None, 'hid'), may hold values from -0.25 to 0.25
- w_up: bfloat16 [512, 2048], P(None, 'hid'), may hold values from -0.25 to 0.25
- w_down: bfloat16 [2048, 512], P('hid'), may hold values from -0.125 to 0.125
- counts: int32 [32], P(('nodes', 'hid')), may hold values from 512 to 1024, as said below
- send_rows: int32 [32, 4, 128], P(('nodes', 'hid')), may hold values from 0 to 1023, as said below
- neighbours: int32 [32768, 16], P(('nodes', 'hid')), may hold values from 0 to 1535
- cotangent: float32 [32768, 512], P(('nodes', 'hid')), may hold values from -6 to 6
Outputs:
- output: float32 [32768, 512], P(('nodes', 'hid'))
- grad_states: float32 [32768, 512], P(('nodes', 'hid'))
- grad_condition: float32 [16], replicated
- grad_mod_w: float32 [16, 2048], replicated
- grad_w_query: float32 [512, 512], replicated
- grad_w_key: float32 [512, 512], replicated
- grad_w_value: float32 [512, 512], replicated
- grad_w_out: float32 [512, 512], replicated
- grad_w_gate: float32 [512, 2048], P(None, 'hid')
- grad_w_up: float32 [512, 2048], P(None, 'hid')
- grad_w_down: float32 [2048, 512], P('hid')
Inputs may be any that keep to these rules, and one draw needn't show every extreme that they name: counts[d] is the number of mesh nodes of device d; its slots below counts[d] hold nodes, the rest are padding. send_rows[d, j, c] is below counts[d].
All inputs are finite; a program needn't handle non-finite values.
Results may differ from a plain program's by a relative error of at most 0.013.
Values may be sent and summed in bfloat16 or wider, within the bound.
No kernel may reach another device: no remote copies, remote signals or barrier semaphores. Data moves between devices by JAX's collectives and lax.ppermute only.
A program may use at most 192 MiB of HBM per device.

v0:
```python
import jax
import jax.numpy as jnp
from jax import lax
from jax.sharding import PartitionSpec as P

HEADS = 4
HEAD_DIM = 128
NEIGH = 16


epsilon = 1e-06
halo_steps = (1, -1, 2, -2)
highest = lax.Precision.HIGHEST


def from_behind(block, axis, distance):
    devices = range(lax.axis_size(axis))
    route = [((i - distance) % len(devices), i) for i in devices]
    return lax.ppermute(block, axis, route)


def matmul(left, right):
    return jnp.dot(left, right, preferred_element_type=jnp.float32)


def times_transposed(left, right):
    return lax.dot_general(
        left, right, (((1,), (1,)), ((), ())), preferred_element_type=jnp.float32
    )


def transposed_times(left, right):
    return lax.dot_general(
        left, right, (((0,), (0,)), ((), ())), preferred_element_type=jnp.float32
    )


def norm_parts(states):
    centred = states - jnp.mean(states, axis=-1, keepdims=True)
    inverse = lax.rsqrt(jnp.mean(centred * centred, axis=-1, keepdims=True) + epsilon)
    return (centred * inverse, inverse)


def norm_back(grad_plain, plain, inverse):
    first_mean = jnp.mean(grad_plain, axis=-1, keepdims=True)
    second_mean = jnp.mean(grad_plain * plain, axis=-1, keepdims=True)
    return inverse * (grad_plain - first_mean - plain * second_mean)


def silu_parts(gate):
    sigmoid = jax.nn.sigmoid(gate)
    return (gate * sigmoid, sigmoid * (1.0 + gate * (1.0 - sigmoid)))


def body(
    states,
    condition,
    mod_w,
    w_query,
    w_key,
    w_value,
    w_out,
    w_gate,
    w_up,
    w_down,
    counts,
    send_rows,
    neighbours,
    cotangent,
):
    slot_count, model_width = states.shape
    score_scale = HEAD_DIM ** (-0.5)
    block_rows = min(slot_count, 512)
    block_count = slot_count // block_rows
    live = (jnp.arange(slot_count) < counts[0]).astype(jnp.float32)[:, None]
    modulation = jnp.dot(condition, mod_w.astype(jnp.float32), precision=highest)
    scale_one, bias_one, scale_two, bias_two = jnp.split(modulation, 4)
    plain_one, inverse_one = norm_parts(states)
    normed = (plain_one * (1.0 + scale_one) + bias_one).astype(jnp.bfloat16)
    queries = matmul(normed, w_query).astype(jnp.bfloat16)
    key_values = jnp.concatenate([matmul(normed, w_key), matmul(normed, w_value)], axis=1).astype(
        jnp.bfloat16
    )
    send_list = send_rows[0]
    sends = send_list.shape[1]
    landed = []
    for position, hop_size in enumerate(halo_steps):
        parcel = key_values[send_list[position]]
        landed.append(from_behind(parcel, ("nodes", "hid"), hop_size))
    extended = jnp.concatenate([key_values] + landed, axis=0)

    def near(id_block):
        gathered = extended[id_block]
        rows = id_block.shape[0]
        near_keys = gathered[..., :model_width].reshape(rows, NEIGH, HEADS, HEAD_DIM)
        near_values = gathered[..., model_width:].reshape(rows, NEIGH, HEADS, HEAD_DIM)
        return (near_keys, near_values)

    def scores_of(heads_query, near_keys):
        return (
            jnp.einsum("bhd,bkhd->bhk", heads_query, near_keys, preferred_element_type=jnp.float32)
            * score_scale
        )

    def attend(inputs_pair):
        query_block, id_block = inputs_pair
        near_keys, near_values = near(id_block)
        scores = scores_of(query_block.reshape(-1, HEADS, HEAD_DIM), near_keys)
        highest_score = jnp.max(scores, axis=-1, keepdims=True)
        raised = jnp.exp(scores - highest_score)
        total = jnp.sum(raised, axis=-1, keepdims=True)
        attn_probs = (raised / total).astype(jnp.bfloat16)
        mixed = jnp.einsum(
            "bhk,bkhd->bhd", attn_probs, near_values, preferred_element_type=jnp.float32
        )
        return (
            mixed.reshape(-1, model_width).astype(jnp.bfloat16),
            (highest_score + jnp.log(total))[..., 0],
        )

    query_blocks = queries.reshape(block_count, block_rows, model_width)
    id_blocks = neighbours.reshape(block_count, block_rows, NEIGH)
    attended, log_total = lax.map(attend, (query_blocks, id_blocks))
    attended = attended.reshape(slot_count, model_width)
    middle = states + live * matmul(attended, w_out)
    plain_two, inverse_two = norm_parts(middle)
    second = (plain_two * (1.0 + scale_two) + bias_two).astype(jnp.bfloat16)
    grad_branch = (live * cotangent).astype(jnp.bfloat16)
    rows_all = lax.all_gather(second, "hid", axis=0, tiled=True)
    gate = matmul(rows_all, w_gate)
    up_proj = matmul(rows_all, w_up)
    activated, slope = silu_parts(gate)
    hidden = (activated * up_proj).astype(jnp.bfloat16)
    mlp_out = lax.psum_scatter(
        matmul(hidden, w_down).astype(jnp.bfloat16), "hid", scatter_dimension=0, tiled=True
    ).astype(jnp.float32)
    grad_rows = lax.all_gather(grad_branch, "hid", axis=0, tiled=True)
    grad_hidden = times_transposed(grad_rows, w_down)
    grad_gate = (grad_hidden * up_proj * slope).astype(jnp.bfloat16)
    grad_up = (grad_hidden * activated).astype(jnp.bfloat16)
    grad_second = lax.psum_scatter(
        times_transposed(grad_gate, w_gate) + times_transposed(grad_up, w_up),
        "hid",
        scatter_dimension=0,
        tiled=True,
    )
    mlp_grads = (
        transposed_times(rows_all, grad_gate),
        transposed_times(rows_all, grad_up),
        transposed_times(hidden, grad_rows),
    )
    output = middle + live * mlp_out
    grad_w_gate, grad_w_up, grad_w_down = (
        lax.psum(mlp_grads[0].astype(jnp.bfloat16), "nodes").astype(jnp.float32),
        lax.psum(mlp_grads[1].astype(jnp.bfloat16), "nodes").astype(jnp.float32),
        lax.psum(mlp_grads[2].astype(jnp.bfloat16), "nodes").astype(jnp.float32),
    )
    grad_scale_two = jnp.sum(grad_second * plain_two, axis=0)
    grad_bias_two = jnp.sum(grad_second, axis=0)
    grad_middle = cotangent + norm_back(grad_second * (1.0 + scale_two), plain_two, inverse_two)
    grad_attn = (live * grad_middle).astype(jnp.bfloat16)
    grad_w_out_part = transposed_times(attended, grad_attn)
    grad_attended = times_transposed(grad_attn, w_out).astype(jnp.bfloat16)

    def attend_back(carry, inputs):
        query_block, id_block, total_block, grad_block = inputs
        rows = id_block.shape[0]
        near_keys, near_values = near(id_block)
        heads_query = query_block.reshape(rows, HEADS, HEAD_DIM)
        scores = scores_of(heads_query, near_keys)
        attn_probs = jnp.exp(scores - total_block[..., None])
        heads_grad = grad_block.reshape(rows, HEADS, HEAD_DIM)
        grad_probs = jnp.einsum(
            "bhd,bkhd->bhk", heads_grad, near_values, preferred_element_type=jnp.float32
        )
        grad_near_values = jnp.einsum(
            "bhk,bhd->bkhd",
            attn_probs.astype(jnp.bfloat16),
            heads_grad,
            preferred_element_type=jnp.float32,
        )
        grad_scores = (
            attn_probs * (grad_probs - jnp.sum(attn_probs * grad_probs, axis=-1, keepdims=True))
        ).astype(jnp.bfloat16)
        grad_query = (
            jnp.einsum("bhk,bkhd->bhd", grad_scores, near_keys, preferred_element_type=jnp.float32)
            * score_scale
        )
        grad_near_keys = (
            jnp.einsum(
                "bhk,bhd->bkhd", grad_scores, heads_query, preferred_element_type=jnp.float32
            )
            * score_scale
        )
        joined = jnp.concatenate(
            [
                grad_near_keys.reshape(rows, NEIGH, model_width),
                grad_near_values.reshape(rows, NEIGH, model_width),
            ],
            axis=-1,
        )
        return (
            carry.at[id_block].add(joined),
            grad_query.reshape(rows, model_width).astype(jnp.bfloat16),
        )

    start_grads = jnp.zeros((slot_count + 4 * sends, 2 * model_width), jnp.float32)
    grad_blocks = grad_attended.reshape(block_count, block_rows, model_width)
    grad_extended, grad_queries = lax.scan(
        attend_back, start_grads, (query_blocks, id_blocks, log_total, grad_blocks)
    )
    grad_queries = grad_queries.reshape(slot_count, model_width)
    grad_own = grad_extended[:slot_count]
    for position, hop_size in enumerate(halo_steps):
        lower = slot_count + position * sends
        parcel = grad_extended[lower : lower + sends]
        returned = from_behind(parcel.astype(jnp.bfloat16), ("nodes", "hid"), -hop_size).astype(
            parcel.dtype
        )
        grad_own = grad_own.at[send_list[position]].add(returned)
    grad_keys = grad_own[:, :model_width].astype(jnp.bfloat16)
    grad_values = grad_own[:, model_width:].astype(jnp.bfloat16)
    grad_normed = (
        times_transposed(grad_queries, w_query)
        + times_transposed(grad_keys, w_key)
        + times_transposed(grad_values, w_value)
    )
    grad_scale_one = jnp.sum(grad_normed * plain_one, axis=0)
    grad_bias_one = jnp.sum(grad_normed, axis=0)
    grad_states = grad_middle + norm_back(grad_normed * (1.0 + scale_one), plain_one, inverse_one)
    mod_part = jnp.concatenate([grad_scale_one, grad_bias_one, grad_scale_two, grad_bias_two])
    attn_parts = (
        transposed_times(normed, grad_queries),
        transposed_times(normed, grad_keys),
        transposed_times(normed, grad_values),
        grad_w_out_part,
        mod_part,
    )
    grad_w_query, grad_w_key, grad_w_value, grad_w_out, mod_grad = lax.psum(
        (attn_parts[0], attn_parts[1], attn_parts[2], attn_parts[3], attn_parts[4]),
        ("nodes", "hid"),
    )
    grad_mod_w = condition[:, None] * mod_grad[None, :]
    grad_condition = jnp.dot(mod_w.astype(jnp.float32), mod_grad, precision=highest)
    return (
        output,
        grad_states,
        grad_condition,
        grad_mod_w,
        grad_w_query,
        grad_w_key,
        grad_w_value,
        grad_w_out,
        grad_w_gate,
        grad_w_up,
        grad_w_down,
    )


def solution(mesh):
    placed = (
        P(("nodes", "hid"), None),
        P(),
        P(),
        P(),
        P(),
        P(),
        P(),
        P(None, "hid"),
        P(None, "hid"),
        P("hid", None),
        P(("nodes", "hid")),
        P(("nodes", "hid"), None, None),
        P(("nodes", "hid"), None),
        P(("nodes", "hid"), None),
    )
    return jax.shard_map(
        body,
        mesh=mesh,
        in_specs=placed,
        out_specs=(
            P(("nodes", "hid"), None),
            P(("nodes", "hid"), None),
            P(),
            P(),
            P(),
            P(),
            P(),
            P(),
            P(None, "hid"),
            P(None, "hid"),
            P("hid", None),
        ),
        check_vma=False,
    )
```

profile of v0, /device:TPU:0, one launch (start us, length us, event | category | flops | bytes accessed | tf_op | source)
XLA Modules:
  0.0 1331.2 jit_solution(10930679802214883901)
XLA Ops:
  23.1 6.4 collective-permute-start.1
  56.7 165.6 %while.24 = (s32[]{:T(128)}, bf16[2,512,512]{2,1,0:T(8,128)(2,1)}, f32[2,512,4]{1,2,0:T(4,128)S(1)}, bf16[2,512,512]{2,1,0:T(8,128)(2,1)}, s32[2,512,16]{2,1,0:T(8,128)}, /*index=5*/bf16[1536,1024]{1,0:T(8,128)(2,1)}, s32[]{:T(128)}) while((s32[]{:T(128)}, bf16[2,512,512]{2,1,0:T(8,128)(2,1)}, f32[2,512,4]{1,2,0:T(4,128)S(1)}, ...), condition=%wide.region_5.6_spmd, body=%wide.region_2.5_spmd.sunk | while | flops 17364992 | bytes 92569696 | solution.py:123
  64.0 43.0 %gather_fusion = bf16[8192,1024]{1,0:T(8,128)(2,1)} fusion(bf16[1536,1024]{1,0:T(8,128)(2,1)} %get-tuple-element.364, s32[8192]{0:T(1024)S(1)} %broadcast_clamp_fusion.4), kind=kCustom, calls=%fused_computation.clone.1 | custom fusion | bytes 33587200 | tf_op jit(solution)/shard_map/while/body/eval_jaxpr/gather | solution.py:93
  107.0 10.7 slice_bitcast_fusion.6
  117.7 6.6 fusion.128
  128.7 6.0 fusion.132
  146.7 43.0 %gather_fusion = bf16[8192,1024]{1,0:T(8,128)(2,1)} fusion(bf16[1536,1024]{1,0:T(8,128)(2,1)} %get-tuple-element.364, s32[8192]{0:T(1024)S(1)} %broadcast_clamp_fusion.4), kind=kCustom, calls=%fused_computation.clone.1 | custom fusion | bytes 33587200 | tf_op jit(solution)/shard_map/while/body/eval_jaxpr/gather | solution.py:93
  189.7 10.7 slice_bitcast_fusion.6
  200.4 6.6 fusion.128
  211.4 6.0 fusion.132
  231.1 28.3 %all-gather.3.cloned.1.call-done = bf16[4096,512]{0,1:T(8,128)(2,1)} async-done(((bf16[1024,512]{0,1:T(8,128)(2,1)}), bf16[4096,512]{0,1:T(8,128)(2,1)}) %all-gather.3.cloned.1.call-update) | async-done | bytes 4194320 | tf_op jit(solution)/shard_map/all_gather | solution.py:129
  259.3 8.0 fusion.56
  273.1 22.9 %all-gather.5.cloned.1.call-done = bf16[4096,512]{0,1:T(8,128)(2,1)} async-done(((bf16[1024,512]{0,1:T(8,128)(2,1)}), bf16[4096,512]{0,1:T(8,128)(2,1)}) %all-gather.5.cloned.1.call-update) | async-done | bytes 4194320 | tf_op jit(solution)/shard_map/all_gather | solution.py:137
  296.0 11.9 multiply_convert_fusion.1
  307.9 8.4 convolution_convert_fusion.5
  333.3 6.6 convolution_convert_fusion
  339.9 72.5 %all-reduce.7.cloned.1.call-done = (bf16[512,512]{1,0:T(8,128)(2,1)}, bf16[512,512]{1,0:T(8,128)(2,1)}, bf16[512,512]{1,0:T(8,128)(2,1)}) async-done(((bf16[512,512]{1,0:T(8,128)(2,1)}, bf16[512,512]{1,0:T(8,128)(2,1)}, bf16[512,512]{1,0:T(8,128)(2,1)}), (bf16[512,512]{1,0:T(8,128)(2,1)}, bf16[512,512]{1,0:T(8,128)(2,1)}, bf16[512,512]{1,0:T(8,128)(2,1)})) %all-reduce.7.cloned.1.call-update) | async-done | bytes 1572880 | tf_op jit(solution)/shard_map/psum | solution.py:154
  418.9 67.1 %reduce-scatter.5.cloned.1.call-done = f32[1024,512]{0,1:T(8,128)} async-done(((f32[4096,512]{0,1:T(8,128)}), f32[1024,512]{0,1:T(8,128)}) %reduce-scatter.5.cloned.1.call-update) | async-done | bytes 2097168 | tf_op jit(solution)/shard_map/reduce_scatter | solution.py:141
  489.0 44.1 %reduce-scatter.3.cloned.1.call-done = bf16[1024,512]{0,1:T(8,128)(2,1)} async-done(((bf16[4096,512]{0,1:T(8,128)(2,1)}), bf16[1024,512]{0,1:T(8,128)(2,1)}) %reduce-scatter.3.cloned.1.call-update) | async-done | bytes 1048592 | tf_op jit(solution)/shard_map/reduce_scatter | solution.py:134
  545.0 566.5 %while.25 = (s32[]{:T(128)}, f32[1536,1024]{1,0:T(8,128)}, bf16[2,512,512]{2,1,0:T(8,128)(2,1)}, s32[2,512,16]{2,1,0:T(8,128)}, bf16[2,512,512]{2,1,0:T(8,128)(2...) while((s32[]{:T(128)}, f32[1536,1024]{1,0:T(8,128)}, ...), condition=%wide.region_15.16_spmd, body=%wide.region_12.15_spmd.sunk | while | flops 56035344 | bytes 431276384 | solution.py:209
  553.8 43.0 %gather_fusion.1 = bf16[8192,1024]{1,0:T(8,128)(2,1)} fusion(bf16[1536,1024]{1,0:T(8,128)(2,1)} %get-tuple-element.389, s32[8192]{0:T(1024)S(1)} %broadcast_clamp_fusion.5), kind=kCustom, calls=%fused_computation.1.clone.1 | custom fusion | bytes 33587200 | tf_op jit(solution)/shard_map/while/body/eval_jaxpr/gather | solution.py:93
  596.8 10.7 slice_bitcast_fusion.7
  607.6 11.1 fusion.141
  618.7 6.7 fusion.139
  635.6 10.2 fusion.142
  648.6 7.2 copy.169
  655.8 6.0 fusion.143
  663.2 12.7 multiply_bitcast_fusion.5
  675.9 20.0 %reshape.497 = f32[512,16,512]{2,1,0:T(8,128)} reshape(f32[512,16,4,128]{3,2,1,0:T(4,128)} %multiply_bitcast_fusion.5) | data formatting | bytes 33554432 | tf_op jit(solution)/shard_map/while/body/eval_jaxpr/reshape | solution.py:197
  695.9 12.7 multiply_bitcast_fusion.4
  708.6 19.9 %reshape.494 = f32[512,16,512]{2,1,0:T(8,128)} reshape(f32[512,16,4,128]{3,2,1,0:T(4,128)} %multiply_bitcast_fusion.4) | data formatting | bytes 33554432 | tf_op jit(solution)/shard_map/while/body/eval_jaxpr/reshape | solution.py:198
  728.5 23.4 %pad_maximum_fusion.4 = f32[512,16,1024]{2,1,0:T(8,128)} fusion(f32[512,16,512]{2,1,0:T(8,128)} %reshape.494, f32[512,16,512]{2,1,0:T(8,128)} %reshape.497), kind=kLoop, calls=%fused_computation.31.clone.1 | loop fusion | flops 8388608 | bytes 67108864 | tf_op jit(solution)/shard_map/while/body/eval_jaxpr/concatenate | solution.py:195
  751.9 76.4 %scatter_fusion = f32[1536,1024]{1,0:T(8,128)} fusion(f32[1536,1024]{1,0:T(8,128)} %get-tuple-element.376, s32[8192]{0:T(1024)S(1)} %reshape.491, f32[8192,1024]{1,0:T(8,128)} %bitcast.226), kind=kCustom, calls=%fused_computation.6.clone.1 | custom fusion | flops 8388608 | bytes 100696064 | tf_op jit(solution)/shard_map/while/body/eval_jaxpr/scatter-add | solution.py:203
  836.8 43.0 %gather_fusion.1 = bf16[8192,1024]{1,0:T(8,128)(2,1)} fusion(bf16[1536,1024]{1,0:T(8,128)(2,1)} %get-tuple-element.389, s32[8192]{0:T(1024)S(1)} %broadcast_clamp_fusion.5), kind=kCustom, calls=%fused_computation.1.clone.1 | custom fusion | bytes 33587200 | tf_op jit(solution)/shard_map/while/body/eval_jaxpr/gather | solution.py:93
  879.8 10.7 slice_bitcast_fusion.7
  890.5 11.1 fusion.141
  901.7 6.7 fusion.139
  918.5 10.2 fusion.142
  931.6 7.2 copy.169
  938.8 6.0 fusion.143
  946.1 12.7 multiply_bitcast_fusion.5
  958.9 20.0 %reshape.497 = f32[512,16,512]{2,1,0:T(8,128)} reshape(f32[512,16,4,128]{3,2,1,0:T(4,128)} %multiply_bitcast_fusion.5) | data formatting | bytes 33554432 | tf_op jit(solution)/shard_map/while/body/eval_jaxpr/reshape | solution.py:197
  978.9 12.7 multiply_bitcast_fusion.4
  991.6 19.9 %reshape.494 = f32[512,16,512]{2,1,0:T(8,128)} reshape(f32[512,16,4,128]{3,2,1,0:T(4,128)} %multiply_bitcast_fusion.4) | data formatting | bytes 33554432 | tf_op jit(solution)/shard_map/while/body/eval_jaxpr/reshape | solution.py:198
  1011.5 23.4 %pad_maximum_fusion.4 = f32[512,16,1024]{2,1,0:T(8,128)} fusion(f32[512,16,512]{2,1,0:T(8,128)} %reshape.494, f32[512,16,512]{2,1,0:T(8,128)} %reshape.497), kind=kLoop, calls=%fused_computation.31.clone.1 | loop fusion | flops 8388608 | bytes 67108864 | tf_op jit(solution)/shard_map/while/body/eval_jaxpr/concatenate | solution.py:195
  1034.9 76.4 %scatter_fusion = f32[1536,1024]{1,0:T(8,128)} fusion(f32[1536,1024]{1,0:T(8,128)} %get-tuple-element.376, s32[8192]{0:T(1024)S(1)} %reshape.491, f32[8192,1024]{1,0:T(8,128)} %bitcast.226), kind=kCustom, calls=%fused_computation.6.clone.1 | custom fusion | flops 8388608 | bytes 100696064 | tf_op jit(solution)/shard_map/while/body/eval_jaxpr/scatter-add | solution.py:203
  1180.2 44.1 %psum.56 = f32[2048]{0:T(1024)S(1)} all-reduce(f32[2048]{0:T(1024)S(1)} %pad_maximum_fusion.2), channel_id=1, replica_groups=mesh['nodes'=8,'hid'=4] {'nodes','hid'}, use_global_device_ids=true, to_apply=%region_26.27 | all-reduce | flops 2048 | bytes 16384 | tf_op jit(solution)/shard_map/psum | solution.py:239
  1225.8 91.8 %all-reduce.5.cloned.1.call-done = (f32[512,512]{1,0:T(8,128)}, f32[512,512]{1,0:T(8,128)}, f32[512,512]{1,0:T(8,128)}, f32[512,512]{1,0:T(8,128)}) async-done(((f32[512,512]{1,0:T(8,128)}, f32[512,512]{1,0:T(8,128)}, f32[512,512]{1,0:T(8,128)}, f32[512,512]{1,0:T(8,128)}), (f32[512,512]{1,0:T(8,128)}, f32[512,512]{1,0:T(8,128)}, f32[512,512]{1,0:T(8,128)}, ...) | async-done | bytes 4194320 | tf_op jit(solution)/shard_map/psum | solution.py:239
  (317 shorter events, 249.8 us)
Async XLA Ops:
  7.2 288.8 %copy-start = (bf16[512,512]{1,0:T(8,128)(2,1)S(1)}, bf16[512,512]{1,0:T(8,128)(2,1)}, u32[]{:S(2)}) copy-start(bf16[512,512]{1,0:T(8,128)(2,1)} %param.27) | copy-start | bytes 1572868
  7.2 252.1 %all-gather.3.cloned.1.call-start = ((), (), s32[]{:S(2)}) async-start(), calls=%async_computation.2 | async-start | bytes 5242880 | tf_op jit(solution)/shard_map/all_gather | solution.py:129
  8.1 13.3 copy-start.61
  8.1 13.3 copy-start.62
  8.1 23.1 %copy-start.59 = (s32[128]{0:T(128)}, s32[128]{0:T(128)S(1)}, u32[]{:S(2)}) copy-start(s32[128]{0:T(128)S(1)} %get-tuple-element.232) | copy-start | bytes 1540
  8.1 23.1 %copy-start.60 = (s32[128]{0:T(128)}, s32[128]{0:T(128)S(1)}, u32[]{:S(2)}) copy-start(s32[128]{0:T(128)S(1)} %get-tuple-element.235) | copy-start | bytes 1540
  23.1 23.6 %collective-permute-start.1 = (bf16[128,1024]{0,1:T(8,128)(2,1)}, bf16[128,1024]{0,1:T(8,128)(2,1)}, u32[]{:S(2)}, u32[]{:S(2)}) collective-permute-start(bf16[128,1024]{0,1:T(8,128)(2,1)} %copy.81), channel_id=1, source_target_pairs={{1,0},{2,1},{3,2},{4,3},{5,4},{6,5},{7,6},{8,7},{9,8},{10,9},{11,1... | collective-permute-start | bytes 786440 | tf_op jit(solution)/shard_map/ppermute | solution.py:19
  29.5 10.4 copy-start.35
  31.2 13.9 %collective-permute-start = (bf16[128,1024]{0,1:T(8,128)(2,1)}, bf16[128,1024]{0,1:T(8,128)(2,1)}, u32[]{:S(2)}, u32[]{:S(2)}) collective-permute-start(bf16[128,1024]{0,1:T(8,128)(2,1)} %copy.79), channel_id=1, source_target_pairs={{31,0},{0,1},{1,2},{2,3},{3,4},{4,5},{5,6},{6,7},{7,8},{8,9},{9,10... | collective-permute-start | bytes 786440 | tf_op jit(solution)/shard_map/ppermute | solution.py:19
  31.2 12.8 copy-start.48
  32.9 15.6 %collective-permute-start.2 = (bf16[128,1024]{0,1:T(8,128)(2,1)}, bf16[128,1024]{0,1:T(8,128)(2,1)}, u32[]{:S(2)}, u32[]{:S(2)}) collective-permute-start(bf16[128,1024]{0,1:T(8,128)(2,1)} %copy.83), channel_id=1, source_target_pairs={{30,0},{31,1},{0,2},{1,3},{2,4},{3,5},{4,6},{5,7},{6,8},{7,9},{8,1... | collective-permute-start | bytes 786440 | tf_op jit(solution)/shard_map/ppermute | solution.py:19
  34.0 16.3 %collective-permute-start.3 = (bf16[128,1024]{0,1:T(8,128)(2,1)S(1)}, bf16[128,1024]{0,1:T(8,128)(2,1)S(1)}, u32[]{:S(2)}, u32[]{:S(2)}) collective-permute-start(bf16[128,1024]{0,1:T(8,128)(2,1)S(1)} %copy.85), channel_id=1, source_target_pairs={{2,0},{3,1},{4,2},{5,3},{6,4},{7,5},{8,6},{9,7},{10,8},{11,9},{12,... | collective-permute-start | bytes 786440 | tf_op jit(solution)/shard_map/ppermute | solution.py:19
  56.7 165.6 %copy-start.8 = (f32[1024,512]{0,1:T(8,128)S(1)}, f32[1024,512]{0,1:T(8,128)}, u32[]{:S(2)}) copy-start(f32[1024,512]{0,1:T(8,128)} %copy-done.7) | copy-start | bytes 6291460
  56.7 165.6 %copy-start.41 = (f32[1024]{0:T(1024)S(1)}, f32[1024]{0:T(1024)}, u32[]{:S(2)}) copy-start(f32[1024]{0:T(1024)} %fusion.45) | copy-start | bytes 12292
  227.1 32.2 %copy-start.27 = (bf16[512,512]{1,0:T(8,128)(2,1)S(1)}, bf16[512,512]{1,0:T(8,128)(2,1)}, u32[]{:S(2)}) copy-start(bf16[512,512]{1,0:T(8,128)(2,1)} %param.26) | copy-start | bytes 1572868
  227.1 68.9 %all-gather.5.cloned.1.call-start = ((), (), s32[]{:S(2)}) async-start(), calls=%async_computation.4 | async-start | bytes 5242880 | tf_op jit(solution)/shard_map/all_gather | solution.py:137
  229.5 37.8 %copy-start.14 = (f32[1024,512]{0,1:T(8,128)}, f32[1024,512]{0,1:T(8,128)S(1)}, u32[]{:S(2)}) copy-start(f32[1024,512]{0,1:T(8,128)S(1)} %copy.93) | copy-start | bytes 6291460
  231.0 181.4 %all-reduce.7.cloned.1.call-start = ((), (), s32[]{:S(2)}) async-start(), calls=%async_computation.7 | async-start | bytes 3145728 | tf_op jit(solution)/shard_map/psum | solution.py:154
  259.3 8.0 copy-start.15
  259.3 8.0 copy-start.28
  296.0 11.9 copy-start.63
  307.9 8.4 copy-start.23
  307.9 11.5 copy-start.25
  307.9 8.4 copy-start.16
  322.6 163.4 %reduce-scatter.5.cloned.1.call-start = ((), (), s32[]{:S(2)}) async-start(), calls=%async_computation.5 | async-start | bytes 10485760 | tf_op jit(solution)/shard_map/reduce_scatter | solution.py:141
  333.1 200.1 %reduce-scatter.3.cloned.1.call-start = ((), (), s32[]{:S(2)}) async-start(), calls=%async_computation.3 | async-start | bytes 5242880 | tf_op jit(solution)/shard_map/reduce_scatter | solution.py:134
  339.9 146.2 %copy-start.11 = (f32[1024,512]{0,1:T(8,128)S(1)}, f32[1024,512]{0,1:T(8,128)}, u32[]{:S(2)}) copy-start(f32[1024,512]{0,1:T(8,128)} %copy-done.10) | copy-start | bytes 6291460
  339.9 977.6 %all-reduce.5.cloned.1.call-start = ((), (), s32[]{:S(2)}) async-start(), calls=%async_computation.6 | async-start | bytes 8388608 | tf_op jit(solution)/shard_map/psum | solution.py:239
  607.5 11.1 copy-start.4
  635.6 10.2 copy-start.3
  675.9 20.0 %copy-start.6 = (f32[512,4,128]{2,1,0:T(4,128)S(1)}, f32[512,4,128]{2,1,0:T(4,128)}, u32[]{:S(2)}) copy-start(f32[512,4,128]{2,1,0:T(4,128)} %convert.57) | copy-start | bytes 3145732 | tf_op jit(solution)/shard_map/while
  751.9 76.4 %copy-start.18 = (bf16[2,512,512]{2,1,0:T(8,128)(2,1)S(1)}, bf16[2,512,512]{2,1,0:T(8,128)(2,1)}, u32[]{:S(2)}) copy-start(bf16[2,512,512]{2,1,0:T(8,128)(2,1)} %copy-done.17) | copy-start | bytes 3145732 | tf_op jit(solution)/shard_map/while
  751.9 76.4 %copy-start.45 = (f32[2,512,4]{1,2,0:T(4,128)S(1)}, f32[2,512,4]{1,2,0:T(4,128)}, u32[]{:S(2)}) copy-start(f32[2,512,4]{1,2,0:T(4,128)} %copy-done.44) | copy-start | bytes 49156 | tf_op jit(solution)/shard_map/while
  828.4 5.7 copy-start.44
  890.5 11.1 copy-start.4
  918.5 10.2 copy-start.3
  958.9 20.0 %copy-start.6 = (f32[512,4,128]{2,1,0:T(4,128)S(1)}, f32[512,4,128]{2,1,0:T(4,128)}, u32[]{:S(2)}) copy-start(f32[512,4,128]{2,1,0:T(4,128)} %convert.57) | copy-start | bytes 3145732 | tf_op jit(solution)/shard_map/while
  1034.9 76.4 %copy-start.18 = (bf16[2,512,512]{2,1,0:T(8,128)(2,1)S(1)}, bf16[2,512,512]{2,1,0:T(8,128)(2,1)}, u32[]{:S(2)}) copy-start(bf16[2,512,512]{2,1,0:T(8,128)(2,1)} %copy-done.17) | copy-start | bytes 3145732 | tf_op jit(solution)/shard_map/while
  1034.9 76.4 %copy-start.45 = (f32[2,512,4]{1,2,0:T(4,128)S(1)}, f32[2,512,4]{1,2,0:T(4,128)}, u32[]{:S(2)}) copy-start(f32[2,512,4]{1,2,0:T(4,128)} %copy-done.44) | copy-start | bytes 49156 | tf_op jit(solution)/shard_map/while
  1120.7 15.8 %copy-start.26 = (bf16[2,512,512]{2,1,0:T(8,128)(2,1)S(1)}, bf16[2,512,512]{2,1,0:T(8,128)(2,1)}, u32[]{:S(2)}) copy-start(bf16[2,512,512]{2,1,0:T(8,128)(2,1)} %get-tuple-element.89) | copy-start | bytes 3145732
  1120.7 15.8 %copy-start.32 = (bf16[1024,512]{0,1:T(8,128)(2,1)S(1)}, bf16[1024,512]{0,1:T(8,128)(2,1)}, u32[]{:S(2)}) copy-start(bf16[1024,512]{0,1:T(8,128)(2,1)} %copy-done.31) | copy-start | bytes 3145732
  1125.5 32.5 %collective-permute-start.7 = (bf16[128,1024]{1,0:T(8,128)(2,1)S(1)}, bf16[128,1024]{1,0:T(8,128)(2,1)S(1)}, u32[]{:S(2)}, u32[]{:S(2)}) collective-permute-start(bf16[128,1024]{1,0:T(8,128)(2,1)S(1)} %get-tuple-element.220), channel_id=1, source_target_pairs={{30,0},{31,1},{0,2},{1,3},{2,4},{3,5},{4,6},{5,7},{6,8},{7,9},{8,1... | collective-permute-start | bytes 786440 | tf_op jit(solution)/shard_map/ppermute | solution.py:19
  1125.9 26.3 %collective-permute-start.6 = (bf16[128,1024]{1,0:T(8,128)(2,1)S(1)}, bf16[128,1024]{1,0:T(8,128)(2,1)S(1)}, u32[]{:S(2)}, u32[]{:S(2)}) collective-permute-start(bf16[128,1024]{1,0:T(8,128)(2,1)S(1)} %get-tuple-element.221), channel_id=1, source_target_pairs={{2,0},{3,1},{4,2},{5,3},{6,4},{7,5},{8,6},{9,7},{10,8},{11,9},{12,... | collective-permute-start | bytes 786440 | tf_op jit(solution)/shard_map/ppermute | solution.py:19
  1131.2 15.1 %collective-permute-start.5 = (bf16[128,1024]{1,0:T(8,128)(2,1)S(1)}, bf16[128,1024]{1,0:T(8,128)(2,1)S(1)}, u32[]{:S(2)}, u32[]{:S(2)}) collective-permute-start(bf16[128,1024]{1,0:T(8,128)(2,1)S(1)} %get-tuple-element.222), channel_id=1, source_target_pairs={{31,0},{0,1},{1,2},{2,3},{3,4},{4,5},{5,6},{6,7},{7,8},{8,9},{9,10... | collective-permute-start | bytes 786440 | tf_op jit(solution)/shard_map/ppermute | solution.py:19
  1131.2 9.2 collective-permute-start.4
  1177.3 47.0 %copy-start.50 = (bf16[16,2048]{1,0:T(8,128)(2,1)S(1)}, bf16[16,2048]{1,0:T(8,128)(2,1)}, u32[]{:S(2)}) copy-start(bf16[16,2048]{1,0:T(8,128)(2,1)} %param.20) | copy-start | bytes 196612
  1177.3 47.7 %copy-start.58 = (f32[16]{0:T(128)S(1)}, f32[16]{0:T(128)}, u32[]{:S(2)}) copy-start(f32[16]{0:T(128)} %param.19) | copy-start | bytes 196
  1317.5 6.6 copy-start.1
  (38 other events, 113.7 us)
Sparse Core Ops, SparseCore 0:
  227.2 32.0 all-gather.2
  261.5 34.4 all-gather.4
  322.7 89.7 all-reduce.6
  414.9 71.0 reduce-scatter.4
  488.6 44.5 reduce-scatter.2
  1169.9 147.5 all-reduce.4
where the time goes:
time: 1340 us; the launch traced here: 1330 us
  local copies, waits for them, and re-layouts  417 us (31%)
  other arithmetic  347 us (26%)
  waiting for transfers between devices  329 us (25%)
  matrix products  154 us (11%)
  blocking collectives  44.1 us (3%)
  starting transfers between devices  24.1 us (2%)
  between operations  15.5 us (1%)
    gather x4, local copies, waits for them, and re-layouts, near(): gathered = extended[id_block]  172 us
    scatter-add x2, other arithmetic, attend_back(): carry.at[id_block].add(joined)  153 us
    psum x1, waiting for transfers between devices, body(): lax.psum((attn_parts[0], attn_parts[1], attn_parts[2], attn_parts[3], att...  91.8 us
    psum x1, waiting for transfers between devices, body(): lax.psum(mlp_grads[0].astype(jnp.bfloat16), 'nodes').astype(jnp.float32)  72.5 us
    reduce_scatter x1, waiting for transfers between devices, body(): lax.psum_scatter(times_transposed(grad_gate, w_gate) + times_transposed(g...  67.1 us
    concatenate x2, other arithmetic, attend_back(): jnp.concatenate([grad_near_keys.reshape(rows, NEIGH, model_width), grad_n...  46.8 us
    reduce_scatter x1, waiting for transfers between devices, body(): lax.psum_scatter(matmul(hidden, w_down).astype(jnp.bfloat16), 'hid', scat...  44.1 us
    psum x1, blocking collectives, body(): lax.psum((attn_parts[0], attn_parts[1], attn_parts[2], attn_parts[3], att...  44.1 us
  transfers between devices with their start and end apart: 14, of which 7 were waited for; matrix products, arithmetic and copies ran while one was open for 7% of the time, Pallas kernels for 0%

commit v1 on v0

--- a/solution.py
+++ b/solution.py
@@ -1,6 +1,8 @@
 import jax
 import jax.numpy as jnp
 from jax import lax
+from jax.experimental import pallas as pl
+from jax.experimental.pallas import tpu as pltpu
 from jax.sharding import PartitionSpec as P
 
 HEADS = 4
@@ -50,6 +52,155 @@
 def silu_parts(gate):
     sigmoid = jax.nn.sigmoid(gate)
     return (gate * sigmoid, sigmoid * (1.0 + gate * (1.0 - sigmoid)))
+
+
+def dot(left, right, left_dim, right_dim):
+    return lax.dot_general(
+        left, right, (((left_dim,), (right_dim,)), ((), ())), preferred_element_type=jnp.float32
+    )
+
+
+BLOCK = 512
+score_scale = HEAD_DIM ** (-0.5)
+
+
+def attend_kernel(near_ref, query_ref, key_ref, value_t_ref, attended_ref, raised_ref, inverse_ref, bias, scores):
+    ext, rows = bias.shape
+    groups = ext // 128
+    half = groups // 2
+
+    @pl.when(pl.program_id(0) == 0)
+    def _():
+        @pl.loop(0, rows // 128)
+        def _(step):
+            cols = pl.ds(pl.multiple_of(step * 128, 128), 128)
+            near = near_ref[:, cols]
+            group = near >> 7
+            upper = group >= half
+            unit = jnp.left_shift(1, 5 * jnp.where(upper, group - half, group))
+            low = near & 127
+            low_unit = jnp.where(upper, 0, unit)
+            high_unit = jnp.where(upper, unit, 0)
+            place = lax.broadcasted_iota(jnp.int32, (128, 128), 0)
+            low_count = jnp.zeros((128, 128), jnp.int32)
+            high_count = low_count
+            for n in range(NEIGH):
+                same = low[n : n + 1] == place
+                low_count = low_count + jnp.where(same, low_unit[n : n + 1], 0)
+                high_count = high_count + jnp.where(same, high_unit[n : n + 1], 0)
+            for g in range(groups):
+                packed = low_count if g < half else high_count
+                count = (packed >> (5 * (g % half))) & 31
+                bias[g * 128 : (g + 1) * 128, cols] = jnp.where(
+                    count > 0, jnp.log(count.astype(jnp.float32)), -1e30
+                )
+
+    width = scores.shape[1]
+
+    @pl.loop(0, rows // width)
+    def _(step):
+        cols = pl.ds(pl.multiple_of(step * width, width), width)
+        query = query_ref[cols, :]
+        top = jnp.full((8, width), -jnp.inf, jnp.float32)
+        for g in range(groups):
+            part = slice(g * 128, (g + 1) * 128)
+            score = dot(key_ref[part, :], query, 1, 1) * score_scale + bias[part, cols]
+            scores[part, :] = score
+            top = jnp.maximum(top, jnp.max(score.reshape(16, 8, width), axis=0))
+        top = jnp.max(top, axis=0, keepdims=True)
+        total = jnp.zeros((8, width), jnp.float32)
+        for g in range(groups):
+            part = slice(g * 128, (g + 1) * 128)
+            raised = jnp.exp(scores[part, :] - top)
+            total = total + jnp.sum(raised.reshape(16, 8, width), axis=0)
+            raised_ref[0, part, cols] = raised.astype(jnp.bfloat16)
+        inverse = 1.0 / jnp.sum(total, axis=0, keepdims=True)
+        inverse_ref[0, :, cols] = inverse
+        mixed = dot(value_t_ref[...], raised_ref[0, :, cols], 1, 0) * inverse
+        attended_ref[cols, :] = mixed.T.astype(jnp.bfloat16)
+
+
+def attend(near, queries, keys, values_t):
+    rows, ext = queries.shape[0], keys.shape[0]
+    return pl.pallas_call(
+        attend_kernel,
+        grid=(HEADS,),
+        in_specs=[
+            pl.BlockSpec((NEIGH, rows), lambda h: (0, 0)),
+            pl.BlockSpec((rows, HEAD_DIM), lambda h: (0, h)),
+            pl.BlockSpec((ext, HEAD_DIM), lambda h: (0, h)),
+            pl.BlockSpec((HEAD_DIM, ext), lambda h: (h, 0)),
+        ],
+        out_specs=[
+            pl.BlockSpec((rows, HEAD_DIM), lambda h: (0, h)),
+            pl.BlockSpec((1, ext, rows), lambda h: (h, 0, 0)),
+            pl.BlockSpec((1, 1, rows), lambda h: (h, 0, 0)),
+        ],
+        out_shape=[
+            jax.ShapeDtypeStruct((rows, HEADS * HEAD_DIM), jnp.bfloat16),
+            jax.ShapeDtypeStruct((HEADS, ext, rows), jnp.bfloat16),
+            jax.ShapeDtypeStruct((HEADS, 1, rows), jnp.float32),
+        ],
+        scratch_shapes=[pltpu.VMEM((ext, rows), jnp.float32), pltpu.VMEM((ext, BLOCK), jnp.float32)],
+        compiler_params=pltpu.CompilerParams(vmem_limit_bytes=48 * 2**20),
+        cost_estimate=pl.CostEstimate(flops=4 * ext * rows * 512, bytes_accessed=2**24, transcendentals=4 * ext * rows),
+    )(near, queries, keys, values_t)
+
+
+def attend_back_kernel(
+    query_ref, key_t_ref, value_ref, grad_ref, raised_ref, inverse_ref, grad_query_ref, grad_key_ref, grad_value_ref, terms, low
+):
+    ext, rows = low.shape
+    width = terms.shape[1]
+
+    @pl.loop(0, rows // width)
+    def _(step):
+        cols = pl.ds(pl.multiple_of(step * width, width), width)
+        grad = grad_ref[cols, :]
+        total = jnp.zeros((8, width), jnp.float32)
+        for g in range(ext // 128):
+            part = slice(g * 128, (g + 1) * 128)
+            term = dot(value_ref[part, :], grad, 1, 1) * raised_ref[0, part, cols].astype(jnp.float32)
+            terms[part, :] = term
+            total = total + jnp.sum(term.reshape(16, 8, width), axis=0)
+        mean = jnp.sum(total, axis=0, keepdims=True) * inverse_ref[0, :, cols]
+        for g in range(ext // 128):
+            part = slice(g * 128, (g + 1) * 128)
+            low[part, cols] = (terms[part, :] - raised_ref[0, part, cols].astype(jnp.float32) * mean).astype(
+                jnp.bfloat16
+            )
+        grad_query = dot(key_t_ref[...], low[:, cols], 1, 0) * score_scale
+        grad_query_ref[cols, :] = grad_query.T.astype(jnp.bfloat16)
+
+    grad_value_ref[...] = dot(raised_ref[0], grad_ref[...], 1, 0)
+    grad_key_ref[...] = dot(low[...], query_ref[...], 1, 0) * score_scale
+
+
+def attend_back(queries, keys_t, values, grads, raised, inverse):
+    rows, ext = queries.shape[0], values.shape[0]
+    by_row = pl.BlockSpec((rows, HEAD_DIM), lambda h: (0, h))
+    by_ext = pl.BlockSpec((ext, HEAD_DIM), lambda h: (0, h))
+    return pl.pallas_call(
+        attend_back_kernel,
+        grid=(HEADS,),
+        in_specs=[
+            by_row,
+            pl.BlockSpec((HEAD_DIM, ext), lambda h: (h, 0)),
+            by_ext,
+            by_row,
+            pl.BlockSpec((1, ext, rows), lambda h: (h, 0, 0)),
+            pl.BlockSpec((1, 1, rows), lambda h: (h, 0, 0)),
+        ],
+        out_specs=[by_row, by_ext, by_ext],
+        out_shape=[
+            jax.ShapeDtypeStruct((rows, HEADS * HEAD_DIM), jnp.bfloat16),
+            jax.ShapeDtypeStruct((ext, HEADS * HEAD_DIM), jnp.float32),
+            jax.ShapeDtypeStruct((ext, HEADS * HEAD_DIM), jnp.float32),
+        ],
+        scratch_shapes=[pltpu.VMEM((ext, BLOCK), jnp.float32), pltpu.VMEM((ext, rows), jnp.bfloat16)],
+        compiler_params=pltpu.CompilerParams(vmem_limit_bytes=48 * 2**20),
+        cost_estimate=pl.CostEstimate(flops=8 * ext * rows * 512, bytes_accessed=2**24, transcendentals=0),
+    )(queries, keys_t, values, grads, raised, inverse)
 
 
 def body(
@@ -69,9 +220,6 @@
     cotangent,
 ):
     slot_count, model_width = states.shape
-    score_scale = HEAD_DIM ** (-0.5)
-    block_rows = min(slot_count, 512)
-    block_count = slot_count // block_rows
     live = (jnp.arange(slot_count) < counts[0]).astype(jnp.float32)[:, None]
     modulation = jnp.dot(condition, mod_w.astype(jnp.float32), precision=highest)
     scale_one, bias_one, scale_two, bias_two = jnp.split(modulation, 4)
@@ -89,39 +237,8 @@
         landed.append(from_behind(parcel, ("nodes", "hid"), hop_size))
     extended = jnp.concatenate([key_values] + landed, axis=0)
 
-    def near(id_block):
-        gathered = extended[id_block]
-        rows = id_block.shape[0]
-        near_keys = gathered[..., :model_width].reshape(rows, NEIGH, HEADS, HEAD_DIM)
-        near_values = gathered[..., model_width:].reshape(rows, NEIGH, HEADS, HEAD_DIM)
-        return (near_keys, near_values)
-
-    def scores_of(heads_query, near_keys):
-        return (
-            jnp.einsum("bhd,bkhd->bhk", heads_query, near_keys, preferred_element_type=jnp.float32)
-            * score_scale
-        )
-
-    def attend(inputs_pair):
-        query_block, id_block = inputs_pair
-        near_keys, near_values = near(id_block)
-        scores = scores_of(query_block.reshape(-1, HEADS, HEAD_DIM), near_keys)
-        highest_score = jnp.max(scores, axis=-1, keepdims=True)
-        raised = jnp.exp(scores - highest_score)
-        total = jnp.sum(raised, axis=-1, keepdims=True)
-        attn_probs = (raised / total).astype(jnp.bfloat16)
-        mixed = jnp.einsum(
-            "bhk,bkhd->bhd", attn_probs, near_values, preferred_element_type=jnp.float32
-        )
-        return (
-            mixed.reshape(-1, model_width).astype(jnp.bfloat16),
-            (highest_score + jnp.log(total))[..., 0],
-        )
-
-    query_blocks = queries.reshape(block_count, block_rows, model_width)
-    id_blocks = neighbours.reshape(block_count, block_rows, NEIGH)
-    attended, log_total = lax.map(attend, (query_blocks, id_blocks))
-    attended = attended.reshape(slot_count, model_width)
+    keys, values = extended[:, :model_width], extended[:, model_width:]
+    attended, raised, inverse_total = attend(neighbours.T, queries, keys, values.T)
     middle = states + live * matmul(attended, w_out)
     plain_two, inverse_two = norm_parts(middle)
     second = (plain_two * (1.0 + scale_two) + bias_two).astype(jnp.bfloat16)
@@ -160,56 +277,12 @@
     grad_middle = cotangent + norm_back(grad_second * (1.0 + scale_two), plain_two, inverse_two)
     grad_attn = (live * grad_middle).astype(jnp.bfloat16)
     grad_w_out_part = transposed_times(attended, grad_attn)
-    grad_attended = times_transposed(grad_attn, w_out).astype(jnp.bfloat16)
-
-    def attend_back(carry, inputs):
-        query_block, id_block, total_block, grad_block = inputs
-        rows = id_block.shape[0]
-        near_keys, near_values = near(id_block)
-        heads_query = query_block.reshape(rows, HEADS, HEAD_DIM)
-        scores = scores_of(heads_query, near_keys)
-        attn_probs = jnp.exp(scores - total_block[..., None])
-        heads_grad = grad_block.reshape(rows, HEADS, HEAD_DIM)
-        grad_probs = jnp.einsum(
-            "bhd,bkhd->bhk", heads_grad, near_values, preferred_element_type=jnp.float32
-        )
-        grad_near_values = jnp.einsum(
-            "bhk,bhd->bkhd",
-            attn_probs.astype(jnp.bfloat16),
-            heads_grad,
-            preferred_element_type=jnp.float32,
-        )
-        grad_scores = (
-            attn_probs * (grad_probs - jnp.sum(attn_probs * grad_probs, axis=-1, keepdims=True))
-        ).astype(jnp.bfloat16)
-        grad_query = (
-            jnp.einsum("bhk,bkhd->bhd", grad_scores, near_keys, preferred_element_type=jnp.float32)
-            * score_scale
-        )
-        grad_near_keys = (
-            jnp.einsum(
-                "bhk,bhd->bkhd", grad_scores, heads_query, preferred_element_type=jnp.float32
-            )
-            * score_scale
-        )
-        joined = jnp.concatenate(
-            [
-                grad_near_keys.reshape(rows, NEIGH, model_width),
-                grad_near_values.reshape(rows, NEIGH, model_width),
-            ],
-            axis=-1,
-        )
-        return (
-            carry.at[id_block].add(joined),
-            grad_query.reshape(rows, model_width).astype(jnp.bfloat16),
-        )
-
-    start_grads = jnp.zeros((slot_count + 4 * sends, 2 * model_width), jnp.float32)
-    grad_blocks = grad_attended.reshape(block_count, block_rows, model_width)
-    grad_extended, grad_queries = lax.scan(
-        attend_back, start_grads, (query_blocks, id_blocks, log_total, grad_blocks)
-    )
-    grad_queries = grad_queries.reshape(slot_count, model_width)
+    spread = jnp.repeat(inverse_total[:, 0].T, HEAD_DIM, axis=1)
+    grad_attended = (times_transposed(grad_attn, w_out) * spread).astype(jnp.bfloat16)
+    grad_queries, *grad_extended = attend_back(
+        queries, keys.T, values, grad_attended, raised, inverse_total
+    )
+    grad_extended = jnp.concatenate(grad_extended, axis=1)
     grad_own = grad_extended[:slot_count]
     for position, hop_size in enumerate(halo_steps):
         lower = slot_count + position * sends

time: 1340 us -> 632 us (0.47)
  local copies, waits for them, and re-layouts: 417 us -> 46.7 us
  other arithmetic: 347 us -> 51.7 us
  matrix products: 154 us -> 72.7 us
  Pallas kernels: 0 us -> 45.7 us
    gather x4 -> x0, local copies, waits for them, and re-layouts: 172 us -> none  [near(): gathered = extended[id_block]]
    scatter-add x2 -> x0, other arithmetic: 153 us -> none  [attend_back(): carry.at[id_block].add(joined)]
    reshape x14 -> x0, local copies, waits for them, and re-layouts: 95.1 us -> none  [the longest x2 40 us: attend_back(): grad_near_keys.reshape(rows, NEIGH, model_width)]
    dot_general x10 -> x0, matrix products: 72.9 us -> none  [the longest x4 26.6 us: scores_of(): jnp.einsum('bhd,bkhd->bhk', heads_query, near_keys, preferred_element_typ...]
    while x38 -> x0, local copies, waits for them, and re-layouts: 48.6 us -> none
    concatenate x2 -> x0, other arithmetic: 46.8 us -> none  [attend_back(): jnp.concatenate([grad_near_keys.reshape(rows, NEIGH, model_width), grad_n...]
    pallas_call x0 -> x2, Pallas kernels: none -> 45.7 us  [the longest x1 25.4 us: attend_back(): pl.pallas_call(attend_back_kernel, grid=(HEADS,), in_specs=[by_row, pl.Bl...]
    mul x2 -> x0, other arithmetic: 25.4 us -> none  [attend_back(): jnp.einsum('bhk,bhd->bkhd', grad_scores, heads_query, preferred_element_t...]
  transfers between devices with their start and end apart: 14 -> 14, of which waited for: 7 -> 6; matrix products, arithmetic and copies ran while one was open for 7% -> 15% of each run, Pallas kernels for 0% -> 0%
where the time goes in v1:
time: 632 us; the launch traced here: 624 us
  waiting for transfers between devices  320 us (51%)
  matrix products  72.7 us (12%)
  other arithmetic  51.7 us (8%)
  local copies, waits for them, and re-layouts  46.7 us (7%)
  Pallas kernels  45.7 us (7%)
  blocking collectives  42 us (7%)
  starting transfers between devices  29.9 us (5%)
  between operations  15.4 us (2%)
    psum x1, waiting for transfers between devices, body(): lax.psum((attn_parts[0], attn_parts[1], attn_parts[2], attn_parts[3], att...  96.2 us
    psum x1, waiting for transfers between devices, body(): lax.psum(mlp_grads[0].astype(jnp.bfloat16), 'nodes').astype(jnp.float32)  69.6 us
    reduce_scatter x1, waiting for transfers between devices, body(): lax.psum_scatter(times_transposed(grad_gate, w_gate) + times_transposed(g...  68.1 us
    reduce_scatter x1, waiting for transfers between devices, body(): lax.psum_scatter(matmul(hidden, w_down).astype(jnp.bfloat16), 'hid', scat...  44.1 us
    psum x1, blocking collectives, body(): lax.psum((attn_parts[0], attn_parts[1], attn_parts[2], attn_parts[3], att...  42 us
    dot_general x7, matrix products, times_transposed(): lax.dot_general(left, right, (((1,), (1,)), ((), ())), preferred_element_...  29.9 us
    unnamed x101, local copies, waits for them, and re-layouts  28.2 us
    dot_general x7, matrix products, matmul(): return jnp.dot(left, right, preferred_element_type=jnp.float32)  25.5 us
  transfers between devices with their start and end apart: 14, of which 6 were waited for; matrix products, arithmetic and copies ran while one was open for 15% of the time, Pallas kernels for 0%

profile of v1, /device:TPU:0, one launch (start us, length us, event | category | flops | bytes accessed | tf_op | source)
XLA Modules:
  0.0 623.8 jit_solution(14421801117340154068)
XLA Ops:
  7.2 2.0 copy.29
  9.3 2.6 reduce_sum.108
  15.4 1.9 pad_maximum_fusion
  20.2 6.0 collective-permute-start.1
  29.3 5.6 collective-permute-start.3
  34.9 2.9 convolution_convert_fusion.3.query_ref
  41.5 2.4 fusion.26
  43.9 2.6 copy.28.value_t_ref
  49.2 20.3 %shard_map.221 = (bf16[1024,512]{1,0:T(8,128)(2,1)S(1)}, bf16[4,1536,1024]{2,1,0:T(8,128)(2,1)}, f32[4,1,1024]{2,1,0:T(1,128)S(1)}) custom-call(s32[16,1024]{1,0:T(8,128)S(1)} %bitcast.79, bf16[1024,512]{1,0:T(8,128)(2,1)S(1)} %copy-done.5, bf16[1536,512]{1,0:T(8,128)(2,1)S(1)} %get-tuple-element.59.key_ref, bf16[512,1536]{1,0:T(8,128)(2,1)S(1)} %copy-done.1), custom_call_target="tpu_custom_call" | custom-call | flops 3221225472 | bytes 16777216 | tf_op jit(solution)/shard_map/pallas_call | solution.py:125
  73.0 2.9 copy.34
  75.9 2.9 multiply_convert_fusion.4
  78.8 11.4 %all-reduce.7.cloned.1.call-start = ((), (), s32[]{:S(2)}) async-start(), calls=%async_computation.7 | async-start | bytes 3145728 | tf_op jit(solution)/shard_map/psum | solution.py:271
  90.2 18.6 %all-gather.3.cloned.1.call-done = bf16[4096,512]{0,1:T(8,128)(2,1)} async-done(((bf16[1024,512]{0,1:T(8,128)(2,1)}), bf16[4096,512]{0,1:T(8,128)(2,1)}) %all-gather.3.cloned.1.call-update) | async-done | bytes 4194320 | tf_op jit(solution)/shard_map/all_gather | solution.py:246
  108.8 7.9 %fusion.28 = f32[4096,512]{1,0:T(8,128)} fusion(bf16[4096,512]{0,1:T(8,128)(2,1)} %all-gather.3.cloned.1.call-done, bf16[512,512]{1,0:T(8,128)(2,1)S(1)} %copy-done.23), kind=kOutput, calls=%fused_computation.101 | convolution fusion | flops 2147483648 | bytes 13107200 | tf_op jit(solution)/shard_map/dot_general | solution.py:25
  116.7 5.8 fusion.29
  122.5 22.9 %all-gather.5.cloned.1.call-done = bf16[4096,512]{0,1:T(8,128)(2,1)} async-done(((bf16[1024,512]{0,1:T(8,128)(2,1)}), bf16[4096,512]{0,1:T(8,128)(2,1)}) %all-gather.5.cloned.1.call-update) | async-done | bytes 4194320 | tf_op jit(solution)/shard_map/all_gather | solution.py:254
  145.4 11.9 %multiply_convert_fusion = (bf16[4096,512]{1,0:T(8,128)(2,1)S(1)}, bf16[4096,512]{1,0:T(8,128)(2,1)S(1)}, bf16[4096,512]{1,0:T(8,128)(2,1)}) fusion(f32[4096,512]{1,0:T(8,128)} %fusion.28, f32[4096,512]{1,0:T(8,128)} %fusion.29, bf16[4096,512]{0,1:T(8,128)(2,1)} %all-gather.5.cloned.1.call-done, bf16[512,512]{1,0:T(8,128)(2,1)S(1)} %copy-done), kind=kOutput, calls=%fused_computation.8 | convolution fusion | flops 2178940928 | bytes 34078720 | tf_op jit(solution)/shard_map/dot_general | solution.py:29
  157.3 3.4 convolution_convert_fusion.5
  160.8 3.1 convolution_convert_fusion.6
  164.4 3.2 convolution_convert_fusion.4
  167.7 4.7 fusion.30
  172.4 5.6 convolution_add_fusion
  178.4 6.6 %convolution_convert_fusion = bf16[4096,512]{0,1:T(8,128)(2,1)} fusion(bf16[4096,512]{1,0:T(8,128)(2,1)} %get-tuple-element.51, bf16[512,512]{1,0:T(8,128)(2,1)S(1)} %copy-done), kind=kOutput, calls=%fused_computation.14 | convolution fusion | flops 2149580800 | bytes 8912896 | tf_op jit(solution)/shard_map/dot_general | solution.py:25
  187.8 69.6 %all-reduce.7.cloned.1.call-done = (bf16[512,512]{1,0:T(8,128)(2,1)}, bf16[512,512]{1,0:T(8,128)(2,1)}, bf16[512,512]{1,0:T(8,128)(2,1)}) async-done(((bf16[512,512]{1,0:T(8,128)(2,1)}, bf16[512,512]{1,0:T(8,128)(2,1)}, bf16[512,512]{1,0:T(8,128)(2,1)}), (bf16[512,512]{1,0:T(8,128)(2,1)}, bf16[512,512]{1,0:T(8,128)(2,1)}, bf16[512,512]{1,0:T(8,128)(2,1)})) %all-reduce.7.cloned.1.call-update) | async-done | bytes 1572880 | tf_op jit(solution)/shard_map/psum | solution.py:271
  257.5 2.2 convert_element_type.100
  259.7 2.1 convert_element_type.96
  262.9 68.1 %reduce-scatter.5.cloned.1.call-done = f32[1024,512]{0,1:T(8,128)} async-done(((f32[4096,512]{0,1:T(8,128)}), f32[1024,512]{0,1:T(8,128)}) %reduce-scatter.5.cloned.1.call-update) | async-done | bytes 2097168 | tf_op jit(solution)/shard_map/reduce_scatter | solution.py:258
  331.1 3.0 multiply_reduce_fusion
  334.1 44.1 %reduce-scatter.3.cloned.1.call-done = bf16[1024,512]{0,1:T(8,128)(2,1)} async-done(((bf16[4096,512]{0,1:T(8,128)(2,1)}), bf16[1024,512]{0,1:T(8,128)(2,1)}) %reduce-scatter.3.cloned.1.call-update) | async-done | bytes 1048592 | tf_op jit(solution)/shard_map/reduce_scatter | solution.py:251
  378.2 5.9 multiply_add_fusion.1
  386.7 25.4 %shard_map.222 = (bf16[1024,512]{1,0:T(8,128)(2,1)S(1)}, f32[1536,512]{1,0:T(8,128)}, f32[1536,512]{1,0:T(8,128)}) custom-call(bf16[1024,512]{1,0:T(8,128)(2,1)S(1)} %copy-done.6, bf16[512,1536]{1,0:T(8,128)(2,1)S(1)} %copy.36.key_t_ref, bf16[1536,512]{1,0:T(8,128)(2,1)} %get-tuple-element.56.value_ref, bf16[1024,512]{1,0:T(8,128)(2,1)S(1)} %fusion.1.grad_ref, ...), custom_call_target="tpu_custom_call" | custom-call | flops 6442450944 | bytes 16777216 | tf_op jit(solution)/shard_map/pallas_call | solution.py:183
  412.0 2.8 constant_dynamic-update-slice_fusion.6
  416.2 2.5 slice.76
  418.7 1.7 fusion.17
  421.5 3.7 collective-permute-start.4
  427.3 2.1 fusion.31
  429.4 3.0 copy.40
  434.1 6.1 scatter_custom_fusion
  440.3 5.7 scatter_custom_fusion.1
  446.0 5.7 scatter_custom_fusion.2
  451.7 5.7 scatter_custom_fusion.3
  457.4 2.5 convert.19
  464.4 2.1 fusion.7
  466.5 2.8 multiply_reduce_fusion.1
  470.0 1.8 copy.41
  471.8 42.0 %psum.56 = f32[2048]{0:T(1024)S(1)} all-reduce(f32[2048]{0:T(1024)S(1)} %pad_maximum_fusion.1), channel_id=1, replica_groups=mesh['nodes'=8,'hid'=4] {'nodes','hid'}, use_global_device_ids=true, to_apply=%region_18.0 | all-reduce | flops 2048 | bytes 16384 | tf_op jit(solution)/shard_map/psum | solution.py:312
  515.2 96.2 %all-reduce.5.cloned.1.call-done = (f32[512,512]{1,0:T(8,128)}, f32[512,512]{1,0:T(8,128)}, f32[512,512]{1,0:T(8,128)}, f32[512,512]{1,0:T(8,128)}) async-done(((f32[512,512]{1,0:T(8,128)}, f32[512,512]{1,0:T(8,128)}, f32[512,512]{1,0:T(8,128)}, f32[512,512]{1,0:T(8,128)}), (f32[512,512]{1,0:T(8,128)}, f32[512,512]{1,0:T(8,128)}, f32[512,512]{1,0:T(8,128)}, ...) | async-done | bytes 4194320 | tf_op jit(solution)/shard_map/psum | solution.py:312
  611.4 2.4 copy.72
  (161 shorter events, 41.9 us)
Async XLA Ops:
  7.2 138.3 %copy-start = (bf16[512,512]{1,0:T(8,128)(2,1)S(1)}, bf16[512,512]{1,0:T(8,128)(2,1)}, u32[]{:S(2)}) copy-start(bf16[512,512]{1,0:T(8,128)(2,1)} %param.23) | copy-start | bytes 1572868
  7.2 101.6 %all-gather.3.cloned.1.call-start = ((), (), s32[]{:S(2)}) async-start(), calls=%async_computation.2 | async-start | bytes 5242880 | tf_op jit(solution)/shard_map/all_gather | solution.py:246
  9.2 3.1 copy-start.7
  9.2 2.9 copy-start.39
  9.2 2.9 copy-start.40
  13.2 2.2 copy-start.27
  18.9 19.7 %collective-permute-start = (bf16[128,1024]{1,0:T(8,128)(2,1)}, bf16[128,1024]{1,0:T(8,128)(2,1)}, u32[]{:S(2)}, u32[]{:S(2)}) collective-permute-start(bf16[128,1024]{1,0:T(8,128)(2,1)} %gather_fusion), channel_id=1, source_target_pairs={{31,0},{0,1},{1,2},{2,3},{3,4},{4,5},{5,6},{6,7},{7,8},{8,9},{9,10... | collective-permute-start | bytes 786440 | tf_op jit(solution)/shard_map/ppermute | solution.py:21
  20.2 19.3 %collective-permute-start.1 = (bf16[128,1024]{1,0:T(8,128)(2,1)S(1)}, bf16[128,1024]{1,0:T(8,128)(2,1)}, u32[]{:S(2)}, u32[]{:S(2)}) collective-permute-start(bf16[128,1024]{1,0:T(8,128)(2,1)S(1)} %gather_fusion.1), channel_id=1, source_target_pairs={{1,0},{2,1},{3,2},{4,3},{5,4},{6,5},{7,6},{8,7},{9,8},{10,9},{11,1... | collective-permute-start | bytes 786440 | tf_op jit(solution)/shard_map/ppermute | solution.py:21
  26.2 8.8 %copy-start.32 = (bf16[512,512]{1,0:T(8,128)(2,1)S(1)}, bf16[512,512]{1,0:T(8,128)(2,1)}, u32[]{:S(2)}) copy-start(bf16[512,512]{1,0:T(8,128)(2,1)} %param.17) | copy-start | bytes 1572868
  27.7 12.8 %collective-permute-start.2 = (bf16[128,1024]{1,0:T(8,128)(2,1)}, bf16[128,1024]{1,0:T(8,128)(2,1)}, u32[]{:S(2)}, u32[]{:S(2)}) collective-permute-start(bf16[128,1024]{1,0:T(8,128)(2,1)} %gather_fusion.2), channel_id=1, source_target_pairs={{30,0},{31,1},{0,2},{1,3},{2,4},{3,5},{4,6},{5,7},{6,8},{7,9},{8,1... | collective-permute-start | bytes 786440 | tf_op jit(solution)/shard_map/ppermute | solution.py:21
  29.3 9.2 %copy-start.15 = (bf16[1536,1024]{1,0:T(8,128)(2,1)S(1)}, bf16[1536,1024]{1,0:T(8,128)(2,1)}, u32[]{:S(2)}) copy-start(bf16[1536,1024]{1,0:T(8,128)(2,1)} %get-tuple-element.63) | copy-start | bytes 9437188
  29.3 12.2 %collective-permute-start.3 = (bf16[128,1024]{1,0:T(8,128)(2,1)}, bf16[128,1024]{1,0:T(8,128)(2,1)S(1)}, u32[]{:S(2)}, u32[]{:S(2)}) collective-permute-start(bf16[128,1024]{1,0:T(8,128)(2,1)} %gather_fusion.3), channel_id=1, source_target_pairs={{2,0},{3,1},{4,2},{5,3},{6,4},{7,5},{8,6},{9,7},{10,8},{11,9},{12,... | collective-permute-start | bytes 786440 | tf_op jit(solution)/shard_map/ppermute | solution.py:21
  43.9 2.6 copy-start.4
  49.2 20.3 %copy-start.8 = (f32[1024,512]{0,1:T(8,128)S(1)}, f32[1024,512]{0,1:T(8,128)}, u32[]{:S(2)}) copy-start(f32[1024,512]{0,1:T(8,128)} %copy-done.7) | copy-start | bytes 6291460
  49.2 20.3 %copy-start.25 = (bf16[512,512]{1,0:T(8,128)(2,1)S(1)}, bf16[512,512]{1,0:T(8,128)(2,1)}, u32[]{:S(2)}) copy-start(bf16[512,512]{1,0:T(8,128)(2,1)} %param.20) | copy-start | bytes 1572868
  73.0 72.5 %all-gather.5.cloned.1.call-start = ((), (), s32[]{:S(2)}) async-start(), calls=%async_computation.4 | async-start | bytes 5242880 | tf_op jit(solution)/shard_map/all_gather | solution.py:254
  75.9 32.9 %copy-start.23 = (bf16[512,512]{1,0:T(8,128)(2,1)S(1)}, bf16[512,512]{1,0:T(8,128)(2,1)}, u32[]{:S(2)}) copy-start(bf16[512,512]{1,0:T(8,128)(2,1)} %param.21) | copy-start | bytes 1572868
  78.8 37.9 %copy-start.22 = (bf16[512,512]{1,0:T(8,128)(2,1)S(1)}, bf16[512,512]{1,0:T(8,128)(2,1)}, u32[]{:S(2)}) copy-start(bf16[512,512]{1,0:T(8,128)(2,1)} %param.22) | copy-start | bytes 1572868
  78.8 178.7 %all-reduce.7.cloned.1.call-start = ((), (), s32[]{:S(2)}) async-start(), calls=%async_computation.7 | async-start | bytes 3145728 | tf_op jit(solution)/shard_map/psum | solution.py:271
  108.8 7.9 %copy-start.13 = (bf16[4096,512]{0,1:T(8,128)(2,1)S(1)}, bf16[4096,512]{0,1:T(8,128)(2,1)}, u32[]{:S(2)}) copy-start(bf16[4096,512]{0,1:T(8,128)(2,1)} %all-gather.3.cloned.1.call-done) | copy-start | bytes 12582916
  145.4 11.9 %copy-start.14 = (bf16[4096,512]{0,1:T(8,128)(2,1)S(1)}, bf16[4096,512]{0,1:T(8,128)(2,1)}, u32[]{:S(2)}) copy-start(bf16[4096,512]{0,1:T(8,128)(2,1)} %all-gather.3.cloned.1.call-done) | copy-start | bytes 12582916
  157.3 3.4 copy-start.18
  157.3 3.4 copy-start.20
  160.8 3.1 copy-start.42
  160.8 3.7 copy-start.43
  167.6 163.5 %reduce-scatter.5.cloned.1.call-start = ((), (), s32[]{:S(2)}) async-start(), calls=%async_computation.5 | async-start | bytes 10485760 | tf_op jit(solution)/shard_map/reduce_scatter | solution.py:258
  167.7 4.7 copy-start.19
  178.0 200.2 %reduce-scatter.3.cloned.1.call-start = ((), (), s32[]{:S(2)}) async-start(), calls=%async_computation.3 | async-start | bytes 5242880 | tf_op jit(solution)/shard_map/reduce_scatter | solution.py:251
  185.0 426.4 %all-reduce.5.cloned.1.call-start = ((), (), s32[]{:S(2)}) async-start(), calls=%async_computation.6 | async-start | bytes 8388608 | tf_op jit(solution)/shard_map/psum | solution.py:312
  257.5 4.4 copy-start.38
  378.2 5.9 copy-start.24
  384.0 34.7 %copy-start.11 = (f32[1024,512]{0,1:T(8,128)}, f32[1024,512]{0,1:T(8,128)S(1)}, u32[]{:S(2)}) copy-start(f32[1024,512]{0,1:T(8,128)S(1)} %get-tuple-element.60) | copy-start | bytes 6291460
  412.0 15.3 %copy-start.2 = (bf16[1024,512]{1,0:T(8,128)(2,1)}, bf16[1024,512]{1,0:T(8,128)(2,1)S(1)}, u32[]{:S(2)}) copy-start(bf16[1024,512]{1,0:T(8,128)(2,1)S(1)} %get-tuple-element.20) | copy-start | bytes 3145732
  412.0 3.2 copy-start.21
  420.5 6.9 %copy-start.33 = (bf16[512,512]{1,0:T(8,128)(2,1)S(1)}, bf16[512,512]{1,0:T(8,128)(2,1)}, u32[]{:S(2)}) copy-start(bf16[512,512]{1,0:T(8,128)(2,1)} %param.17) | copy-start | bytes 1572868
  421.5 12.6 %collective-permute-start.4 = (bf16[128,1024]{1,0:T(8,128)(2,1)}, bf16[128,1024]{1,0:T(8,128)(2,1)}, u32[]{:S(2)}, u32[]{:S(2)}) collective-permute-start(bf16[128,1024]{1,0:T(8,128)(2,1)} %get-tuple-element.55), channel_id=1, source_target_pairs={{1,0},{2,1},{3,2},{4,3},{5,4},{6,5},{7,6},{8,7},{9,8},{10,9},{11,1... | collective-permute-start | bytes 786440 | tf_op jit(solution)/shard_map/ppermute | solution.py:21
  425.1 15.1 %collective-permute-start.5 = (bf16[128,1024]{1,0:T(8,128)(2,1)}, bf16[128,1024]{1,0:T(8,128)(2,1)S(1)}, u32[]{:S(2)}, u32[]{:S(2)}) collective-permute-start(bf16[128,1024]{1,0:T(8,128)(2,1)} %get-tuple-element.54), channel_id=1, source_target_pairs={{31,0},{0,1},{1,2},{2,3},{3,4},{4,5},{5,6},{6,7},{7,8},{8,9},{9,10... | collective-permute-start | bytes 786440 | tf_op jit(solution)/shard_map/ppermute | solution.py:21
  425.1 20.8 %collective-permute-start.6 = (bf16[128,1024]{1,0:T(8,128)(2,1)}, bf16[128,1024]{1,0:T(8,128)(2,1)S(1)}, u32[]{:S(2)}, u32[]{:S(2)}) collective-permute-start(bf16[128,1024]{1,0:T(8,128)(2,1)} %get-tuple-element.53), channel_id=1, source_target_pairs={{2,0},{3,1},{4,2},{5,3},{6,4},{7,5},{8,6},{9,7},{10,8},{11,9},{12,... | collective-permute-start | bytes 786440 | tf_op jit(solution)/shard_map/ppermute | solution.py:21
  426.6 25.1 %collective-permute-start.7 = (bf16[128,1024]{1,0:T(8,128)(2,1)}, bf16[128,1024]{1,0:T(8,128)(2,1)S(1)}, u32[]{:S(2)}, u32[]{:S(2)}) collective-permute-start(bf16[128,1024]{1,0:T(8,128)(2,1)} %get-tuple-element.52), channel_id=1, source_target_pairs={{30,0},{31,1},{0,2},{1,3},{2,4},{3,5},{4,6},{5,7},{6,8},{7,9},{8,1... | collective-permute-start | bytes 786440 | tf_op jit(solution)/shard_map/ppermute | solution.py:21
  429.4 3.0 copy-start.3
  429.4 3.0 copy-start.28
  463.3 3.2 copy-start.16
  464.4 2.1 copy-start.9
  464.4 2.1 copy-start.37
  466.5 2.8 copy-start.12
  611.4 2.4 copy-start.31
  611.4 3.4 copy-start.30
  613.8 1.9 copy-start.29
  (10 other events, 12.5 us)
Sparse Core Ops, SparseCore 0:
  73.1 35.6 all-gather.2
  110.9 34.4 all-gather.4
  167.7 89.7 all-reduce.6
  259.9 71.0 reduce-scatter.4
  333.6 44.5 reduce-scatter.2
  463.5 147.8 all-reduce.4

commit v2 on v1

v2 whole, which is shorter than its diff:
```python
import functools

import jax
import jax.numpy as jnp
from jax import lax
from jax.experimental import pallas as pl
from jax.experimental.pallas import tpu as pltpu
from jax.sharding import PartitionSpec as P

HEADS = 4
HEAD_DIM = 128
NEIGH = 16
BLOCK = 512
ROW_BLOCK = 256

epsilon = 1e-06
halo_steps = (1, -1, 2, -2)
highest = lax.Precision.HIGHEST
score_scale = HEAD_DIM ** (-0.5)
low_type = jnp.bfloat16
everywhere = ("nodes", "hid")
whole = pl.BlockSpec(memory_space=pltpu.VMEM)
scalars = pl.BlockSpec(memory_space=pltpu.SMEM)


def dot(left, right, left_dim, right_dim):
    return lax.dot_general(
        left, right, (((left_dim,), (right_dim,)), ((), ())), preferred_element_type=jnp.float32
    )


def shaped(shape, dtype=low_type):
    return jax.ShapeDtypeStruct(shape, dtype)


def norm_parts(states):
    centred = states - jnp.mean(states, axis=-1, keepdims=True)
    inverse = lax.rsqrt(jnp.mean(centred * centred, axis=-1, keepdims=True) + epsilon)
    return (centred * inverse, inverse)


def norm_back(grad_plain, plain, inverse):
    first_mean = jnp.mean(grad_plain, axis=-1, keepdims=True)
    second_mean = jnp.mean(grad_plain * plain, axis=-1, keepdims=True)
    return inverse * (grad_plain - first_mean - plain * second_mean)


def call(kernel, out_shape, args, specs=None, scratch=(), flops=0, moved=0):
    single = not isinstance(out_shape, list)
    return pl.pallas_call(
        kernel,
        in_specs=specs or [whole] * len(args),
        out_specs=whole if single else [whole] * len(out_shape),
        out_shape=out_shape,
        scratch_shapes=list(scratch),
        compiler_params=pltpu.CompilerParams(vmem_limit_bytes=56 * 2**20),
        cost_estimate=pl.CostEstimate(flops=flops, bytes_accessed=moved, transcendentals=0),
    )(*args)


def chosen_rows(send_ref, position, rows):
    sends = send_ref.shape[1]
    place = lax.broadcasted_iota(jnp.int32, (rows, sends), 0)
    return jnp.where(place == send_ref[position : position + 1, :], 1.0, 0.0).astype(low_type)


def prepare_kernel(states_ref, condition_ref, mod_w_ref, send_ref, normed_ref, modulation_ref, *parcel_refs):
    width = states_ref.shape[1]
    mixed = jnp.sum(condition_ref[...] * mod_w_ref[...].astype(jnp.float32), axis=0, keepdims=True)
    for piece in range(4):
        modulation_ref[piece : piece + 1, :] = mixed[:, piece * width : (piece + 1) * width]

    @pl.loop(0, states_ref.shape[0] // ROW_BLOCK)
    def _(step):
        rows = pl.ds(pl.multiple_of(step * ROW_BLOCK, ROW_BLOCK), ROW_BLOCK)
        plain, _ = norm_parts(states_ref[rows, :])
        normed_ref[rows, :] = (plain * (1.0 + modulation_ref[0:1, :]) + modulation_ref[1:2, :]).astype(low_type)

    for position, parcel_ref in enumerate(parcel_refs):
        chosen = chosen_rows(send_ref, position, states_ref.shape[0])
        parcel_ref[...] = dot(chosen, normed_ref[...], 0, 0).astype(low_type)


def project_kernel(normed_ref, near_ref, w_query_ref, w_key_ref, w_value_ref, query_ref, key_ref, value_ref, packed_ref):
    rows = normed_ref.shape[0]

    @pl.loop(0, rows // ROW_BLOCK)
    def _(step):
        part = pl.ds(pl.multiple_of(step * ROW_BLOCK, ROW_BLOCK), ROW_BLOCK)
        for weight_ref, out_ref in ((w_query_ref, query_ref), (w_key_ref, key_ref), (w_value_ref, value_ref)):
            out_ref[part, :] = dot(normed_ref[part, :], weight_ref[...], 1, 0).astype(low_type)

    half = (rows + 512) // 256

    @pl.loop(0, rows // 128)
    def _(step):
        cols = pl.ds(pl.multiple_of(step * 128, 128), 128)
        near = near_ref[:, cols]
        group = near >> 7
        upper = group >= half
        unit = jnp.left_shift(1, 5 * jnp.where(upper, group - half, group))
        low = near & 127
        low_unit = jnp.where(upper, 0, unit)
        high_unit = jnp.where(upper, unit, 0)
        place = lax.broadcasted_iota(jnp.int32, (128, 128), 0)
        low_count = jnp.zeros((128, 128), jnp.int32)
        high_count = low_count
        for n in range(NEIGH):
            same = low[n : n + 1] == place
            low_count = low_count + jnp.where(same, low_unit[n : n + 1], 0)
            high_count = high_count + jnp.where(same, high_unit[n : n + 1], 0)
        packed_ref[0, :, cols] = low_count
        packed_ref[1, :, cols] = high_count


def attend_kernel(
    packed_ref, query_ref, key_own_ref, value_own_ref, w_key_ref, w_value_ref, *refs
):
    landed_refs, (attended_ref, raised_ref, inverse_ref, spread_ref, key_ref, value_ref) = refs[:4], refs[4:10]
    bias, scores, value_t = refs[10:]
    ext, rows = bias.shape
    groups = ext // 128
    half = groups // 2

    @pl.when(pl.program_id(0) == 0)
    def _():
        @pl.loop(0, rows // 128)
        def _(step):
            cols = pl.ds(pl.multiple_of(step * 128, 128), 128)
            for g in range(groups):
                count = (packed_ref[g // half, :, cols] >> (5 * (g % half))) & 31
                bias[g * 128 : (g + 1) * 128, cols] = jnp.where(
                    count > 0, jnp.log(count.astype(jnp.float32)), -1e30
                )

    key_ref[:rows, :] = key_own_ref[...]
    value_ref[:rows, :] = value_own_ref[...]
    for position, landed_ref in enumerate(landed_refs):
        sends = landed_ref.shape[0]
        part = slice(rows + position * sends, rows + (position + 1) * sends)
        key_ref[part, :] = dot(landed_ref[...], w_key_ref[...], 1, 0).astype(low_type)
        value_ref[part, :] = dot(landed_ref[...], w_value_ref[...], 1, 0).astype(low_type)
    value_t[...] = value_ref[...].T

    width = scores.shape[1]

    @pl.loop(0, rows // width)
    def _(step):
        cols = pl.ds(pl.multiple_of(step * width, width), width)
        query = query_ref[cols, :]
        top = jnp.full((8, width), -jnp.inf, jnp.float32)
        for g in range(groups):
            part = slice(g * 128, (g + 1) * 128)
            score = dot(key_ref[part, :], query, 1, 1) * score_scale + bias[part, cols]
            scores[part, :] = score
            top = jnp.maximum(top, jnp.max(score.reshape(16, 8, width), axis=0))
        top = jnp.max(top, axis=0, keepdims=True)
        total = jnp.zeros((8, width), jnp.float32)
        for g in range(groups):
            part = slice(g * 128, (g + 1) * 128)
            raised = jnp.exp(scores[part, :] - top)
            total = total + jnp.sum(raised.reshape(16, 8, width), axis=0)
            raised_ref[0, part, cols] = raised.astype(low_type)
        inverse = 1.0 / jnp.sum(total, axis=0, keepdims=True)
        inverse_ref[0, :, cols] = inverse
        spread_ref[cols, :] = jnp.broadcast_to(inverse, (HEAD_DIM, width)).T
        mixed = dot(value_t[...], raised_ref[0, :, cols], 1, 0) * inverse
        attended_ref[cols, :] = mixed.T.astype(low_type)


def attend(packed, queries, keys, values, w_key, w_value, landed):
    rows, width = queries.shape
    ext = rows + sum(part.shape[0] for part in landed)
    by_row = pl.BlockSpec((rows, HEAD_DIM), lambda h: (0, h))
    by_ext = pl.BlockSpec((ext, HEAD_DIM), lambda h: (0, h))
    by_weight = pl.BlockSpec((width, HEAD_DIM), lambda h: (0, h))
    return pl.pallas_call(
        attend_kernel,
        grid=(HEADS,),
        in_specs=[
            pl.BlockSpec(packed.shape, lambda h: (0, 0, 0)),
            by_row,
            by_row,
            by_row,
            by_weight,
            by_weight,
        ]
        + [pl.BlockSpec(part.shape, lambda h: (0, 0)) for part in landed],
        out_specs=[
            by_row,
            pl.BlockSpec((1, ext, rows), lambda h: (h, 0, 0)),
            pl.BlockSpec((1, 1, rows), lambda h: (h, 0, 0)),
            by_row,
            by_ext,
            by_ext,
        ],
        out_shape=[
            shaped((rows, width)),
            shaped((HEADS, ext, rows)),
            shaped((HEADS, 1, rows), jnp.float32),
            shaped((rows, width), jnp.float32),
            shaped((ext, width)),
            shaped((ext, width)),
        ],
        scratch_shapes=[
            pltpu.VMEM((ext, rows), jnp.float32),
            pltpu.VMEM((ext, BLOCK), jnp.float32),
            pltpu.VMEM((HEAD_DIM, ext), low_type),
        ],
        compiler_params=pltpu.CompilerParams(vmem_limit_bytes=56 * 2**20),
        cost_estimate=pl.CostEstimate(flops=2**35, bytes_accessed=2**24, transcendentals=0),
    )(packed, queries, keys, values, w_key, w_value, *landed)


def attend_back_kernel(
    query_ref, key_ref, value_ref, grad_ref, raised_ref, inverse_ref, grad_query_ref, grad_key_ref, grad_value_ref, terms, low, key_t
):
    ext, rows = low.shape
    width = terms.shape[1]
    key_t[...] = key_ref[...].T

    @pl.loop(0, rows // width)
    def _(step):
        cols = pl.ds(pl.multiple_of(step * width, width), width)
        grad = grad_ref[cols, :]
        total = jnp.zeros((8, width), jnp.float32)
        for g in range(ext // 128):
            part = slice(g * 128, (g + 1) * 128)
            term = dot(value_ref[part, :], grad, 1, 1) * raised_ref[0, part, cols].astype(jnp.float32)
            terms[part, :] = term
            total = total + jnp.sum(term.reshape(16, 8, width), axis=0)
        mean = jnp.sum(total, axis=0, keepdims=True) * inverse_ref[0, :, cols]
        for g in range(ext // 128):
            part = slice(g * 128, (g + 1) * 128)
            low[part, cols] = (terms[part, :] - raised_ref[0, part, cols].astype(jnp.float32) * mean).astype(low_type)
        grad_query = dot(key_t[...], low[:, cols], 1, 0) * score_scale
        grad_query_ref[cols, :] = grad_query.T.astype(low_type)

    grad_value_ref[...] = dot(raised_ref[0], grad_ref[...], 1, 0).astype(low_type)
    grad_key_ref[...] = (dot(low[...], query_ref[...], 1, 0) * score_scale).astype(low_type)


def attend_back(first, heads, queries, keys, values, grads, raised, inverse):
    rows, ext = queries.shape[0], values.shape[0]
    by_row = pl.BlockSpec((rows, HEAD_DIM), lambda h: (0, h + first))
    by_ext = pl.BlockSpec((ext, HEAD_DIM), lambda h: (0, h + first))
    to_row = pl.BlockSpec((rows, HEAD_DIM), lambda h: (0, h))
    to_ext = pl.BlockSpec((ext, HEAD_DIM), lambda h: (0, h))
    return pl.pallas_call(
        attend_back_kernel,
        grid=(heads,),
        in_specs=[
            by_row,
            by_ext,
            by_ext,
            by_row,
            pl.BlockSpec((1, ext, rows), lambda h: (h + first, 0, 0)),
            pl.BlockSpec((1, 1, rows), lambda h: (h + first, 0, 0)),
        ],
        out_specs=[to_row, to_ext, to_ext],
        out_shape=[
            shaped((rows, heads * HEAD_DIM)),
            shaped((ext, heads * HEAD_DIM)),
            shaped((ext, heads * HEAD_DIM)),
        ],
        scratch_shapes=[
            pltpu.VMEM((ext, BLOCK), jnp.float32),
            pltpu.VMEM((ext, rows), low_type),
            pltpu.VMEM((HEAD_DIM, ext), low_type),
        ],
        compiler_params=pltpu.CompilerParams(vmem_limit_bytes=56 * 2**20),
        cost_estimate=pl.CostEstimate(flops=heads * 2**33, bytes_accessed=2**22, transcendentals=0),
    )(queries, keys, values, grads, raised, inverse)


def live_rows(count_ref, start, rows):
    place = lax.broadcasted_iota(jnp.int32, (rows, 1), 0) + start
    return (place < count_ref[0]).astype(jnp.float32)


def feed_chunk(weight_ref, second_ref, branch_ref, out_ref, grad_ref, hidden, grad_gate, grad_up, weight_grad_ref, fresh):
    width = second_ref.shape[1]
    units = weight_ref.shape[1]
    gate_rows, up_rows, down_rows = (slice(i * units, (i + 1) * units) for i in range(3))

    @pl.loop(0, second_ref.shape[0] // ROW_BLOCK)
    def _(step):
        rows = pl.ds(pl.multiple_of(step * ROW_BLOCK, ROW_BLOCK), ROW_BLOCK)
        second = second_ref[rows, :]
        gate = dot(second, weight_ref[gate_rows, :], 1, 0)
        up = dot(second, weight_ref[up_rows, :], 1, 0)
        sigmoid = 1.0 / (1.0 + jnp.exp(-gate))
        activated = gate * sigmoid
        hidden[rows, :] = (activated * up).astype(low_type)
        back = dot(branch_ref[rows, :], weight_ref[down_rows, :], 1, 1)
        grad_gate[rows, :] = (back * up * (sigmoid + activated * (1.0 - sigmoid))).astype(low_type)
        grad_up[rows, :] = (back * activated).astype(low_type)
        out = dot(hidden[rows, :], weight_ref[down_rows, :], 1, 0)
        grad = dot(grad_gate[rows, :], weight_ref[gate_rows, :], 1, 1) + dot(
            grad_up[rows, :], weight_ref[up_rows, :], 1, 1
        )
        if fresh:
            out_ref[rows, :] = out
            grad_ref[rows, :] = grad
        else:
            out_ref[rows, :] += out
            grad_ref[rows, :] += grad

    weight_grad_ref[gate_rows, :] = dot(second_ref[...], grad_gate[...], 0, 0).astype(low_type)
    weight_grad_ref[up_rows, :] = dot(second_ref[...], grad_up[...], 0, 0).astype(low_type)
    weight_grad_ref[down_rows, :] = dot(hidden[...], branch_ref[...], 0, 0).astype(low_type)


def feed_first_kernel(
    count_ref, modulation_ref, states_ref, cotangent_ref, attended_ref, w_out_ref, weight_a_ref, weight_b_ref,
    middle_ref, second_ref, branch_ref, out_ref, grad_ref, weight_grad_a_ref, weight_grad_b_ref,
    hidden, grad_gate, grad_up,
):
    @pl.loop(0, states_ref.shape[0] // ROW_BLOCK)
    def _(step):
        start = pl.multiple_of(step * ROW_BLOCK, ROW_BLOCK)
        rows = pl.ds(start, ROW_BLOCK)
        live = live_rows(count_ref, start, ROW_BLOCK)
        middle = states_ref[rows, :] + live * dot(attended_ref[rows, :], w_out_ref[...], 1, 0)
        middle_ref[rows, :] = middle
        plain, _ = norm_parts(middle)
        second_ref[rows, :] = (plain * (1.0 + modulation_ref[2:3, :]) + modulation_ref[3:4, :]).astype(low_type)
        branch_ref[rows, :] = (live * cotangent_ref[rows, :]).astype(low_type)

    for weight_ref, weight_grad_ref, fresh in (
        (weight_a_ref, weight_grad_a_ref, True),
        (weight_b_ref, weight_grad_b_ref, False),
    ):
        feed_chunk(
            weight_ref, second_ref, branch_ref, out_ref, grad_ref, hidden, grad_gate, grad_up, weight_grad_ref, fresh
        )


def feed_last_kernel(
    count_ref, modulation_ref, cotangent_ref, attended_ref, w_out_ref, spread_ref, weight_a_ref, weight_b_ref,
    middle_ref, second_ref, branch_ref, out_in_ref, grad_in_ref,
    output_ref, grad_middle_ref, grad_attended_ref, w_out_grad_ref, mod_grad_ref, weight_grad_a_ref, weight_grad_b_ref,
    hidden, grad_gate, grad_up, out, grad,
):
    for weight_ref, weight_grad_ref, fresh in (
        (weight_a_ref, weight_grad_a_ref, True),
        (weight_b_ref, weight_grad_b_ref, False),
    ):
        feed_chunk(weight_ref, second_ref, branch_ref, out, grad, hidden, grad_gate, grad_up, weight_grad_ref, fresh)
    mod_grad_ref[...] = jnp.zeros_like(mod_grad_ref)
    low_grad = hidden

    @pl.loop(0, middle_ref.shape[0] // ROW_BLOCK)
    def _(step):
        start = pl.multiple_of(step * ROW_BLOCK, ROW_BLOCK)
        rows = pl.ds(start, ROW_BLOCK)
        live = live_rows(count_ref, start, ROW_BLOCK)
        middle = middle_ref[rows, :]
        output_ref[rows, :] = middle + live * (out_in_ref[rows, :] + out[rows, :])
        plain, inverse = norm_parts(middle)
        grad_second = grad_in_ref[rows, :] + grad[rows, :]
        mod_grad_ref[0:1, :] += jnp.sum(grad_second * plain, axis=0, keepdims=True)
        mod_grad_ref[1:2, :] += jnp.sum(grad_second, axis=0, keepdims=True)
        grad_middle = cotangent_ref[rows, :] + norm_back(grad_second * (1.0 + modulation_ref[2:3, :]), plain, inverse)
        grad_middle_ref[rows, :] = grad_middle
        low_grad[rows, :] = (live * grad_middle).astype(low_type)
        grad_attended = dot(low_grad[rows, :], w_out_ref[...], 1, 1) * spread_ref[rows, :]
        grad_attended_ref[rows, :] = grad_attended.astype(low_type)

    w_out_grad_ref[...] = dot(attended_ref[...], low_grad[...], 0, 0).astype(low_type)


def project_back_kernel(parts, normed_ref, w_query_ref, w_key_ref, w_value_ref, *refs):
    landed_refs, refs = refs[:4], refs[4:]
    pieces, refs = refs[: 3 * parts], refs[3 * parts :]
    weight_grad_ref, grad_normed_ref, *parcel_refs = refs
    rows, width = normed_ref.shape
    cols = width // parts
    for kind, weight_ref in enumerate((w_query_ref, w_key_ref, w_value_ref)):
        for part in range(parts):
            piece = pieces[part * 3 + kind]
            to = slice(part * cols, (part + 1) * cols)
            grad = dot(normed_ref[...], piece[:rows, :], 0, 0)
            if kind:
                for position, landed_ref in enumerate(landed_refs):
                    sends = landed_ref.shape[0]
                    lower = rows + position * sends
                    grad += dot(landed_ref[...], piece[lower : lower + sends, :], 0, 0)
            weight_grad_ref[kind * width : (kind + 1) * width, to] = grad.astype(low_type)
    for position, parcel_ref in enumerate(parcel_refs):
        sends = parcel_ref.shape[0]
        lower = rows + position * sends
        parcel_ref[...] = sum(
            dot(pieces[part * 3 + kind][lower : lower + sends, :], weight_ref[:, part * cols : (part + 1) * cols], 1, 1)
            for part in range(parts)
            for kind, weight_ref in ((1, w_key_ref), (2, w_value_ref))
        ).astype(low_type)

    @pl.loop(0, rows // ROW_BLOCK)
    def _(step):
        block = pl.ds(pl.multiple_of(step * ROW_BLOCK, ROW_BLOCK), ROW_BLOCK)
        grad_normed_ref[block, :] = sum(
            dot(pieces[part * 3 + kind][block, :], weight_ref[:, part * cols : (part + 1) * cols], 1, 1)
            for part in range(parts)
            for kind, weight_ref in enumerate((w_query_ref, w_key_ref, w_value_ref))
        )


def finish_kernel(states_ref, modulation_ref, send_ref, grad_normed_ref, grad_middle_ref, *refs):
    returned_refs, (grad_states_ref, mod_grad_ref, chosen) = refs[:4], refs[4:]
    rows = states_ref.shape[0]
    sends = send_ref.shape[1]
    for position in range(len(returned_refs)):
        chosen[:, position * sends : (position + 1) * sends] = chosen_rows(send_ref, position, rows)
    mod_grad_ref[...] = jnp.zeros_like(mod_grad_ref)

    @pl.loop(0, rows // ROW_BLOCK)
    def _(step):
        block = pl.ds(pl.multiple_of(step * ROW_BLOCK, ROW_BLOCK), ROW_BLOCK)
        grad = grad_normed_ref[block, :]
        for position, returned_ref in enumerate(returned_refs):
            grad += dot(chosen[block, position * sends : (position + 1) * sends], returned_ref[...], 1, 0)
        plain, inverse = norm_parts(states_ref[block, :])
        mod_grad_ref[0:1, :] += jnp.sum(grad * plain, axis=0, keepdims=True)
        mod_grad_ref[1:2, :] += jnp.sum(grad, axis=0, keepdims=True)
        grad_states_ref[block, :] = grad_middle_ref[block, :] + norm_back(
            grad * (1.0 + modulation_ref[0:1, :]), plain, inverse
        )


def from_behind(block, axis, distance):
    devices = range(lax.axis_size(axis))
    route = [((i - distance) % len(devices), i) for i in devices]
    return lax.ppermute(block, axis, route)


def swap(block, axis, bit):
    return lax.ppermute(block, axis, [(i, i ^ (1 << bit)) for i in range(lax.axis_size(axis))])


def axis_bits(axis):
    return [(axis, bit) for bit in range(lax.axis_size(axis).bit_length() - 1)]


def side(axis, bit):
    return (lax.axis_index(axis) >> bit) & 1


def halve_sum(block, links):
    for axis, bit in links:
        half = block.shape[0] // 2
        here = side(axis, bit)
        kept = lax.dynamic_slice_in_dim(block, here * half, half)
        sent = lax.dynamic_slice_in_dim(block, (1 - here) * half, half)
        block = kept + swap(sent, axis, bit)
    return block


def join(block, links):
    for axis, bit in reversed(links):
        other = swap(block, axis, bit)
        here = side(axis, bit)
        block = jnp.where(here == 0, jnp.concatenate([block, other]), jnp.concatenate([other, block]))
    return block


def sum_all(block, links):
    return join(halve_sum(block, links), links)


def body(
    states,
    condition,
    mod_w,
    w_query,
    w_key,
    w_value,
    w_out,
    w_gate,
    w_up,
    w_down,
    counts,
    send_rows,
    neighbours,
    cotangent,
):
    rows, width = states.shape
    sends = send_rows.shape[2]
    ext = rows + len(halo_steps) * sends
    f32 = jnp.float32
    parcel = shaped((sends, width))
    send_list = send_rows[0]

    normed, modulation, *parcels = call(
        prepare_kernel,
        [shaped((rows, width)), shaped((4, width), f32)] + [parcel] * 4,
        (states, condition[:, None], mod_w, send_list),
        flops=2**30,
        moved=2**22,
    )
    landed = [from_behind(part, everywhere, hop) for part, hop in zip(parcels, halo_steps)]
    queries, keys, values, packed = call(
        project_kernel,
        [shaped((rows, width))] * 3 + [shaped((2, 128, rows), jnp.int32)],
        (normed, neighbours.T, w_query, w_key, w_value),
        flops=2**32,
        moved=2**22,
    )

    own_weights = jnp.concatenate([w_gate, w_up, w_down], axis=0)
    core_weights = swap(own_weights, "hid", 0)
    landed, late_weights = lax.optimization_barrier((landed, own_weights))
    far_weights = swap(late_weights, "hid", 1)
    cross_weights = swap(far_weights, "hid", 0)

    attended, raised, inverse, spread, keys, values = attend(packed, queries, keys, values, w_key, w_value, landed)

    low_rows = shaped((rows, width))
    wide_rows = shaped((rows, width), f32)
    weight_grad = shaped(own_weights.shape)
    row_scratch = [pltpu.VMEM((rows, width), low_type)] * 3
    middle, second, branch, out, grad, own_grad, core_grad = call(
        feed_first_kernel,
        [wide_rows, low_rows, low_rows, wide_rows, wide_rows, weight_grad, weight_grad],
        (counts, modulation, states, cotangent, attended, w_out, own_weights, core_weights),
        specs=[scalars] + [whole] * 7,
        scratch=row_scratch,
        flops=2**34,
        moved=2**24,
    )
    output, grad_middle, grad_attended, w_out_grad, mod_two, far_grad, cross_grad = call(
        feed_last_kernel,
        [wide_rows, wide_rows, low_rows, shaped((width, width)), shaped((2, width), f32), weight_grad, weight_grad],
        (counts, modulation, cotangent, attended, w_out, spread, far_weights, cross_weights)
        + (middle, second, branch, out, grad),
        specs=[scalars] + [whole] * 12,
        scratch=row_scratch + [pltpu.VMEM((rows, width), f32)] * 2,
        flops=2**34,
        moved=2**24,
    )

    node_links = axis_bits("nodes")
    all_links = axis_bits("hid") + node_links
    own_grad = own_grad + swap(core_grad, "hid", 0)
    far_grad = far_grad + swap(cross_grad, "hid", 0)
    own_grad = own_grad + swap(far_grad, "hid", 1)
    own_grad = sum_all(own_grad, node_links)
    grad_w_gate, grad_w_up, grad_w_down = jnp.split(own_grad.astype(f32), 3)
    grad_w_out = sum_all(w_out_grad, all_links).astype(f32)

    parts = 2
    pieces = []
    for part in range(parts):
        heads = HEADS // parts
        pieces += attend_back(part * heads, heads, queries, keys, values, grad_attended, raised, inverse)
    attn_grad, grad_normed, *parcels = call(
        functools.partial(project_back_kernel, parts),
        [shaped((3 * width, width)), wide_rows] + [parcel] * 4,
        (normed, w_query, w_key, w_value, *landed, *pieces),
        flops=2**32,
        moved=2**23,
    )
    returned = [from_behind(part, everywhere, -hop) for part, hop in zip(parcels, halo_steps)]
    attn_grad = sum_all(attn_grad, all_links)
    grad_w_query, grad_w_key, grad_w_value = jnp.split(attn_grad.astype(f32), 3)
    grad_states, mod_one = call(
        finish_kernel,
        [wide_rows, shaped((2, width), f32)],
        (states, modulation, send_list, grad_normed, grad_middle, *returned),
        scratch=[pltpu.VMEM((rows, 4 * sends), low_type)],
        flops=2**31,
        moved=2**23,
    )
    mod_grad = jnp.concatenate([mod_one, mod_two])
    for axis, bit in all_links:
        mod_grad = mod_grad + swap(mod_grad, axis, bit)
    mod_grad = mod_grad.reshape(-1)
    grad_mod_w = condition[:, None] * mod_grad[None, :]
    grad_condition = jnp.sum(mod_w.astype(f32) * mod_grad[None, :], axis=1)
    return (
        output,
        grad_states,
        grad_condition,
        grad_mod_w,
        grad_w_query,
        grad_w_key,
        grad_w_value,
        grad_w_out,
        grad_w_gate,
        grad_w_up,
        grad_w_down,
    )


def solution(mesh):
    rows = P(everywhere, None)
    placed = (
        rows,
        P(),
        P(),
        P(),
        P(),
        P(),
        P(),
        P(None, "hid"),
        P(None, "hid"),
        P("hid", None),
        P(everywhere),
        P(everywhere, None, None),
        rows,
        rows,
    )
    return jax.shard_map(
        body,
        mesh=mesh,
        in_specs=placed,
        out_specs=(rows, rows, P(), P(), P(), P(), P(), P(), P(None, "hid"), P(None, "hid"), P("hid", None)),
        check_vma=False,
    )
```

time: 632 us -> 313 us (0.50); the launches traced: 624 us -> 312 us
  waiting for transfers between devices: 320 us -> 119 us
  Pallas kernels: 45.7 us -> 125 us
  matrix products: 72.7 us -> 0 us
  blocking collectives: 42 us -> 0 us
  other arithmetic: 51.7 us -> 10.9 us
  local copies, waits for them, and re-layouts: 46.7 us -> 10.6 us
  starting transfers between devices: 29.9 us -> 45.3 us
  between operations: 15.4 us -> 1.91 us
    psum x2 -> x0, waiting for transfers between devices: 166 us -> none  [the longest x1 96.2 us: body(): lax.psum((attn_parts[0], attn_parts[1], attn_parts[2], attn_parts[3], att...]
    ppermute x0 -> x37, waiting for transfers between devices: none -> 116 us  [swap(): lax.ppermute(block, axis, [(i, i ^ 1 << bit) for i in range(lax.axis_size...]
    reduce_scatter x2 -> x0, waiting for transfers between devices: 112 us -> none  [the longest x1 68.1 us: body(): lax.psum_scatter(times_transposed(grad_gate, w_gate) + times_transposed(g...]
    pallas_call x2 -> x9, Pallas kernels: 45.7 us -> 125 us  [the longest x6 73.9 us: call(): pl.pallas_call(kernel, in_specs=specs or [whole] * len(args), out_specs=w...]
    dot_general x23 -> x0, matrix products: 72.7 us -> none  [the longest x7 29.9 us: times_transposed(): lax.dot_general(left, right, (((1,), (1,)), ((), ())), preferred_element_...]
    psum x1 -> x0, blocking collectives: 42 us -> none  [body(): lax.psum((attn_parts[0], attn_parts[1], attn_parts[2], attn_parts[3], att...]
    all_gather x2 -> x0, waiting for transfers between devices: 41.5 us -> none  [the longest x1 22.9 us: body(): grad_rows = lax.all_gather(grad_branch, 'hid', axis=0, tiled=True)]
    ppermute x0 -> x37, starting transfers between devices: none -> 27.1 us  [swap(): lax.ppermute(block, axis, [(i, i ^ 1 << bit) for i in range(lax.axis_size...]
  transfers between devices with their start and end apart: 14 -> 45, of which waited for: 6 -> 19; matrix products, arithmetic and copies ran while one was open for 15% -> 5% of each run, Pallas kernels for 0% -> 22%
where the time goes in v2:
time: 313 us; the launch traced here: 312 us
  Pallas kernels  125 us (40%)
  waiting for transfers between devices  119 us (38%)
  starting transfers between devices  45.3 us (14%)
  other arithmetic  10.9 us (3%)
  local copies, waits for them, and re-layouts  10.6 us (3%)
    ppermute x37, waiting for transfers between devices, swap(): lax.ppermute(block, axis, [(i, i ^ 1 << bit) for i in range(lax.axis_size...  116 us
    pallas_call x6, Pallas kernels, call(): pl.pallas_call(kernel, in_specs=specs or [whole] * len(args), out_specs=w...  73.9 us
    pallas_call x2, Pallas kernels, attend_back(): pl.pallas_call(attend_back_kernel, grid=(heads,), in_specs=[by_row, by_ex...  28.7 us
    ppermute x37, starting transfers between devices, swap(): lax.ppermute(block, axis, [(i, i ^ 1 << bit) for i in range(lax.axis_size...  27.1 us
    pallas_call x1, Pallas kernels, attend(): pl.pallas_call(attend_kernel, grid=(HEADS,), in_specs=[pl.BlockSpec(packe...  22 us
    ppermute x8, starting transfers between devices, from_behind(): return lax.ppermute(block, axis, route)  18.2 us
  transfers between devices with their start and end apart: 45, of which 19 were waited for; matrix products, arithmetic and copies ran while one was open for 5% of the time, Pallas kernels for 22%

profile of v2, /device:TPU:0, one launch (start us, length us, event | category | flops | bytes accessed | tf_op | source)
XLA Modules:
  0.0 312.5 jit_solution(1598073394733280116)
XLA Ops:
  0.6 1.3 copy.25.condition_ref
  2.0 4.2 %shard_map.221 = (bf16[1024,512]{1,0:T(8,128)(2,1)}, f32[4,512]{1,0:T(4,128)}, bf16[128,512]{1,0:T(8,128)(2,1)}, bf16[128,512]{1,0:T(8,128)(2,1)}, bf16[128,512]{1,0:T(8,128)(2,1)}, /*index=5*/bf16[128,512]{1,0:T(8,128)(2,1)}) custom-call(f32[1024,512]{1,0:T(8,128)} %states_ref.5, f32[16,1]{1,0:T(8,128)} %copy.25.condition_ref, bf16[16,2048]{1,0:T(8,128)(2,1)} %mod_w_ref.1, ...), custom_call_target="tpu_custom_call" | custom-call | flops 1073741824 | bytes 4194304 | tf_op jit(solution)/shard_map/pallas_call | solution.py:50
  6.6 6.0 %collective-permute-start.1 = (bf16[128,512]{1,0:T(8,128)(2,1)}, bf16[128,512]{1,0:T(8,128)(2,1)S(1)}, u32[]{:S(2)}, u32[]{:S(2)}) collective-permute-start(bf16[128,512]{1,0:T(8,128)(2,1)} %get-tuple-element.67), channel_id=1, source_target_pairs={{1,0},{2,1},{3,2},{4,3},{5,4},{6,5},{7,6},{8,7},{9,8},{10,9},{11,1... | collective-permute-start | bytes 393224 | tf_op jit(solution)/shard_map/ppermute | solution.py:434
  12.6 5.6 %collective-permute-start.3 = (bf16[128,512]{1,0:T(8,128)(2,1)}, bf16[128,512]{1,0:T(8,128)(2,1)}, u32[]{:S(2)}, u32[]{:S(2)}) collective-permute-start(bf16[128,512]{1,0:T(8,128)(2,1)} %get-tuple-element.69), channel_id=1, source_target_pairs={{2,0},{3,1},{4,2},{5,3},{6,4},{7,5},{8,6},{9,7},{10,8},{11,9},{12,... | collective-permute-start | bytes 393224 | tf_op jit(solution)/shard_map/ppermute | solution.py:434
  18.4 8.6 %shard_map.222 = (bf16[1024,512]{1,0:T(8,128)(2,1)}, bf16[1024,512]{1,0:T(8,128)(2,1)}, bf16[1024,512]{1,0:T(8,128)(2,1)}, s32[2,128,1024]{2,1,0:T(8,128)}) custom-call(bf16[1024,512]{1,0:T(8,128)(2,1)} %get-tuple-element.61.normed_ref, s32[16,1024]{1,0:T(8,128)} %bitcast.8, bf16[512,512]{1,0:T(8,128)(2,1)} %w_query_ref.3, bf16[512,512]{1,0:T(8,128)(2,1)} %w_key_ref.5, ...), custom_call_target="tpu_custom_call" | custom-call | flops 4294967296 | bytes 4194304 | tf_op jit(solution)/shard_map/pallas_call | solution.py:50
  28.5 22.0 %shard_map.223 = (bf16[1024,512]{1,0:T(8,128)(2,1)}, bf16[4,1536,1024]{2,1,0:T(8,128)(2,1)}, f32[4,1,1024]{2,1,0:T(1,128)}, f32[1024,512]{1,0:T(8,128)}, bf16[15...) custom-call(s32[2,128,1024]{2,1,0:T(8,128)} %get-tuple-element.62.packed_ref, ...), custom_call_target="tpu_custom_call" | custom-call | flops 34359738368 | bytes 16777216 | tf_op jit(solution)/shard_map/pallas_call | solution.py:177
  50.4 13.7 %collective-permute-done.4.weight_a_ref = bf16[1536,512]{1,0:T(8,128)(2,1)S(1)} collective-permute-done((bf16[1536,512]{1,0:T(8,128)(2,1)S(1)}, bf16[1536,512]{1,0:T(8,128)(2,1)S(1)}, u32[]{:S(2)}, u32[]{:S(2)}) %collective-permute-start.4) | collective-permute-done | bytes 1572896 | tf_op jit(solution)/shard_map/ppermute | solution.py:438
  64.2 1.2 copy-done.13
  65.4 18.9 %shard_map.224 = (f32[1024,512]{1,0:T(8,128)}, bf16[1024,512]{1,0:T(8,128)(2,1)}, bf16[1024,512]{1,0:T(8,128)(2,1)}, f32[1024,512]{1,0:T(8,128)}, f32[1024,512]{...) custom-call(s32[1]{0:T(128)S(6)} %copy.29.count_ref, f32[4,512]{1,0:T(4,128)} %get-tuple-element.60.modulation_ref, ...), custom_call_target="tpu_custom_call" | custom-call | flops 17179869184 | bytes 16777216 | tf_op jit(solution)/shard_map/pallas_call | solution.py:50
  85.4 23.9 %shard_map.225 = (f32[1024,512]{1,0:T(8,128)}, f32[1024,512]{1,0:T(8,128)}, bf16[1024,512]{1,0:T(8,128)(2,1)}, bf16[512,512]{1,0:T(8,128)(2,1)}, f32[2,512]{1,0:...) custom-call(s32[1]{0:T(128)S(6)} %copy.29.count_ref, f32[4,512]{1,0:T(4,128)} %get-tuple-element.60.modulation_ref, ...), custom_call_target="tpu_custom_call" | custom-call | flops 17179869184 | bytes 16777216 | tf_op jit(solution)/shard_map/pallas_call | solution.py:50
  109.3 14.4 %shard_map.227 = (bf16[1024,256]{1,0:T(8,128)(2,1)}, bf16[1536,256]{1,0:T(8,128)(2,1)}, bf16[1536,256]{1,0:T(8,128)(2,1)}) custom-call(bf16[1024,512]{1,0:T(8,128)(2,1)} %get-tuple-element.63.query_ref, bf16[1536,512]{1,0:T(8,128)(2,1)} %get-tuple-element.83.key_ref, bf16[1536,512]{1,0:T(8,128)(2,1)} %get-tuple-element.84.value_ref, ...), custom_call_target="tpu_custom_call" | custom-call | flops 17179869184 | bytes 4194304 | tf_op jit(solution)/shard_map/pallas_call | solution.py:249
  123.7 14.4 %shard_map.226 = (bf16[1024,256]{1,0:T(8,128)(2,1)}, bf16[1536,256]{1,0:T(8,128)(2,1)}, bf16[1536,256]{1,0:T(8,128)(2,1)}) custom-call(bf16[1024,512]{1,0:T(8,128)(2,1)} %get-tuple-element.63.query_ref, bf16[1536,512]{1,0:T(8,128)(2,1)} %get-tuple-element.83.key_ref, bf16[1536,512]{1,0:T(8,128)(2,1)} %get-tuple-element.84.value_ref, ...), custom_call_target="tpu_custom_call" | custom-call | flops 17179869184 | bytes 4194304 | tf_op jit(solution)/shard_map/pallas_call | solution.py:249
  138.5 11.2 %shard_map.228 = (bf16[1536,512]{1,0:T(8,128)(2,1)}, f32[1024,512]{1,0:T(8,128)}, bf16[128,512]{1,0:T(8,128)(2,1)}, bf16[128,512]{1,0:T(8,128)(2,1)}, bf16[128,5...) custom-call(bf16[1024,512]{1,0:T(8,128)(2,1)} %get-tuple-element.61.normed_ref, bf16[512,512]{1,0:T(8,128)(2,1)} %w_query_ref.3, ...), custom_call_target="tpu_custom_call" | custom-call | flops 4294967296 | bytes 8388608 | tf_op jit(solution)/shard_map/pallas_call | solution.py:50
  150.0 4.7 %collective-permute-start.7 = (bf16[128,512]{1,0:T(8,128)(2,1)}, bf16[128,512]{1,0:T(8,128)(2,1)S(1)}, u32[]{:S(2)}, u32[]{:S(2)}) collective-permute-start(bf16[128,512]{1,0:T(8,128)(2,1)} %get-tuple-element.96), channel_id=1, source_target_pairs={{1,0},{2,1},{3,2},{4,3},{5,4},{6,5},{7,6},{8,7},{9,8},{10,9},{11,1... | collective-permute-start | bytes 393224 | tf_op jit(solution)/shard_map/ppermute | solution.py:434
  154.7 1.2 collective-permute-start.9
  155.9 1.2 constant_dynamic-slice_fusion.12
  157.0 2.0 collective-permute-done.10.refs_3_
  159.1 2.4 collective-permute-start.16
  163.0 7.2 %shard_map.229 = (f32[1024,512]{1,0:T(8,128)}, f32[2,512]{1,0:T(2,128)}) custom-call(f32[1024,512]{1,0:T(8,128)} %states_ref.5, f32[4,512]{1,0:T(4,128)} %get-tuple-element.60.modulation_ref, s32[4,128]{1,0:T(4,128)} %bitcast.10, f32[1024,512]{1,0:T(8,128)} %get-tuple-element.94.grad_normed_ref, f32[1024,512]{1,0:T(8,128)} %get-tuple-element.95.grad_middle_ref, ...), custom_call_target="tpu_custom_call" | custom-call | flops 2147483648 | bytes 8388608 | tf_op jit(solution)/shard_map/pallas_call | solution.py:50
  172.5 2.1 collective-permute-start.17
  174.6 3.1 add.177
  177.7 2.1 collective-permute-start.12
  179.8 40.4 %collective-permute-done.12 = f32[4,512]{1,0:T(4,128)S(1)} collective-permute-done((f32[4,512]{1,0:T(4,128)S(1)}, f32[4,512]{1,0:T(4,128)S(1)}, u32[]{:S(2)}, u32[]{:S(2)}) %collective-permute-start.12) | collective-permute-done | bytes 8224 | tf_op jit(solution)/shard_map/ppermute | solution.py:438
  220.2 3.6 %collective-permute-done.13 = f32[4,512]{1,0:T(4,128)S(1)} collective-permute-done((f32[4,512]{1,0:T(4,128)S(1)}, f32[4,512]{1,0:T(4,128)S(1)}, u32[]{:S(2)}, u32[]{:S(2)}) %collective-permute-start.13) | collective-permute-done | bytes 8224 | tf_op jit(solution)/shard_map/ppermute | solution.py:438
  223.9 3.6 %collective-permute-done.14 = f32[4,512]{1,0:T(4,128)S(1)} collective-permute-done((f32[4,512]{1,0:T(4,128)S(1)}, f32[4,512]{1,0:T(4,128)S(1)}, u32[]{:S(2)}, u32[]{:S(2)}) %collective-permute-start.14) | collective-permute-done | bytes 8224 | tf_op jit(solution)/shard_map/ppermute | solution.py:438
  228.1 2.1 collective-permute-start.28
  230.4 2.4 collective-permute-done.28
  232.9 1.8 collective-permute-start.29
  234.7 1.4 collective-permute-done.18
  236.2 2.1 collective-permute-start.19
  238.3 1.6 add_add_fusion
  242.0 2.6 collective-permute-start.30
  244.6 2.1 collective-permute-done.20
  247.1 8.0 %collective-permute-done.39 = bf16[768,512]{1,0:T(8,128)(2,1)S(1)} collective-permute-done((bf16[768,512]{1,0:T(8,128)(2,1)S(1)}, bf16[768,512]{1,0:T(8,128)(2,1)S(1)}, u32[]{:S(2)}, u32[]{:S(2)}) %collective-permute-start.39) | collective-permute-done | bytes 786464 | tf_op jit(solution)/shard_map/ppermute | solution.py:438
  256.3 1.4 collective-permute-start.22
  257.7 6.3 %collective-permute-done.31 = bf16[16,512]{1,0:T(8,128)(2,1)S(1)} collective-permute-done((bf16[16,512]{1,0:T(8,128)(2,1)S(1)}, bf16[16,512]{1,0:T(8,128)(2,1)S(1)}, u32[]{:S(2)}, u32[]{:S(2)}) %collective-permute-start.31) | collective-permute-done | bytes 16416 | tf_op jit(solution)/shard_map/ppermute | solution.py:438
  264.7 1.9 collective-permute-done.22
  267.9 4.5 %collective-permute-done.23 = bf16[192,512]{1,0:T(8,128)(2,1)S(1)} collective-permute-done((bf16[192,512]{1,0:T(8,128)(2,1)S(1)}, bf16[192,512]{1,0:T(8,128)(2,1)S(1)}, u32[]{:S(2)}, u32[]{:S(2)}) %collective-permute-start.23) | collective-permute-done | bytes 196640 | tf_op jit(solution)/shard_map/ppermute | solution.py:438
  272.5 1.1 collective-permute-start.24
  274.5 3.4 %collective-permute-done.41 = bf16[192,512]{1,0:T(8,128)(2,1)S(1)} collective-permute-done((bf16[192,512]{1,0:T(8,128)(2,1)S(1)}, bf16[192,512]{1,0:T(8,128)(2,1)S(1)}, u32[]{:S(2)}, u32[]{:S(2)}) %collective-permute-start.41) | collective-permute-done | bytes 196640 | tf_op jit(solution)/shard_map/ppermute | solution.py:438
  278.1 1.4 collective-permute-start.34
  280.7 5.5 %collective-permute-done.42 = bf16[192,512]{1,0:T(8,128)(2,1)S(1)} collective-permute-done((bf16[192,512]{1,0:T(8,128)(2,1)S(1)}, bf16[192,512]{1,0:T(8,128)(2,1)S(1)}, u32[]{:S(2)}, u32[]{:S(2)}) %collective-permute-start.42) | collective-permute-done | bytes 196640 | tf_op jit(solution)/shard_map/ppermute | solution.py:438
  286.7 1.4 broadcast_multiply_fusion
  288.0 6.4 %collective-permute-done.43 = bf16[384,512]{1,0:T(8,128)(2,1)S(1)} collective-permute-done((bf16[384,512]{1,0:T(8,128)(2,1)S(1)}, bf16[384,512]{1,0:T(8,128)(2,1)S(1)}, u32[]{:S(2)}, u32[]{:S(2)}) %collective-permute-start.43) | collective-permute-done | bytes 393248 | tf_op jit(solution)/shard_map/ppermute | solution.py:438
  295.8 1.2 fusion.2
  297.5 1.7 fusion.5
  299.2 11.1 %collective-permute-done.44 = bf16[768,512]{1,0:T(8,128)(2,1)S(1)} collective-permute-done((bf16[768,512]{1,0:T(8,128)(2,1)S(1)}, bf16[768,512]{1,0:T(8,128)(2,1)S(1)}, u32[]{:S(2)}, u32[]{:S(2)}) %collective-permute-start.44) | collective-permute-done | bytes 786464 | tf_op jit(solution)/shard_map/ppermute | solution.py:438
  310.8 1.7 fusion.4
  (148 shorter events, 18.7 us)
Async XLA Ops:
  2.0 16.2 %copy-start.3 = (bf16[512,512]{1,0:T(8,128)(2,1)S(1)}, bf16[512,512]{1,0:T(8,128)(2,1)}, u32[]{:S(2)}) copy-start(bf16[512,512]{1,0:T(8,128)(2,1)} %param.21) | copy-start | bytes 1572868
  2.0 16.3 %copy-start.4 = (bf16[512,512]{1,0:T(8,128)(2,1)S(1)}, bf16[512,512]{1,0:T(8,128)(2,1)}, u32[]{:S(2)}) copy-start(bf16[512,512]{1,0:T(8,128)(2,1)} %param.22) | copy-start | bytes 1572868
  6.2 21.6 %collective-permute-start = (bf16[128,512]{1,0:T(8,128)(2,1)}, bf16[128,512]{1,0:T(8,128)(2,1)S(1)}, u32[]{:S(2)}, u32[]{:S(2)}) collective-permute-start(bf16[128,512]{1,0:T(8,128)(2,1)} %get-tuple-element.66), channel_id=1, source_target_pairs={{31,0},{0,1},{1,2},{2,3},{3,4},{4,5},{5,6},{6,7},{7,8},{8,9},{9,10... | collective-permute-start | bytes 393224 | tf_op jit(solution)/shard_map/ppermute | solution.py:434
  6.6 21.1 %collective-permute-start.1 = (bf16[128,512]{1,0:T(8,128)(2,1)}, bf16[128,512]{1,0:T(8,128)(2,1)S(1)}, u32[]{:S(2)}, u32[]{:S(2)}) collective-permute-start(bf16[128,512]{1,0:T(8,128)(2,1)} %get-tuple-element.67), channel_id=1, source_target_pairs={{1,0},{2,1},{3,2},{4,3},{5,4},{6,5},{7,6},{8,7},{9,8},{10,9},{11,1... | collective-permute-start | bytes 393224 | tf_op jit(solution)/shard_map/ppermute | solution.py:434
  12.6 15.2 %collective-permute-start.2 = (bf16[128,512]{1,0:T(8,128)(2,1)}, bf16[128,512]{1,0:T(8,128)(2,1)S(1)}, u32[]{:S(2)}, u32[]{:S(2)}) collective-permute-start(bf16[128,512]{1,0:T(8,128)(2,1)} %get-tuple-element.68), channel_id=1, source_target_pairs={{30,0},{31,1},{0,2},{1,3},{2,4},{3,5},{4,6},{5,7},{6,8},{7,9},{8,1... | collective-permute-start | bytes 393224 | tf_op jit(solution)/shard_map/ppermute | solution.py:434
  12.6 15.2 %collective-permute-start.3 = (bf16[128,512]{1,0:T(8,128)(2,1)}, bf16[128,512]{1,0:T(8,128)(2,1)}, u32[]{:S(2)}, u32[]{:S(2)}) collective-permute-start(bf16[128,512]{1,0:T(8,128)(2,1)} %get-tuple-element.69), channel_id=1, source_target_pairs={{2,0},{3,1},{4,2},{5,3},{6,4},{7,5},{8,6},{9,7},{10,8},{11,9},{12,... | collective-permute-start | bytes 393224 | tf_op jit(solution)/shard_map/ppermute | solution.py:434
  18.4 45.8 %collective-permute-start.6 = (bf16[1536,512]{1,0:T(8,128)(2,1)S(1)}, bf16[1536,512]{1,0:T(8,128)(2,1)S(1)}, u32[]{:S(2)}, u32[]{:S(2)}) collective-permute-start(bf16[1536,512]{1,0:T(8,128)(2,1)S(1)} %constant_dynamic-update-slice_fusion.weight_a_ref), channel_id=1, source_target_pairs={{0,1},{1,0},{2,3},{3,2},{4,5},{5,4},{6,7},{7,6},{8,9},{9,8},{10,11... | collective-permute-start | bytes 4718600 | tf_op jit(solution)/shard_map/ppermute | solution.py:438
  27.8 36.4 %collective-permute-start.4 = (bf16[1536,512]{1,0:T(8,128)(2,1)S(1)}, bf16[1536,512]{1,0:T(8,128)(2,1)S(1)}, u32[]{:S(2)}, u32[]{:S(2)}) collective-permute-start(bf16[1536,512]{1,0:T(8,128)(2,1)S(1)} %constant_dynamic-update-slice_fusion.weight_a_ref), channel_id=1, source_target_pairs={{0,2},{1,3},{2,0},{3,1},{4,6},{5,7},{6,4},{7,5},{8,10},{9,11},{10,... | collective-permute-start | bytes 4718600 | tf_op jit(solution)/shard_map/ppermute | solution.py:438
  64.2 20.1 %copy-start.14 = (bf16[1536,512]{1,0:T(8,128)(2,1)}, bf16[1536,512]{1,0:T(8,128)(2,1)S(1)}, u32[]{:S(2)}) copy-start(bf16[1536,512]{1,0:T(8,128)(2,1)S(1)} %collective-permute-done.4.weight_a_ref) | copy-start | bytes 4718596
  64.2 20.1 %collective-permute-start.5 = (bf16[1536,512]{1,0:T(8,128)(2,1)S(1)}, bf16[1536,512]{1,0:T(8,128)(2,1)S(1)}, u32[]{:S(2)}, u32[]{:S(2)}) collective-permute-start(bf16[1536,512]{1,0:T(8,128)(2,1)S(1)} %collective-permute-done.4.weight_a_ref), channel_id=1, source_target_pairs={{0,1},{1,0},{2,3},{3,2},{4,5},{5,4},{6,7},{7,6},{8,9},{9,8},{10,11... | collective-permute-start | bytes 4718600 | tf_op jit(solution)/shard_map/ppermute | solution.py:438
  138.0 36.6 %collective-permute-start.37 = (bf16[1536,512]{1,0:T(8,128)(2,1)}, bf16[1536,512]{1,0:T(8,128)(2,1)}, u32[]{:S(2)}, u32[]{:S(2)}) collective-permute-start(bf16[1536,512]{1,0:T(8,128)(2,1)} %get-tuple-element.108), channel_id=1, source_target_pairs={{0,1},{1,0},{2,3},{3,2},{4,5},{5,4},{6,7},{7,6},{8,9},{9,8},{10,11... | collective-permute-start | bytes 4718600 | tf_op jit(solution)/shard_map/ppermute | solution.py:438
  149.7 9.4 %collective-permute-start.10 = (bf16[128,512]{1,0:T(8,128)(2,1)}, bf16[128,512]{1,0:T(8,128)(2,1)S(1)}, u32[]{:S(2)}, u32[]{:S(2)}) collective-permute-start(bf16[128,512]{1,0:T(8,128)(2,1)} %get-tuple-element.99), channel_id=1, source_target_pairs={{30,0},{31,1},{0,2},{1,3},{2,4},{3,5},{4,6},{5,7},{6,8},{7,9},{8,1... | collective-permute-start | bytes 393224 | tf_op jit(solution)/shard_map/ppermute | solution.py:434
  150.0 11.4 %collective-permute-start.7 = (bf16[128,512]{1,0:T(8,128)(2,1)}, bf16[128,512]{1,0:T(8,128)(2,1)S(1)}, u32[]{:S(2)}, u32[]{:S(2)}) collective-permute-start(bf16[128,512]{1,0:T(8,128)(2,1)} %get-tuple-element.96), channel_id=1, source_target_pairs={{1,0},{2,1},{3,2},{4,3},{5,4},{6,5},{7,6},{8,7},{9,8},{10,9},{11,1... | collective-permute-start | bytes 393224 | tf_op jit(solution)/shard_map/ppermute | solution.py:434
  154.7 8.3 %collective-permute-start.8 = (bf16[128,512]{1,0:T(8,128)(2,1)}, bf16[128,512]{1,0:T(8,128)(2,1)}, u32[]{:S(2)}, u32[]{:S(2)}) collective-permute-start(bf16[128,512]{1,0:T(8,128)(2,1)} %get-tuple-element.97), channel_id=1, source_target_pairs={{31,0},{0,1},{1,2},{2,3},{3,4},{4,5},{5,6},{6,7},{7,8},{8,9},{9,10... | collective-permute-start | bytes 393224 | tf_op jit(solution)/shard_map/ppermute | solution.py:434
  154.7 8.3 %collective-permute-start.9 = (bf16[128,512]{1,0:T(8,128)(2,1)}, bf16[128,512]{1,0:T(8,128)(2,1)}, u32[]{:S(2)}, u32[]{:S(2)}) collective-permute-start(bf16[128,512]{1,0:T(8,128)(2,1)} %get-tuple-element.98), channel_id=1, source_target_pairs={{2,0},{3,1},{4,2},{5,3},{6,4},{7,5},{8,6},{9,7},{10,8},{11,9},{12,... | collective-permute-start | bytes 393224 | tf_op jit(solution)/shard_map/ppermute | solution.py:434
  159.1 13.2 %collective-permute-start.16 = (bf16[768,512]{1,0:T(8,128)(2,1)S(1)}, bf16[768,512]{1,0:T(8,128)(2,1)S(1)}, u32[]{:S(2)}, u32[]{:S(2)}) collective-permute-start(bf16[768,512]{1,0:T(8,128)(2,1)S(1)} %constant_dynamic-slice_fusion.12), channel_id=1, source_target_pairs={{0,1},{1,0},{2,3},{3,2},{4,5},{5,4},{6,7},{7,6},{8,9},{9,8},{10,11... | collective-permute-start | bytes 2359304 | tf_op jit(solution)/shard_map/ppermute | solution.py:438
  162.1 76.2 %collective-permute-start.36 = (bf16[1536,512]{1,0:T(8,128)(2,1)}, bf16[1536,512]{1,0:T(8,128)(2,1)S(1)}, u32[]{:S(2)}, u32[]{:S(2)}) collective-permute-start(bf16[1536,512]{1,0:T(8,128)(2,1)} %get-tuple-element.106), channel_id=1, source_target_pairs={{0,1},{1,0},{2,3},{3,2},{4,5},{5,4},{6,7},{7,6},{8,9},{9,8},{10,11... | collective-permute-start | bytes 4718600 | tf_op jit(solution)/shard_map/ppermute | solution.py:438
  163.0 8.5 %collective-permute-start.26 = (bf16[256,512]{1,0:T(8,128)(2,1)S(1)}, bf16[256,512]{1,0:T(8,128)(2,1)S(1)}, u32[]{:S(2)}, u32[]{:S(2)}) collective-permute-start(bf16[256,512]{1,0:T(8,128)(2,1)S(1)} %constant_dynamic-slice_fusion.7), channel_id=1, source_target_pairs={{0,1},{1,0},{2,3},{3,2},{4,5},{5,4},{6,7},{7,6},{8,9},{9,8},{10,11... | collective-permute-start | bytes 786440 | tf_op jit(solution)/shard_map/ppermute | solution.py:438
  171.0 6.7 %collective-permute-start.11 = (f32[4,512]{1,0:T(4,128)S(1)}, f32[4,512]{1,0:T(4,128)S(1)}, u32[]{:S(2)}, u32[]{:S(2)}) collective-permute-start(f32[4,512]{1,0:T(4,128)S(1)} %pad_maximum_fusion), channel_id=1, source_target_pairs={{0,1},{1,0},{2,3},{3,2},{4,5},{5,4},{6,7},{7,6},{8,9},{9,8},{10,11... | collective-permute-start | bytes 24584 | tf_op jit(solution)/shard_map/ppermute | solution.py:438
  172.2 55.8 %collective-permute-start.27 = (bf16[128,512]{1,0:T(8,128)(2,1)}, bf16[128,512]{1,0:T(8,128)(2,1)S(1)}, u32[]{:S(2)}, u32[]{:S(2)}) collective-permute-start(bf16[128,512]{1,0:T(8,128)(2,1)} %constant_dynamic-slice_fusion.6), channel_id=1, source_target_pairs={{0,2},{1,3},{2,0},{3,1},{4,6},{5,7},{6,4},{7,5},{8,10},{9,11},{10,... | collective-permute-start | bytes 393224 | tf_op jit(solution)/shard_map/ppermute | solution.py:438
  172.5 57.7 %collective-permute-start.17 = (bf16[384,512]{1,0:T(8,128)(2,1)S(1)}, bf16[384,512]{1,0:T(8,128)(2,1)S(1)}, u32[]{:S(2)}, u32[]{:S(2)}) collective-permute-start(bf16[384,512]{1,0:T(8,128)(2,1)S(1)} %constant_dynamic-slice_fusion.11), channel_id=1, source_target_pairs={{0,2},{1,3},{2,0},{3,1},{4,6},{5,7},{6,4},{7,5},{8,10},{9,11},{10,... | collective-permute-start | bytes 1179656 | tf_op jit(solution)/shard_map/ppermute | solution.py:438
  177.7 60.6 %collective-permute-start.38 = (bf16[1536,512]{1,0:T(8,128)(2,1)}, bf16[1536,512]{1,0:T(8,128)(2,1)}, u32[]{:S(2)}, u32[]{:S(2)}) collective-permute-start(bf16[1536,512]{1,0:T(8,128)(2,1)} %add.177), channel_id=1, source_target_pairs={{0,2},{1,3},{2,0},{3,1},{4,6},{5,7},{6,4},{7,5},{8,10},{9,11},{10,... | collective-permute-start | bytes 4718600 | tf_op jit(solution)/shard_map/ppermute | solution.py:438
  177.7 42.5 %collective-permute-start.12 = (f32[4,512]{1,0:T(4,128)S(1)}, f32[4,512]{1,0:T(4,128)S(1)}, u32[]{:S(2)}, u32[]{:S(2)}) collective-permute-start(f32[4,512]{1,0:T(4,128)S(1)} %fusion.3), channel_id=1, source_target_pairs={{0,2},{1,3},{2,0},{3,1},{4,6},{5,7},{6,4},{7,5},{8,10},{9,11},{10,... | collective-permute-start | bytes 24584 | tf_op jit(solution)/shard_map/ppermute | solution.py:438
  220.2 3.7 %collective-permute-start.13 = (f32[4,512]{1,0:T(4,128)S(1)}, f32[4,512]{1,0:T(4,128)S(1)}, u32[]{:S(2)}, u32[]{:S(2)}) collective-permute-start(f32[4,512]{1,0:T(4,128)S(1)} %add.142), channel_id=1, source_target_pairs={{0,4},{4,0},{8,12},{12,8},{16,20},{20,16},{24,28},{28,24},{1,5},{5... | collective-permute-start | bytes 24584 | tf_op jit(solution)/shard_map/ppermute | solution.py:438
  223.8 3.7 %collective-permute-start.14 = (f32[4,512]{1,0:T(4,128)S(1)}, f32[4,512]{1,0:T(4,128)S(1)}, u32[]{:S(2)}, u32[]{:S(2)}) collective-permute-start(f32[4,512]{1,0:T(4,128)S(1)} %add.143), channel_id=1, source_target_pairs={{0,8},{4,12},{8,0},{12,4},{16,24},{20,28},{24,16},{28,20},{1,9},{5... | collective-permute-start | bytes 24584 | tf_op jit(solution)/shard_map/ppermute | solution.py:438
  227.5 59.0 %collective-permute-start.15 = (f32[4,512]{1,0:T(4,128)S(1)}, f32[4,512]{1,0:T(4,128)S(1)}, u32[]{:S(2)}, u32[]{:S(2)}) collective-permute-start(f32[4,512]{1,0:T(4,128)S(1)} %add.144), channel_id=1, source_target_pairs={{0,16},{4,20},{8,24},{12,28},{16,0},{20,4},{24,8},{28,12},{1,17},{... | collective-permute-start | bytes 24584 | tf_op jit(solution)/shard_map/ppermute | solution.py:438
  228.1 4.7 %collective-permute-start.28 = (bf16[64,512]{1,0:T(8,128)(2,1)S(1)}, bf16[64,512]{1,0:T(8,128)(2,1)S(1)}, u32[]{:S(2)}, u32[]{:S(2)}) collective-permute-start(bf16[64,512]{1,0:T(8,128)(2,1)S(1)} %constant_dynamic-slice_fusion.5), channel_id=1, source_target_pairs={{0,4},{4,0},{8,12},{12,8},{16,20},{20,16},{24,28},{28,24},{1,5},{5... | collective-permute-start | bytes 196616 | tf_op jit(solution)/shard_map/ppermute | solution.py:438
  230.4 5.7 %collective-permute-start.18 = (bf16[192,512]{1,0:T(8,128)(2,1)S(1)}, bf16[192,512]{1,0:T(8,128)(2,1)S(1)}, u32[]{:S(2)}, u32[]{:S(2)}) collective-permute-start(bf16[192,512]{1,0:T(8,128)(2,1)S(1)} %constant_dynamic-slice_fusion.10), channel_id=1, source_target_pairs={{0,4},{4,0},{8,12},{12,8},{16,20},{20,16},{24,28},{28,24},{1,5},{5... | collective-permute-start | bytes 589832 | tf_op jit(solution)/shard_map/ppermute | solution.py:438
  232.9 7.7 %collective-permute-start.29 = (bf16[32,512]{1,0:T(8,128)(2,1)S(1)}, bf16[32,512]{1,0:T(8,128)(2,1)S(1)}, u32[]{:S(2)}, u32[]{:S(2)}) collective-permute-start(bf16[32,512]{1,0:T(8,128)(2,1)S(1)} %constant_dynamic-slice_fusion.4), channel_id=1, source_target_pairs={{0,8},{4,12},{8,0},{12,4},{16,24},{20,28},{24,16},{28,20},{1,9},{5... | collective-permute-start | bytes 98312 | tf_op jit(solution)/shard_map/ppermute | solution.py:438
  236.2 5.4 %collective-permute-start.19 = (bf16[96,512]{1,0:T(8,128)(2,1)S(1)}, bf16[96,512]{1,0:T(8,128)(2,1)S(1)}, u32[]{:S(2)}, u32[]{:S(2)}) collective-permute-start(bf16[96,512]{1,0:T(8,128)(2,1)S(1)} %constant_dynamic-slice_fusion.9), channel_id=1, source_target_pairs={{0,8},{4,12},{8,0},{12,4},{16,24},{20,28},{24,16},{28,20},{1,9},{5... | collective-permute-start | bytes 294920 | tf_op jit(solution)/shard_map/ppermute | solution.py:438
  240.0 15.1 %collective-permute-start.39 = (bf16[768,512]{1,0:T(8,128)(2,1)S(1)}, bf16[768,512]{1,0:T(8,128)(2,1)S(1)}, u32[]{:S(2)}, u32[]{:S(2)}) collective-permute-start(bf16[768,512]{1,0:T(8,128)(2,1)S(1)} %constant_dynamic-slice_fusion.2), channel_id=1, source_target_pairs={{0,4},{4,0},{8,12},{12,8},{16,20},{20,16},{24,28},{28,24},{1,5},{5... | collective-permute-start | bytes 2359304 | tf_op jit(solution)/shard_map/ppermute | solution.py:438
  241.6 5.1 %collective-permute-start.20 = (bf16[48,512]{1,0:T(8,128)(2,1)S(1)}, bf16[48,512]{1,0:T(8,128)(2,1)S(1)}, u32[]{:S(2)}, u32[]{:S(2)}) collective-permute-start(bf16[48,512]{1,0:T(8,128)(2,1)S(1)} %constant_dynamic-slice_fusion.8), channel_id=1, source_target_pairs={{0,16},{4,20},{8,24},{12,28},{16,0},{20,4},{24,8},{28,12},{1,17},{... | collective-permute-start | bytes 147464 | tf_op jit(solution)/shard_map/ppermute | solution.py:438
  242.0 14.0 %collective-permute-start.30 = (bf16[16,512]{1,0:T(8,128)(2,1)S(1)}, bf16[16,512]{1,0:T(8,128)(2,1)S(1)}, u32[]{:S(2)}, u32[]{:S(2)}) collective-permute-start(bf16[16,512]{1,0:T(8,128)(2,1)S(1)} %constant_dynamic-slice_fusion.3), channel_id=1, source_target_pairs={{0,16},{4,20},{8,24},{12,28},{16,0},{20,4},{24,8},{28,12},{1,17},{... | collective-permute-start | bytes 49160 | tf_op jit(solution)/shard_map/ppermute | solution.py:438
  246.7 9.6 %collective-permute-start.21 = (bf16[48,512]{1,0:T(8,128)(2,1)S(1)}, bf16[48,512]{1,0:T(8,128)(2,1)S(1)}, u32[]{:S(2)}, u32[]{:S(2)}) collective-permute-start(bf16[48,512]{1,0:T(8,128)(2,1)S(1)} %dynamic-slice_add_fusion.10), channel_id=1, source_target_pairs={{0,16},{4,20},{8,24},{12,28},{16,0},{20,4},{24,8},{28,12},{1,17},{... | collective-permute-start | bytes 147464 | tf_op jit(solution)/shard_map/ppermute | solution.py:438
  255.4 11.3 %collective-permute-start.40 = (bf16[384,512]{1,0:T(8,128)(2,1)S(1)}, bf16[384,512]{1,0:T(8,128)(2,1)S(1)}, u32[]{:S(2)}, u32[]{:S(2)}) collective-permute-start(bf16[384,512]{1,0:T(8,128)(2,1)S(1)} %constant_dynamic-slice_fusion.1), channel_id=1, source_target_pairs={{0,8},{4,12},{8,0},{12,4},{16,24},{20,28},{24,16},{28,20},{1,9},{5... | collective-permute-start | bytes 1179656 | tf_op jit(solution)/shard_map/ppermute | solution.py:438
  256.0 7.9 %collective-permute-start.31 = (bf16[16,512]{1,0:T(8,128)(2,1)S(1)}, bf16[16,512]{1,0:T(8,128)(2,1)S(1)}, u32[]{:S(2)}, u32[]{:S(2)}) collective-permute-start(bf16[16,512]{1,0:T(8,128)(2,1)S(1)} %dynamic-slice_add_fusion.12), channel_id=1, source_target_pairs={{0,16},{4,20},{8,24},{12,28},{16,0},{20,4},{24,8},{28,12},{1,17},{... | collective-permute-start | bytes 49160 | tf_op jit(solution)/shard_map/ppermute | solution.py:438
  256.3 10.3 %collective-permute-start.22 = (bf16[96,512]{1,0:T(8,128)(2,1)S(1)}, bf16[96,512]{1,0:T(8,128)(2,1)S(1)}, u32[]{:S(2)}, u32[]{:S(2)}) collective-permute-start(bf16[96,512]{1,0:T(8,128)(2,1)S(1)} %maximum_select_fusion.10), channel_id=1, source_target_pairs={{0,8},{4,12},{8,0},{12,4},{16,24},{20,28},{24,16},{28,20},{1,9},{5... | collective-permute-start | bytes 294920 | tf_op jit(solution)/shard_map/ppermute | solution.py:438
  264.0 9.7 %collective-permute-start.32 = (bf16[32,512]{1,0:T(8,128)(2,1)S(1)}, bf16[32,512]{1,0:T(8,128)(2,1)S(1)}, u32[]{:S(2)}, u32[]{:S(2)}) collective-permute-start(bf16[32,512]{1,0:T(8,128)(2,1)S(1)} %maximum_select_fusion.12), channel_id=1, source_target_pairs={{0,8},{4,12},{8,0},{12,4},{16,24},{20,28},{24,16},{28,20},{1,9},{5... | collective-permute-start | bytes 98312 | tf_op jit(solution)/shard_map/ppermute | solution.py:438
  266.6 5.7 %collective-permute-start.23 = (bf16[192,512]{1,0:T(8,128)(2,1)S(1)}, bf16[192,512]{1,0:T(8,128)(2,1)S(1)}, u32[]{:S(2)}, u32[]{:S(2)}) collective-permute-start(bf16[192,512]{1,0:T(8,128)(2,1)S(1)} %maximum_select_fusion.8), channel_id=1, source_target_pairs={{0,4},{4,0},{8,12},{12,8},{16,20},{20,16},{24,28},{28,24},{1,5},{5... | collective-permute-start | bytes 589832 | tf_op jit(solution)/shard_map/ppermute | solution.py:438
  266.9 11.0 %collective-permute-start.41 = (bf16[192,512]{1,0:T(8,128)(2,1)S(1)}, bf16[192,512]{1,0:T(8,128)(2,1)S(1)}, u32[]{:S(2)}, u32[]{:S(2)}) collective-permute-start(bf16[192,512]{1,0:T(8,128)(2,1)S(1)} %constant_dynamic-slice_fusion), channel_id=1, source_target_pairs={{0,16},{4,20},{8,24},{12,28},{16,0},{20,4},{24,8},{28,12},{1,17},{... | collective-permute-start | bytes 589832 | tf_op jit(solution)/shard_map/ppermute | solution.py:438
  272.5 7.8 %collective-permute-start.24 = (bf16[384,512]{1,0:T(8,128)(2,1)S(1)}, bf16[384,512]{1,0:T(8,128)(2,1)S(1)}, u32[]{:S(2)}, u32[]{:S(2)}) collective-permute-start(bf16[384,512]{1,0:T(8,128)(2,1)S(1)} %maximum_select_fusion.5), channel_id=1, source_target_pairs={{0,2},{1,3},{2,0},{3,1},{4,6},{5,7},{6,4},{7,5},{8,10},{9,11},{10,... | collective-permute-start | bytes 1179656 | tf_op jit(solution)/shard_map/ppermute | solution.py:438
  273.6 4.4 %collective-permute-start.33 = (bf16[64,512]{1,0:T(8,128)(2,1)S(1)}, bf16[64,512]{1,0:T(8,128)(2,1)S(1)}, u32[]{:S(2)}, u32[]{:S(2)}) collective-permute-start(bf16[64,512]{1,0:T(8,128)(2,1)S(1)} %maximum_select_fusion.11), channel_id=1, source_target_pairs={{0,4},{4,0},{8,12},{12,8},{16,20},{20,16},{24,28},{28,24},{1,5},{5... | collective-permute-start | bytes 196616 | tf_op jit(solution)/shard_map/ppermute | solution.py:438
  278.0 8.3 %collective-permute-start.42 = (bf16[192,512]{1,0:T(8,128)(2,1)S(1)}, bf16[192,512]{1,0:T(8,128)(2,1)S(1)}, u32[]{:S(2)}, u32[]{:S(2)}) collective-permute-start(bf16[192,512]{1,0:T(8,128)(2,1)S(1)} %dynamic-slice_add_fusion.5), channel_id=1, source_target_pairs={{0,16},{4,20},{8,24},{12,28},{16,0},{20,4},{24,8},{28,12},{1,17},{... | collective-permute-start | bytes 589832 | tf_op jit(solution)/shard_map/ppermute | solution.py:438
  278.1 8.4 %collective-permute-start.34 = (bf16[128,512]{1,0:T(8,128)(2,1)S(1)}, bf16[128,512]{1,0:T(8,128)(2,1)S(1)}, u32[]{:S(2)}, u32[]{:S(2)}) collective-permute-start(bf16[128,512]{1,0:T(8,128)(2,1)S(1)} %maximum_select_fusion.9), channel_id=1, source_target_pairs={{0,2},{1,3},{2,0},{3,1},{4,6},{5,7},{6,4},{7,5},{8,10},{9,11},{10,... | collective-permute-start | bytes 393224 | tf_op jit(solution)/shard_map/ppermute | solution.py:438
  280.6 16.4 %collective-permute-start.25 = (bf16[768,512]{1,0:T(8,128)(2,1)S(1)}, bf16[768,512]{1,0:T(8,128)(2,1)S(1)}, u32[]{:S(2)}, u32[]{:S(2)}) collective-permute-start(bf16[768,512]{1,0:T(8,128)(2,1)S(1)} %maximum_select_fusion.2), channel_id=1, source_target_pairs={{0,1},{1,0},{2,3},{3,2},{4,5},{5,4},{6,7},{7,6},{8,9},{9,8},{10,11... | collective-permute-start | bytes 2359304 | tf_op jit(solution)/shard_map/ppermute | solution.py:438
  286.4 8.1 %collective-permute-start.43 = (bf16[384,512]{1,0:T(8,128)(2,1)S(1)}, bf16[384,512]{1,0:T(8,128)(2,1)S(1)}, u32[]{:S(2)}, u32[]{:S(2)}) collective-permute-start(bf16[384,512]{1,0:T(8,128)(2,1)S(1)} %maximum_select_fusion.6), channel_id=1, source_target_pairs={{0,8},{4,12},{8,0},{12,4},{16,24},{20,28},{24,16},{28,20},{1,9},{5... | collective-permute-start | bytes 1179656 | tf_op jit(solution)/shard_map/ppermute | solution.py:438
  286.6 9.3 %collective-permute-start.35 = (bf16[256,512]{1,0:T(8,128)(2,1)S(1)}, bf16[256,512]{1,0:T(8,128)(2,1)S(1)}, u32[]{:S(2)}, u32[]{:S(2)}) collective-permute-start(bf16[256,512]{1,0:T(8,128)(2,1)S(1)} %maximum_select_fusion.7), channel_id=1, source_target_pairs={{0,1},{1,0},{2,3},{3,2},{4,5},{5,4},{6,7},{7,6},{8,9},{9,8},{10,11... | collective-permute-start | bytes 786440 | tf_op jit(solution)/shard_map/ppermute | solution.py:438
  294.7 15.6 %collective-permute-start.44 = (bf16[768,512]{1,0:T(8,128)(2,1)S(1)}, bf16[768,512]{1,0:T(8,128)(2,1)S(1)}, u32[]{:S(2)}, u32[]{:S(2)}) collective-permute-start(bf16[768,512]{1,0:T(8,128)(2,1)S(1)} %maximum_select_fusion.3), channel_id=1, source_target_pairs={{0,4},{4,0},{8,12},{12,8},{16,20},{20,16},{24,28},{28,24},{1,5},{5... | collective-permute-start | bytes 2359304 | tf_op jit(solution)/shard_map/ppermute | solution.py:438
  (18 other events, 100.8 us)

commit v3 on v2

v3 whole, which is shorter than its diff:
```python
import functools

import jax
import jax.numpy as jnp
from jax import lax
from jax.experimental import pallas as pl
from jax.experimental.pallas import tpu as pltpu
from jax.sharding import PartitionSpec as P

HEADS = 4
HEAD_DIM = 128
NEIGH = 16
BLOCK = 512
ROW_BLOCK = 256

epsilon = 1e-06
halo_steps = (1, -1, 2, -2)
highest = lax.Precision.HIGHEST
score_scale = HEAD_DIM ** (-0.5)
low_type = jnp.bfloat16
everywhere = ("nodes", "hid")
whole = pl.BlockSpec(memory_space=pltpu.VMEM)
scalars = pl.BlockSpec(memory_space=pltpu.SMEM)
anywhere = pl.BlockSpec(memory_space=pl.ANY)


def dot(left, right, left_dim, right_dim):
    return lax.dot_general(
        left, right, (((left_dim,), (right_dim,)), ((), ())), preferred_element_type=jnp.float32
    )


def shaped(shape, dtype=low_type):
    return jax.ShapeDtypeStruct(shape, dtype)


def norm_parts(states):
    centred = states - jnp.mean(states, axis=-1, keepdims=True)
    inverse = lax.rsqrt(jnp.mean(centred * centred, axis=-1, keepdims=True) + epsilon)
    return (centred * inverse, inverse)


def norm_back(grad_plain, plain, inverse):
    first_mean = jnp.mean(grad_plain, axis=-1, keepdims=True)
    second_mean = jnp.mean(grad_plain * plain, axis=-1, keepdims=True)
    return inverse * (grad_plain - first_mean - plain * second_mean)


def call(kernel, out_shape, args, specs=None, out_specs=None, scratch=(), flops=0, moved=0):
    single = not isinstance(out_shape, list)
    return pl.pallas_call(
        kernel,
        in_specs=specs or [whole] * len(args),
        out_specs=out_specs or (whole if single else [whole] * len(out_shape)),
        out_shape=out_shape,
        scratch_shapes=list(scratch),
        compiler_params=pltpu.CompilerParams(vmem_limit_bytes=56 * 2**20),
        cost_estimate=pl.CostEstimate(flops=flops, bytes_accessed=moved, transcendentals=0),
    )(*args)


def chosen_rows(send_ref, position, rows, first=0):
    sends = send_ref.shape[1]
    place = lax.broadcasted_iota(jnp.int32, (rows, sends), 0) + first
    return jnp.where(place == send_ref[position : position + 1, :], 1.0, 0.0).astype(low_type)


def prepare_kernel(states_ref, condition_ref, mod_w_ref, send_ref, normed_ref, plain_ref, modulation_ref, *parcel_refs):
    width = states_ref.shape[1]
    mixed = sum(
        condition_ref[i] * mod_w_ref[i : i + 1, :].astype(jnp.float32) for i in range(condition_ref.shape[0])
    )
    for piece in range(4):
        modulation_ref[piece : piece + 1, :] = mixed[:, piece * width : (piece + 1) * width]

    @pl.loop(0, states_ref.shape[0] // ROW_BLOCK)
    def _(step):
        rows = pl.ds(pl.multiple_of(step * ROW_BLOCK, ROW_BLOCK), ROW_BLOCK)
        plain, _ = norm_parts(states_ref[rows, :])
        plain_ref[rows, :] = plain.astype(low_type)
        normed_ref[rows, :] = (plain * (1.0 + modulation_ref[0:1, :]) + modulation_ref[1:2, :]).astype(low_type)

    for position, parcel_ref in enumerate(parcel_refs):
        chosen = chosen_rows(send_ref, position, states_ref.shape[0])
        parcel_ref[...] = dot(chosen, plain_ref[...], 0, 0).astype(low_type)


def count_near(near_ref, cols, groups):
    half = groups // 2
    near = near_ref[:, cols]
    group = near >> 7
    upper = group >= half
    unit = jnp.left_shift(1, 5 * jnp.where(upper, group - half, group))
    low = near & 127
    low_unit = jnp.where(upper, 0, unit)
    high_unit = jnp.where(upper, unit, 0)
    place = lax.broadcasted_iota(jnp.int32, (128, 128), 0)
    low_count = jnp.zeros((128, 128), jnp.int32)
    high_count = low_count
    for n in range(NEIGH):
        same = low[n : n + 1] == place
        low_count = low_count + jnp.where(same, low_unit[n : n + 1], 0)
        high_count = high_count + jnp.where(same, high_unit[n : n + 1], 0)
    return low_count, high_count


def count_bias(packed, position):
    count = (packed >> (5 * position)) & 31
    return jnp.where(count > 0, jnp.log(count.astype(jnp.float32)), -1e30)


def score_pass(key_ref, query, bias, scores, cols, top):
    width = scores.shape[1]
    for g in range(scores.shape[0] // 128):
        part = slice(g * 128, (g + 1) * 128)
        score = dot(key_ref[part, :], query, 1, 1) * score_scale + bias[part, cols]
        scores[part, :] = score
        top = jnp.maximum(top, jnp.max(score.reshape(16, 8, width), axis=0))
    return jnp.max(top, axis=0, keepdims=True)


def raise_pass(scores, top, raised_ref, cols):
    width = scores.shape[1]
    total = jnp.zeros((8, width), jnp.float32)
    for g in range(scores.shape[0] // 128):
        part = slice(g * 128, (g + 1) * 128)
        raised = jnp.exp(scores[part, :] - top)
        total = total + jnp.sum(raised.reshape(16, 8, width), axis=0)
        raised_ref[0, part, cols] = raised.astype(low_type)
    return jnp.sum(total, axis=0, keepdims=True)


def attend_own_kernel(
    groups, normed_ref, near_ref, w_query_ref, w_key_ref, w_value_ref,
    query_ref, key_ref, value_ref, raised_ref, top_ref, total_ref, mixed_ref, packed_ref,
    bias, scores, value_t,
):
    rows = normed_ref.shape[0]
    half = groups // 2

    @pl.when(pl.program_id(0) == 0)
    def _():
        @pl.loop(0, rows // 128)
        def _(step):
            cols = pl.ds(pl.multiple_of(step * 128, 128), 128)
            packed = count_near(near_ref, cols, groups)
            packed_ref[:, cols] = packed[1]
            for g in range(rows // 128):
                bias[g * 128 : (g + 1) * 128, cols] = count_bias(packed[g // half], g % half)

    for weight_ref, out_ref in ((w_query_ref, query_ref), (w_key_ref, key_ref), (w_value_ref, value_ref)):
        out_ref[...] = dot(normed_ref[...], weight_ref[...], 1, 0).astype(low_type)
    value_t[...] = value_ref[...].T
    width = scores.shape[1]

    @pl.loop(0, rows // width)
    def _(step):
        cols = pl.ds(pl.multiple_of(step * width, width), width)
        least = jnp.full((8, width), -jnp.inf, jnp.float32)
        top = score_pass(key_ref, query_ref[cols, :], bias, scores, cols, least)
        top_ref[0, :, cols] = top
        total_ref[0, :, cols] = raise_pass(scores, top, raised_ref, cols)
        mixed_ref[0, :, cols] = dot(value_t[...], raised_ref[0, :, cols], 1, 0)


def attend_own(normed, near, w_query, w_key, w_value, far_rows):
    rows, width = normed.shape
    groups = (rows + far_rows) // 128
    by_row = pl.BlockSpec((rows, HEAD_DIM), lambda h: (0, h))
    by_weight = pl.BlockSpec((width, HEAD_DIM), lambda h: (0, h))
    by_head = pl.BlockSpec((1, 1, rows), lambda h: (h, 0, 0))
    return pl.pallas_call(
        functools.partial(attend_own_kernel, groups),
        grid=(HEADS,),
        in_specs=[pl.BlockSpec((rows, width), lambda h: (0, 0)), pl.BlockSpec((NEIGH, rows), lambda h: (0, 0))]
        + [by_weight] * 3,
        out_specs=[
            by_row,
            by_row,
            by_row,
            pl.BlockSpec((1, rows, rows), lambda h: (h, 0, 0)),
            by_head,
            by_head,
            pl.BlockSpec((1, HEAD_DIM, rows), lambda h: (h, 0, 0)),
            pl.BlockSpec((128, rows), lambda h: (0, 0)),
        ],
        out_shape=[shaped((rows, width))] * 3
        + [
            shaped((HEADS, rows, rows)),
            shaped((HEADS, 1, rows), jnp.float32),
            shaped((HEADS, 1, rows), jnp.float32),
            shaped((HEADS, HEAD_DIM, rows), jnp.float32),
            shaped((128, rows), jnp.int32),
        ],
        scratch_shapes=[
            pltpu.VMEM((rows, rows), jnp.float32),
            pltpu.VMEM((rows, BLOCK), jnp.float32),
            pltpu.VMEM((HEAD_DIM, rows), low_type),
        ],
        compiler_params=pltpu.CompilerParams(vmem_limit_bytes=48 * 2**20),
        cost_estimate=pl.CostEstimate(flops=2**34, bytes_accessed=2**24, transcendentals=0),
    )(normed, near, w_query, w_key, w_value)


def fetch(parts, to_ref, sems):
    copies, lower = [], 0
    for position, part in enumerate(parts):
        upper = lower + part.shape[0]
        copies.append(pltpu.make_async_copy(part, to_ref.at[lower:upper, :], sems.at[position]))
        copies[-1].start()
        lower = upper
    return copies


def attend_far_kernel(
    skip, modulation_ref, query_ref, w_key_ref, w_value_ref, packed_ref, top_ref, total_ref, mixed_ref, *refs
):
    landed_refs, refs = refs[:4], refs[4:]
    attended_ref, raised_ref, spread_own_ref, spread_far_ref, key_ref, value_ref, plain_ref, normed_ref, *refs = refs
    bias, scores, value_t, sems = refs
    far, rows = bias.shape

    @pl.when(pl.program_id(0) == 0)
    def _():
        copies = fetch(landed_refs, plain_ref, sems)

        @pl.loop(0, rows // 128)
        def _(step):
            cols = pl.ds(pl.multiple_of(step * 128, 128), 128)
            for g in range(far // 128):
                bias[g * 128 : (g + 1) * 128, cols] = count_bias(packed_ref[:, cols], g + skip)

        for copy in copies:
            copy.wait()
        plain = plain_ref[...].astype(jnp.float32)
        normed_ref[...] = (plain * (1.0 + modulation_ref[0:1, :]) + modulation_ref[1:2, :]).astype(low_type)

    key_ref[...] = dot(normed_ref[...], w_key_ref[...], 1, 0).astype(low_type)
    value_ref[...] = dot(normed_ref[...], w_value_ref[...], 1, 0).astype(low_type)
    value_t[...] = value_ref[...].T
    width = scores.shape[1]

    @pl.loop(0, rows // width)
    def _(step):
        cols = pl.ds(pl.multiple_of(step * width, width), width)
        own_top = top_ref[0, :, cols]
        least = jnp.broadcast_to(own_top, (8, width))
        top = score_pass(key_ref, query_ref[cols, :], bias, scores, cols, least)
        factor = jnp.exp(own_top - top)
        total = raise_pass(scores, top, raised_ref, cols) + total_ref[0, :, cols] * factor
        inverse = 1.0 / total
        own_inverse = inverse * factor
        spread_far_ref[cols, :] = jnp.broadcast_to(inverse, (HEAD_DIM, width)).T
        spread_own_ref[cols, :] = jnp.broadcast_to(own_inverse, (HEAD_DIM, width)).T
        mixed = dot(value_t[...], raised_ref[0, :, cols], 1, 0) * inverse + mixed_ref[0, :, cols] * own_inverse
        attended_ref[cols, :] = mixed.T.astype(low_type)


def attend_far(modulation, queries, w_key, w_value, packed, top, total, mixed, landed):
    rows, width = queries.shape
    far = sum(part.shape[0] for part in landed)
    by_row = pl.BlockSpec((rows, HEAD_DIM), lambda h: (0, h))
    by_far = pl.BlockSpec((far, HEAD_DIM), lambda h: (0, h))
    by_weight = pl.BlockSpec((width, HEAD_DIM), lambda h: (0, h))
    by_head = pl.BlockSpec((1, 1, rows), lambda h: (h, 0, 0))
    groups = (rows + far) // 128
    return pl.pallas_call(
        functools.partial(attend_far_kernel, rows // 128 - groups // 2),
        grid=(HEADS,),
        in_specs=[
            pl.BlockSpec(modulation.shape, lambda h: (0, 0)),
            by_row,
            by_weight,
            by_weight,
            pl.BlockSpec(packed.shape, lambda h: (0, 0)),
            by_head,
            by_head,
            pl.BlockSpec((1, HEAD_DIM, rows), lambda h: (h, 0, 0)),
        ]
        + [anywhere] * len(landed),
        out_specs=[by_row, pl.BlockSpec((1, far, rows), lambda h: (h, 0, 0)), by_row, by_row, by_far, by_far]
        + [pl.BlockSpec((far, width), lambda h: (0, 0))] * 2,
        out_shape=[
            shaped((rows, width)),
            shaped((HEADS, far, rows)),
            shaped((rows, width), jnp.float32),
            shaped((rows, width), jnp.float32),
            shaped((far, width)),
            shaped((far, width)),
            shaped((far, width)),
            shaped((far, width)),
        ],
        scratch_shapes=[
            pltpu.VMEM((far, rows), jnp.float32),
            pltpu.VMEM((far, BLOCK), jnp.float32),
            pltpu.VMEM((HEAD_DIM, far), low_type),
            pltpu.SemaphoreType.DMA((len(landed),)),
        ],
        compiler_params=pltpu.CompilerParams(vmem_limit_bytes=48 * 2**20),
        cost_estimate=pl.CostEstimate(flops=2**33, bytes_accessed=2**23, transcendentals=0),
    )(modulation, queries, w_key, w_value, packed, top, total, mixed, *landed)


def attend_back_kernel(query_ref, attended_ref, *refs):
    sides, refs = (refs[:4], refs[4:8]), refs[8:]
    grad_query_ref, refs = refs[0], refs[1:]
    grads, scratch = (refs[0:2], refs[2:4]), (refs[4:6], refs[6:8])
    rows = query_ref.shape[0]
    for (key_ref, *_), (_, key_t) in zip(sides, scratch):
        key_t[...] = key_ref[...].T

    @pl.loop(0, rows // BLOCK)
    def _(step):
        cols = pl.ds(pl.multiple_of(step * BLOCK, BLOCK), BLOCK)
        attended = attended_ref[cols, :].astype(jnp.float32)
        total = 0.0
        for (_, value_ref, grad_ref, raised_ref), (low, key_t) in zip(sides, scratch):
            grad = grad_ref[cols, :]
            mean = jnp.sum((grad.astype(jnp.float32) * attended).T, axis=0, keepdims=True)
            for g in range(value_ref.shape[0] // 128):
                part = slice(g * 128, (g + 1) * 128)
                term = dot(value_ref[part, :], grad, 1, 1) - mean
                low[part, cols] = (term * raised_ref[0, part, cols].astype(jnp.float32)).astype(low_type)
            total = total + dot(key_t[...], low[:, cols], 1, 0)
        grad_query_ref[cols, :] = (total * score_scale).T.astype(low_type)

    for (_, _, grad_ref, raised_ref), (low, _), (grad_key_ref, grad_value_ref) in zip(sides, scratch, grads):
        grad_value_ref[...] = dot(raised_ref[0], grad_ref[...], 1, 0).astype(low_type)
        grad_key_ref[...] = (dot(low[...], query_ref[...], 1, 0) * score_scale).astype(low_type)


def attend_back(first, heads, queries, attended, own, far):
    rows = queries.shape[0]
    by_row = pl.BlockSpec((rows, HEAD_DIM), lambda h: (0, h + first))
    in_specs, out_specs, out_shape, scratch = [], [], [], []
    for keys, _, _, raised in (own, far):
        count = keys.shape[0]
        by_count = pl.BlockSpec((count, HEAD_DIM), lambda h: (0, h + first))
        in_specs += [by_count, by_count, by_row, pl.BlockSpec((1, count, rows), lambda h: (h + first, 0, 0))]
        out_specs += [pl.BlockSpec((count, HEAD_DIM), lambda h: (0, h))] * 2
        out_shape += [shaped((count, heads * HEAD_DIM))] * 2
        scratch += [pltpu.VMEM((count, rows), low_type), pltpu.VMEM((HEAD_DIM, count), low_type)]
    return pl.pallas_call(
        attend_back_kernel,
        grid=(heads,),
        in_specs=[by_row, by_row] + in_specs,
        out_specs=[pl.BlockSpec((rows, HEAD_DIM), lambda h: (0, h))] + out_specs,
        out_shape=[shaped((rows, heads * HEAD_DIM))] + out_shape,
        scratch_shapes=scratch,
        compiler_params=pltpu.CompilerParams(vmem_limit_bytes=48 * 2**20),
        cost_estimate=pl.CostEstimate(flops=heads * 2**33, bytes_accessed=2**22, transcendentals=0),
    )(queries, attended, *own, *far)


def live_rows(count_ref, start, rows):
    place = lax.broadcasted_iota(jnp.int32, (rows, 1), 0) + start
    return (place < count_ref[0]).astype(jnp.float32)


class Mover:
    def __init__(self, sems):
        self.sems, self.used, self.open = sems, 0, []

    def start(self, source, target):
        copy = pltpu.make_async_copy(source, target, self.sems.at[self.used])
        self.used += 1
        copy.start()
        return copy

    def send(self, source, target):
        self.open.append(self.start(source, target))

    def finish(self):
        for copy in self.open:
            copy.wait()


def feed_chunk(weight_ref, second_ref, branch_ref, out_ref, grad_ref, hidden, grad_gate, grad_up, store, fresh, done):
    units = weight_ref.shape[0] // 3
    gate_rows, up_rows, down_rows = (slice(i * units, (i + 1) * units) for i in range(3))
    for step in range(second_ref.shape[0] // ROW_BLOCK):
        rows = slice(step * ROW_BLOCK, (step + 1) * ROW_BLOCK)
        second = second_ref[rows, :]
        gate = dot(second, weight_ref[gate_rows, :], 1, 0)
        up = dot(second, weight_ref[up_rows, :], 1, 0)
        sigmoid = 1.0 / (1.0 + jnp.exp(-gate))
        activated = gate * sigmoid
        hidden[rows, :] = (activated * up).astype(low_type)
        back = dot(branch_ref[rows, :], weight_ref[down_rows, :], 1, 1)
        grad_gate[rows, :] = (back * up * (sigmoid + activated * (1.0 - sigmoid))).astype(low_type)
        grad_up[rows, :] = (back * activated).astype(low_type)
        out = dot(hidden[rows, :], weight_ref[down_rows, :], 1, 0)
        grad = dot(grad_gate[rows, :], weight_ref[gate_rows, :], 1, 1) + dot(
            grad_up[rows, :], weight_ref[up_rows, :], 1, 1
        )
        if fresh:
            out_ref[rows, :] = out
            grad_ref[rows, :] = grad
        else:
            out_ref[rows, :] += out
            grad_ref[rows, :] += grad
        if done is not None:
            done(rows)

    one, two = store
    half = units // 2
    one[:units, :] = dot(second_ref[...], grad_gate[...], 0, 0).astype(low_type)
    grad_up_weight = dot(second_ref[...], grad_up[...], 0, 0).astype(low_type)
    one[units:, :] = grad_up_weight[:half, :]
    two[:half, :] = grad_up_weight[half:, :]
    two[half : half + units, :] = dot(hidden[...], branch_ref[...], 0, 0).astype(low_type)


def feed_first_kernel(
    count_ref, modulation_ref, states_in, cotangent_in, attended_in, w_out_in, core_in, own_in,
    middle_out, second_out, branch_out, out_out, grad_out, core_one_out, core_two_out, own_one_out, own_two_out,
    states, cotangent, attended, w_out, core, own, second, branch, out, grad,
    core_one, core_two, own_one, own_two, hidden, grad_gate, grad_up, in_sems, out_sems,
):
    come, go = Mover(in_sems), Mover(out_sems)
    w_out_copy = come.start(w_out_in, w_out)
    blocks = [slice(lower, lower + ROW_BLOCK) for lower in range(0, states.shape[0], ROW_BLOCK)]
    row_copies = [
        [come.start(source.at[rows, :], target.at[rows, :])
         for source, target in ((attended_in, attended), (states_in, states), (cotangent_in, cotangent))]
        for rows in blocks
    ]
    weight_copies = [come.start(core_in, core), come.start(own_in, own)]
    w_out_copy.wait()
    for rows, copies in zip(blocks, row_copies):
        for copy in copies:
            copy.wait()
        live = live_rows(count_ref, rows.start, ROW_BLOCK)
        middle = states[rows, :] + live * dot(attended[rows, :], w_out[...], 1, 0)
        states[rows, :] = middle
        plain, _ = norm_parts(middle)
        second[rows, :] = (plain * (1.0 + modulation_ref[2:3, :]) + modulation_ref[3:4, :]).astype(low_type)
        branch[rows, :] = (live * cotangent[rows, :]).astype(low_type)
        for source, target in ((states, middle_out), (second, second_out), (branch, branch_out)):
            go.send(source.at[rows, :], target.at[rows, :])

    def done(rows):
        go.send(out.at[rows, :], out_out.at[rows, :])
        go.send(grad.at[rows, :], grad_out.at[rows, :])

    scratch = (hidden, grad_gate, grad_up)
    weight_copies[0].wait()
    feed_chunk(core, second, branch, out, grad, *scratch, (core_one, core_two), True, None)
    go.send(core_one, core_one_out)
    go.send(core_two, core_two_out)
    weight_copies[1].wait()
    feed_chunk(own, second, branch, out, grad, *scratch, (own_one, own_two), False, done)
    go.send(own_one, own_one_out)
    go.send(own_two, own_two_out)
    go.finish()


def feed_last_kernel(
    count_ref, core_ref, modulation_ref, cotangent_in, attended_in, w_out_in, spread_own_in, spread_far_in,
    middle_in, second_in, branch_in, out_in, grad_in, cross_in, far_in,
    output_out, grad_middle_out, grad_own_out, grad_far_out, mod_grad_ref,
    cross_one_out, cross_two_out, far_one_out, far_two_out,
    cotangent, attended, w_out, spread_own, spread_far, middle, second, branch, out, grad, cross, far,
    grad_own, grad_far, cross_one, cross_two, far_one, far_two, w_out_grad,
    hidden, grad_gate, grad_up, in_sems, out_sems,
):
    come, go = Mover(in_sems), Mover(out_sems)
    first_copies = [
        come.start(source, target)
        for source, target in ((second_in, second), (cross_in, cross), (branch_in, branch), (out_in, out), (grad_in, grad))
    ]
    late_copies = [
        come.start(source, target)
        for source, target in (
            (far_in, far), (w_out_in, w_out), (middle_in, middle), (cotangent_in, cotangent),
            (spread_own_in, spread_own), (spread_far_in, spread_far), (attended_in, attended),
        )
    ]
    scratch = (hidden, grad_gate, grad_up)
    for copy in first_copies:
        copy.wait()
    feed_chunk(cross, second, branch, out, grad, *scratch, (cross_one, cross_two), False, None)
    go.send(cross_one, cross_one_out)
    for copy in late_copies:
        copy.wait()
    feed_chunk(far, second, branch, out, grad, *scratch, (far_one, far_two), False, None)
    go.send(far_one, far_one_out)
    low_grad = hidden
    scale, bias = 0.0, 0.0
    for lower in range(0, middle.shape[0], ROW_BLOCK):
        rows = slice(lower, lower + ROW_BLOCK)
        live = live_rows(count_ref, lower, ROW_BLOCK)
        block = middle[rows, :]
        plain, inverse = norm_parts(block)
        middle[rows, :] = block + live * out[rows, :]
        go.send(middle.at[rows, :], output_out.at[rows, :])
        grad_second = grad[rows, :]
        scale += jnp.sum(grad_second * plain, axis=0, keepdims=True)
        bias += jnp.sum(grad_second, axis=0, keepdims=True)
        grad_middle = cotangent[rows, :] + norm_back(grad_second * (1.0 + modulation_ref[2:3, :]), plain, inverse)
        cotangent[rows, :] = grad_middle
        go.send(cotangent.at[rows, :], grad_middle_out.at[rows, :])
        low_grad[rows, :] = (live * grad_middle).astype(low_type)
        grad_attended = dot(low_grad[rows, :], w_out[...], 1, 1)
        grad_own[rows, :] = (grad_attended * spread_own[rows, :]).astype(low_type)
        grad_far[rows, :] = (grad_attended * spread_far[rows, :]).astype(low_type)
        go.send(grad_own.at[rows, :], grad_own_out.at[rows, :])
        go.send(grad_far.at[rows, :], grad_far_out.at[rows, :])
    mod_grad_ref[0:1, :] = scale
    mod_grad_ref[1:2, :] = bias

    half = w_out_grad.shape[0] // 2
    w_out_grad[...] = dot(attended[...], low_grad[...], 0, 0).astype(low_type)
    for two, two_out, side_of in ((far_two, far_two_out, core_ref[0]), (cross_two, cross_two_out, 1 - core_ref[0])):
        start = pl.multiple_of(side_of * half, half)
        two[two.shape[0] - half :, :] = w_out_grad[pl.ds(start, half), :]
        go.send(two, two_out)
    go.finish()


def return_kernel(parts, w_key_ref, w_value_ref, *refs):
    plain_ref, *refs = refs
    pieces, (*parcel_refs, mod_grad_ref) = refs[: 2 * parts], refs[2 * parts :]
    cols = w_key_ref.shape[1] // parts
    scale, bias = 0.0, 0.0
    for position, parcel_ref in enumerate(parcel_refs):
        sends = parcel_ref.shape[0]
        part_rows = slice(position * sends, (position + 1) * sends)
        grad = sum(
            dot(pieces[part * 2 + kind][part_rows, :], weight_ref[:, part * cols : (part + 1) * cols], 1, 1)
            for part in range(parts)
            for kind, weight_ref in enumerate((w_key_ref, w_value_ref))
        )
        scale += jnp.sum(grad * plain_ref[part_rows, :].astype(jnp.float32), axis=0, keepdims=True)
        bias += jnp.sum(grad, axis=0, keepdims=True)
        parcel_ref[...] = grad.astype(low_type)
    mod_grad_ref[0:1, :] = scale
    mod_grad_ref[1:2, :] = bias


def project_back_kernel(
    parts, normed_ref, plain_ref, normed_far_ref, mod_far_ref, mod_two_ref, w_query_ref, w_key_ref, w_value_ref, *refs
):
    pieces, refs = refs[: 5 * parts], refs[5 * parts :]
    weight_grad_ref, grad_normed_ref, mod_grad_ref = refs
    rows, width = normed_ref.shape
    cols = width // parts
    for kind in range(3):
        for part in range(parts):
            grad = dot(normed_ref[...], pieces[part * 5 + kind][...], 0, 0)
            if kind:
                grad += dot(normed_far_ref[...], pieces[part * 5 + kind + 2][...], 0, 0)
            weight_grad_ref[kind, :, part * cols : (part + 1) * cols] = grad.astype(low_type)
    mod_grad_ref[0:2, :] = mod_far_ref[...]
    mod_grad_ref[2:4, :] = mod_two_ref[...]

    @pl.loop(0, rows // ROW_BLOCK)
    def _(step):
        block = pl.ds(pl.multiple_of(step * ROW_BLOCK, ROW_BLOCK), ROW_BLOCK)
        grad = sum(
            dot(pieces[part * 5 + kind][block, :], weight_ref[:, part * cols : (part + 1) * cols], 1, 1)
            for part in range(parts)
            for kind, weight_ref in enumerate((w_query_ref, w_key_ref, w_value_ref))
        )
        grad_normed_ref[block, :] = grad
        mod_grad_ref[0:1, :] += jnp.sum(grad * plain_ref[block, :].astype(jnp.float32), axis=0, keepdims=True)
        mod_grad_ref[1:2, :] += jnp.sum(grad, axis=0, keepdims=True)


def finish_kernel(states_ref, grad_normed_ref, grad_middle_ref, modulation_ref, send_ref, *refs):
    returned_refs, (grad_states_ref, returned, sems) = refs[:4], refs[4:]

    @pl.when(pl.program_id(0) == 0)
    def _():
        for copy in fetch(returned_refs, returned, sems):
            copy.wait()

    rows = states_ref.shape[0]
    sends = send_ref.shape[1]
    grad = grad_normed_ref[...]
    for position in range(len(returned_refs)):
        chosen = chosen_rows(send_ref, position, rows, pl.program_id(0) * rows)
        grad += dot(chosen, returned[position * sends : (position + 1) * sends, :], 1, 0)
    plain, inverse = norm_parts(states_ref[...])
    grad_states_ref[...] = grad_middle_ref[...] + norm_back(grad * (1.0 + modulation_ref[0:1, :]), plain, inverse)


def finish(states, grad_normed, grad_middle, modulation, send_list, returned):
    rows, width = states.shape
    by_block = pl.BlockSpec((ROW_BLOCK, width), lambda i: (i, 0))
    return pl.pallas_call(
        finish_kernel,
        grid=(rows // ROW_BLOCK,),
        in_specs=[by_block] * 3
        + [pl.BlockSpec(modulation.shape, lambda i: (0, 0)), pl.BlockSpec(send_list.shape, lambda i: (0, 0))]
        + [anywhere] * len(returned),
        out_specs=by_block,
        out_shape=shaped((rows, width), jnp.float32),
        scratch_shapes=[
            pltpu.VMEM((sum(part.shape[0] for part in returned), width), low_type),
            pltpu.SemaphoreType.DMA((len(returned),)),
        ],
        compiler_params=pltpu.CompilerParams(vmem_limit_bytes=32 * 2**20),
        cost_estimate=pl.CostEstimate(flops=2**31, bytes_accessed=2**23, transcendentals=0),
    )(states, grad_normed, grad_middle, modulation, send_list, *returned)


def from_behind(block, axis, distance):
    devices = range(lax.axis_size(axis))
    route = [((i - distance) % len(devices), i) for i in devices]
    return lax.ppermute(block, axis, route)


def swap(block, mask):
    count = lax.axis_size("nodes") * lax.axis_size("hid")
    return lax.ppermute(block, everywhere, [(i, i ^ mask) for i in range(count)])


def place():
    return lax.axis_index("nodes") * lax.axis_size("hid") + lax.axis_index("hid")


def side(link):
    return (place() >> link) & 1


def pieces_of(block, count, index):
    size = block.shape[1] // count
    return lax.dynamic_slice_in_dim(block, index * size, size, 1)


def half_sum(block, link):
    return pieces_of(block, 2, side(link)) + swap(pieces_of(block, 2, 1 - side(link)), 1 << link)


def half_join(block, link):
    other = swap(block, 1 << link)
    return jnp.where(
        side(link) == 0, jnp.concatenate([block, other], axis=1), jnp.concatenate([other, block], axis=1)
    )


def pack_wide(values):
    high = lax.reduce_precision(values, 8, 7)
    both = jnp.concatenate([high, values - high]).astype(low_type)
    return jnp.concatenate([both, jnp.zeros((16 - both.shape[0], both.shape[1]), low_type)])


def unpack_wide(packed, count):
    packed = packed.astype(jnp.float32)
    return packed[:count] + packed[count : 2 * count]


def group_sum(block, wide, links):
    count = 1 << len(links)
    here = sum(side(link) << i for i, link in enumerate(links))
    total = pieces_of(block, count, here).astype(jnp.float32)
    shape = total.shape
    packed = pack_wide(wide)
    for mask in range(1, count):
        sent = pieces_of(block, count, here ^ mask).reshape(-1, shape[-1])
        come = swap(jnp.concatenate([sent, packed]), sum(((mask >> i) & 1) << link for i, link in enumerate(links)))
        total = total + come[: -packed.shape[0]].reshape(shape).astype(jnp.float32)
        wide = wide + unpack_wide(come[-packed.shape[0] :], wide.shape[0])
    return total.astype(low_type), wide


def group_join(block, links):
    found = [block]
    for mask in range(1, 1 << len(links)):
        found.append(swap(block, sum(((mask >> i) & 1) << link for i, link in enumerate(links))))
    for i, link in enumerate(links):
        turned = [found[k ^ (1 << i)] for k in range(len(found))]
        found = [jnp.where(side(link) == 0, kept, other) for kept, other in zip(found, turned)]
    return jnp.concatenate(found, axis=1)


def after(values, previous):
    return lax.optimization_barrier((values, previous))


def body(
    states,
    condition,
    mod_w,
    w_query,
    w_key,
    w_value,
    w_out,
    w_gate,
    w_up,
    w_down,
    counts,
    send_rows,
    neighbours,
    cotangent,
):
    rows, width = states.shape
    sends = send_rows.shape[2]
    ext = rows + len(halo_steps) * sends
    f32 = jnp.float32
    parcel = shaped((sends, width))
    send_list = send_rows[0]

    links = (lax.axis_size("nodes") * lax.axis_size("hid")).bit_length() - 1
    core, across, *around = range(links)

    normed, plain, modulation, *parcels = call(
        prepare_kernel,
        [shaped((rows, width)), shaped((rows, width)), shaped((4, width), f32)] + [parcel] * 4,
        (states, condition, mod_w, send_list),
        specs=[whole, scalars, whole, whole],
        flops=2**30,
        moved=2**22,
    )
    landed = [from_behind(part, everywhere, hop) for part, hop in zip(parcels, halo_steps)]
    shard = jnp.concatenate([w_gate, w_up, w_down])
    far_shard = swap(shard, 1 << across)
    core_shard = swap(shard, 1 << core)

    queries, own_keys, own_values, own_raised, top, total, mixed, packed = attend_own(
        normed, neighbours.T, w_query, w_key, w_value, ext - rows
    )
    attended, far_raised, spread_own, spread_far, far_keys, far_values, plain_far, normed_far = attend_far(
        modulation, queries, w_key, w_value, packed, top, total, mixed, landed
    )
    far_shard, attended = after(far_shard, attended)
    cross_shard = swap(far_shard, 1 << core)

    low_rows = shaped((rows, width))
    wide_rows = shaped((rows, width), f32)
    shard_rows = shard.shape[0]
    half_grad = shaped((shard_rows // 2, width))
    joint_grad = shaped((shard_rows // 2 + width // 2, width))

    def room(*shapes):
        return [pltpu.VMEM(one.shape, one.dtype) for one in shapes]

    middle, second, branch, out, grad, core_one, core_two, own_one, own_two = call(
        feed_first_kernel,
        [wide_rows, low_rows, low_rows, wide_rows, wide_rows] + [half_grad] * 4,
        (counts, modulation, states, cotangent, attended, w_out, core_shard, shard),
        specs=[scalars, whole] + [anywhere] * 6,
        out_specs=[anywhere] * 9,
        scratch=room(wide_rows, wide_rows, low_rows, w_out, shard, shard, low_rows, low_rows, wide_rows, wide_rows)
        + room(*[half_grad] * 4, *[low_rows] * 3)
        + [pltpu.SemaphoreType.DMA((3 + 3 * rows // ROW_BLOCK,)), pltpu.SemaphoreType.DMA((4 + 5 * rows // ROW_BLOCK,))],
        flops=2**34,
        moved=2**24,
    )
    core_index = lax.axis_index("hid")[None] & 1
    output, grad_middle, grad_own, grad_far, mod_two, cross_one, cross_two, far_one, far_two = call(
        feed_last_kernel,
        [wide_rows, wide_rows, low_rows, low_rows, shaped((2, width), f32)] + [half_grad, joint_grad] * 2,
        (counts, core_index, modulation, cotangent, attended, w_out, spread_own, spread_far)
        + (middle, second, branch, out, grad, cross_shard, far_shard),
        specs=[scalars, scalars, whole] + [anywhere] * 12,
        out_specs=[anywhere] * 4 + [whole] + [anywhere] * 4,
        scratch=room(wide_rows, low_rows, w_out, wide_rows, wide_rows, wide_rows, low_rows, low_rows)
        + room(wide_rows, wide_rows, shard, shard, low_rows, low_rows, half_grad, joint_grad, half_grad, joint_grad)
        + room(w_out, *[low_rows] * 3)
        + [pltpu.SemaphoreType.DMA((12,)), pltpu.SemaphoreType.DMA((4 + 4 * rows // ROW_BLOCK,))],
        flops=2**34,
        moved=2**24,
    )

    fold = (-1, width // 2, width)

    def over_cores(kept, sent):
        return (kept + swap(sent, 1 << core)).reshape(fold)

    one_own, two_own = over_cores(own_one, core_one), over_cores(own_two, core_two)
    one_far, two_far = over_cores(far_one, cross_one), over_cores(far_two, cross_two)
    kept = one_own.shape[0]
    first, second_link, *rest = around

    own = (own_keys, own_values, grad_own, own_raised)
    far = (far_keys, far_values, grad_far, far_raised)
    parts = 2
    heads = HEADS // parts
    pieces = [attend_back(0, heads, queries, attended, own, far)]
    own, (one_own, one_far, two_own, two_far) = after(own, (one_own, one_far, two_own, two_far))
    one = one_own + swap(one_far, 1 << across)
    here = side(second_link)
    come = swap(
        jnp.concatenate([pieces_of(two_own, 2, 1 - here), pieces_of(two_far, 2, 1 - here)]), 1 << second_link
    )
    two_own = pieces_of(two_own, 2, here) + come[:kept]
    two_far = pieces_of(two_far, 2, here) + come[kept:]
    pieces.append(attend_back(heads, heads, queries, attended, own, far))
    far_pieces = [piece for found in pieces for piece in found[3:]]
    *parcels, mod_far = call(
        functools.partial(return_kernel, parts),
        [parcel] * 4 + [shaped((2, width), f32)],
        (w_key, w_value, plain_far, *far_pieces),
        flops=2**30,
        moved=2**22,
    )
    returned = [from_behind(part, everywhere, -hop) for part, hop in zip(parcels, halo_steps)]
    (one, two_own, two_far), pieces = after((one, two_own, two_far), pieces)
    attn_grad, grad_normed, mod_grad = call(
        functools.partial(project_back_kernel, parts),
        [shaped((3, width, width)), wide_rows, shaped((4, width), f32)],
        (normed, plain, normed_far, mod_far, mod_two, w_query, w_key, w_value)
        + tuple(piece for found in pieces for piece in found),
        flops=2**33,
        moved=2**23,
    )

    one = half_sum(one, first)
    come = swap(two_far, 1 << across)
    two = jnp.concatenate([two_own + come[:kept], two_far[kept:] + come[kept:]])
    one = half_sum(one, second_link)
    two = half_sum(two, first)
    both = jnp.concatenate([one, two])
    for link in rest:
        both = half_sum(both, link)
    for link in reversed(rest):
        both = half_join(both, link)
    one, two = half_join(both[:kept], second_link), half_join(both[kept:], first)
    one, two = half_join(one, first), half_join(two, second_link)
    shard_grad = jnp.concatenate([one, two[:kept]]).reshape(-1, width).astype(f32)
    grad_w_gate, grad_w_up, grad_w_down = jnp.split(shard_grad, 3)

    groups = [[across, first]] + [around[i : i + 2] for i in range(1, len(around), 2)]
    attn_grad, mod_grad = group_sum(attn_grad, mod_grad, [core])
    for group in groups:
        attn_grad, mod_grad = group_sum(attn_grad, mod_grad, group)
    for group in reversed(groups):
        attn_grad = group_join(attn_grad, group)
    attn_grad = half_join(attn_grad, core).astype(f32)
    grad_w_query, grad_w_key, grad_w_value = attn_grad
    grad_w_out = half_join(two[kept:], core)[0].astype(f32)

    grad_states = finish(states, grad_normed, grad_middle, modulation, send_list, returned)
    mod_grad = mod_grad.reshape(-1)
    grad_mod_w = condition[:, None] * mod_grad[None, :]
    grad_condition = jnp.sum(mod_w.astype(f32) * mod_grad[None, :], axis=1)
    return (
        output,
        grad_states,
        grad_condition,
        grad_mod_w,
        grad_w_query,
        grad_w_key,
        grad_w_value,
        grad_w_out,
        grad_w_gate,
        grad_w_up,
        grad_w_down,
    )


def solution(mesh):
    rows = P(everywhere, None)
    placed = (
        rows,
        P(),
        P(),
        P(),
        P(),
        P(),
        P(),
        P(None, "hid"),
        P(None, "hid"),
        P("hid", None),
        P(everywhere),
        P(everywhere, None, None),
        rows,
        rows,
    )
    return jax.shard_map(
        body,
        mesh=mesh,
        in_specs=placed,
        out_specs=(rows, rows, P(), P(), P(), P(), P(), P(), P(None, "hid"), P(None, "hid"), P("hid", None)),
        check_vma=False,
    )
```

time: 313 us -> 268 us (0.86); the launches traced: 312 us -> 263 us
  waiting for transfers between devices: 119 us -> 54 us
  starting transfers between devices: 45.3 us -> 60.3 us
  Pallas kernels: 125 us -> 115 us
  local copies, waits for them, and re-layouts: 10.6 us -> 18.2 us
    ppermute x37 -> x34, waiting for transfers between devices: 116 us -> 44.5 us  [swap(): lax.ppermute(block, everywhere, [(i, i ^ mask) for i in range(count)])]
    ppermute x37 -> x34, starting transfers between devices: 27.1 us -> 46 us  [swap(): lax.ppermute(block, everywhere, [(i, i ^ mask) for i in range(count)])]
    unnamed x45 -> x93, local copies, waits for them, and re-layouts: 3.69 us -> 12.9 us
    pallas_call x9 -> x10, Pallas kernels: 125 us -> 115 us  [the longest x5 54.6 us: call(): pl.pallas_call(kernel, in_specs=specs or [whole] * len(args), out_specs=o...]
    ppermute x8, waiting for transfers between devices: 2.86 us -> 9.47 us  [from_behind(): return lax.ppermute(block, axis, route)]
    ppermute x8, starting transfers between devices: 18.2 us -> 14.3 us  [from_behind(): return lax.ppermute(block, axis, route)]
  transfers between devices with their start and end apart: 45 -> 42, of which waited for: 19 -> 16; matrix products, arithmetic and copies ran while one was open for 5% -> 6% of each run, Pallas kernels for 22% -> 35%
where the time goes in v3:
time: 268 us; the launch traced here: 263 us
  Pallas kernels  115 us (43%)
  starting transfers between devices  60.3 us (22%)
  waiting for transfers between devices  54 us (20%)
  local copies, waits for them, and re-layouts  18.2 us (7%)
  other arithmetic  12.2 us (5%)
    pallas_call x5, Pallas kernels, call(): pl.pallas_call(kernel, in_specs=specs or [whole] * len(args), out_specs=o...  54.6 us
    ppermute x34, starting transfers between devices, swap(): lax.ppermute(block, everywhere, [(i, i ^ mask) for i in range(count)])  46 us
    ppermute x34, waiting for transfers between devices, swap(): lax.ppermute(block, everywhere, [(i, i ^ mask) for i in range(count)])  44.5 us
    pallas_call x2, Pallas kernels, attend_back(): pl.pallas_call(attend_back_kernel, grid=(heads,), in_specs=[by_row, by_ro...  22 us
    pallas_call x1, Pallas kernels, attend_own(): pl.pallas_call(functools.partial(attend_own_kernel, groups), grid=(HEADS,...  20.9 us
    ppermute x8, starting transfers between devices, from_behind(): return lax.ppermute(block, axis, route)  14.3 us
    pallas_call x1, Pallas kernels, attend_far(): pl.pallas_call(functools.partial(attend_far_kernel, rows // 128 - groups...  14 us
    unnamed x93, local copies, waits for them, and re-layouts  12.9 us
  transfers between devices with their start and end apart: 42, of which 16 were waited for; matrix products, arithmetic and copies ran while one was open for 6% of the time, Pallas kernels for 35%

profile of v3, /device:TPU:0, one launch (start us, length us, event | category | flops | bytes accessed | tf_op | source)
XLA Modules:
  0.0 262.7 jit_solution(8071712066968889424)
XLA Ops:
  0.7 4.4 %shard_map.221 = (bf16[1024,512]{1,0:T(8,128)(2,1)}, bf16[1024,512]{1,0:T(8,128)(2,1)}, f32[4,512]{1,0:T(4,128)}, bf16[128,512]{1,0:T(8,128)(2,1)}, bf16[128,512...) custom-call(f32[1024,512]{1,0:T(8,128)} %states_ref.3, f32[16]{0:T(128)} %condition_ref.1, ...), custom_call_target="tpu_custom_call" | custom-call | flops 1073741824 | bytes 4194304 | tf_op jit(solution)/shard_map/pallas_call | solution.py:51
  6.1 3.0 %collective-permute-start = (bf16[1536,512]{1,0:T(8,128)(2,1)S(1)}, bf16[1536,512]{1,0:T(8,128)(2,1)}, u32[]{:S(2)}, u32[]{:S(2)}) collective-permute-start(bf16[1536,512]{1,0:T(8,128)(2,1)S(1)} %constant_dynamic-update-slice_fusion.own_in), channel_id=1, source_target_pairs={{0,2},{1,3},{2,0},{3,1},{4,6},{5,7},{6,4},{7,5},{8,10},{9,11},{10,... | collective-permute-start | bytes 4718600 | tf_op jit(solution)/shard_map/ppermute | solution.py:616
  9.6 4.1 %collective-permute-start.2 = (bf16[128,512]{1,0:T(8,128)(2,1)S(1)}, bf16[128,512]{1,0:T(8,128)(2,1)S(1)}, u32[]{:S(2)}, u32[]{:S(2)}) collective-permute-start(bf16[128,512]{1,0:T(8,128)(2,1)S(1)} %copy-done.42), channel_id=1, source_target_pairs={{1,0},{2,1},{3,2},{4,3},{5,4},{6,5},{7,6},{8,7},{9,8},{10,9},{11,1... | collective-permute-start | bytes 393224 | tf_op jit(solution)/shard_map/ppermute | solution.py:611
  14.5 4.9 %collective-permute-start.4 = (bf16[128,512]{1,0:T(8,128)(2,1)S(1)}, bf16[128,512]{1,0:T(8,128)(2,1)S(1)}, u32[]{:S(2)}, u32[]{:S(2)}) collective-permute-start(bf16[128,512]{1,0:T(8,128)(2,1)S(1)} %copy-done.40), channel_id=1, source_target_pairs={{2,0},{3,1},{4,2},{5,3},{6,4},{7,5},{8,6},{9,7},{10,8},{11,9},{12,... | collective-permute-start | bytes 393224 | tf_op jit(solution)/shard_map/ppermute | solution.py:611
  19.4 20.9 %shard_map.222 = (bf16[1024,512]{1,0:T(8,128)(2,1)S(1)}, bf16[1024,512]{1,0:T(8,128)(2,1)S(1)}, bf16[1024,512]{1,0:T(8,128)(2,1)S(1)}, bf16[4,1024,1024]{2,1,0:T...) custom-call(bf16[1024,512]{1,0:T(8,128)(2,1)} %get-tuple-element.94., ...), custom_call_target="tpu_custom_call" | custom-call | flops 17179869184 | bytes 16777216 | tf_op jit(solution)/shard_map/pallas_call | solution.py:172
  44.0 7.0 %collective-permute-done.3.refs_2_ = bf16[128,512]{1,0:T(8,128)(2,1)S(1)} collective-permute-done((bf16[128,512]{1,0:T(8,128)(2,1)S(1)}, bf16[128,512]{1,0:T(8,128)(2,1)S(1)}, u32[]{:S(2)}, u32[]{:S(2)}) %collective-permute-start.3) | collective-permute-done | bytes 131104 | tf_op jit(solution)/shard_map/ppermute | solution.py:611
  51.0 1.7 collective-permute-done.4.refs_3_
  52.7 14.0 %shard_map.223 = (bf16[1024,512]{1,0:T(8,128)(2,1)S(1)}, bf16[4,512,1024]{2,1,0:T(8,128)(2,1)}, f32[1024,512]{1,0:T(8,128)}, f32[1024,512]{1,0:T(8,128)}, bf16[5...) custom-call(f32[4,512]{1,0:T(4,128)S(1)} %copy-done.3, ...), custom_call_target="tpu_custom_call" | custom-call | flops 8589934592 | bytes 8388608 | tf_op jit(solution)/shard_map/pallas_call | solution.py:267
  68.6 1.2 copy-done.39
  69.8 16.8 %shard_map.224 = (f32[1024,512]{1,0:T(8,128)}, bf16[1024,512]{1,0:T(8,128)(2,1)}, bf16[1024,512]{1,0:T(8,128)(2,1)}, f32[1024,512]{1,0:T(8,128)}, f32[1024,512]{...) custom-call(s32[1]{0:T(128)S(6)} %copy.36.count_ref, ...), custom_call_target="tpu_custom_call" | custom-call | flops 17179869184 | bytes 16777216 | tf_op jit(solution)/shard_map/pallas_call | solution.py:51
  87.1 2.1 collective-permute-done.9
  89.3 1.6 add.211
  91.1 19.8 %shard_map.225 = (f32[1024,512]{1,0:T(8,128)}, f32[1024,512]{1,0:T(8,128)}, bf16[1024,512]{1,0:T(8,128)(2,1)}, bf16[1024,512]{1,0:T(8,128)(2,1)}, f32[2,512]{1,0...) custom-call(s32[1]{0:T(128)S(6)} %copy.36.count_ref, ...), custom_call_target="tpu_custom_call" | custom-call | flops 17179869184 | bytes 16777216 | tf_op jit(solution)/shard_map/pallas_call | solution.py:51
  111.5 11.1 %shard_map.226 = (bf16[1024,256]{1,0:T(8,128)(2,1)S(1)}, bf16[1024,256]{1,0:T(8,128)(2,1)S(1)}, bf16[1024,256]{1,0:T(8,128)(2,1)S(1)}, bf16[512,256]{1,0:T(8,128)(2,1)S(1)}, bf16[512,256]{1,0:T(8,128)(2,1)S(1)}) custom-call(bf16[1024,512]{1,0:T(8,128)(2,1)S(1)} %copy-done.16, bf16[1024,512]{1,0:T(8,128)(2,1)S(1)} %copy-done.18, ...), custom_call_target="tpu_custom_call" | custom-call | flops 17179869184 | bytes 4194304 | tf_op jit(solution)/shard_map/pallas_call | solution.py:343
  125.2 2.2 collective-permute-start.12
  127.3 1.5 collective-permute-start.11
  128.8 10.9 %shard_map.227 = (bf16[1024,256]{1,0:T(8,128)(2,1)S(1)}, bf16[1024,256]{1,0:T(8,128)(2,1)S(1)}, bf16[1024,256]{1,0:T(8,128)(2,1)S(1)}, bf16[512,256]{1,0:T(8,128)(2,1)S(1)}, bf16[512,256]{1,0:T(8,128)(2,1)S(1)}) custom-call(bf16[1024,512]{1,0:T(8,128)(2,1)S(1)} %copy-done.16, bf16[1024,512]{1,0:T(8,128)(2,1)S(1)} %copy-done.18, ...), custom_call_target="tpu_custom_call" | custom-call | flops 17179869184 | bytes 4194304 | tf_op jit(solution)/shard_map/pallas_call | solution.py:343
  143.6 3.8 %shard_map.228 = (bf16[128,512]{1,0:T(8,128)(2,1)}, bf16[128,512]{1,0:T(8,128)(2,1)}, bf16[128,512]{1,0:T(8,128)(2,1)}, bf16[128,512]{1,0:T(8,128)(2,1)}, f32[2,512]{1,0:T(2,128)}) custom-call(bf16[512,512]{1,0:T(8,128)(2,1)} %w_key_ref.7, bf16[512,512]{1,0:T(8,128)(2,1)} %w_value_ref.7, bf16[512,512]{1,0:T(8,128)(2,1)} %copy-done.10, ...), custom_call_target="tpu_custom_call" | custom-call | flops 1073741824 | bytes 4194304 | tf_op jit(solution)/shard_map/pallas_call | solution.py:51
  147.4 2.7 %collective-permute-start.13 = (bf16[128,512]{1,0:T(8,128)(2,1)}, bf16[128,512]{1,0:T(8,128)(2,1)S(1)}, u32[]{:S(2)}, u32[]{:S(2)}) collective-permute-start(bf16[128,512]{1,0:T(8,128)(2,1)} %get-tuple-element.166), channel_id=1, source_target_pairs={{1,0},{2,1},{3,2},{4,3},{5,4},{6,5},{7,6},{8,7},{9,8},{10,9},{11,1... | collective-permute-start | bytes 393224 | tf_op jit(solution)/shard_map/ppermute | solution.py:611
  152.3 1.2 slice_add_fusion
  154.8 9.9 %shard_map.229 = (bf16[3,512,512]{2,1,0:T(8,128)(2,1)}, f32[1024,512]{1,0:T(8,128)}, f32[4,512]{1,0:T(4,128)}) custom-call(bf16[1024,512]{1,0:T(8,128)(2,1)} %get-tuple-element.94.normed_ref, bf16[1024,512]{1,0:T(8,128)(2,1)} %get-tuple-element.115.plain_ref, bf16[512,512]{1,0:T(8,128)(2,1)} %copy-done.19, f32[2,512]{1,0:T(2,128)} %get-tuple-element.142.mod_far_ref, ...), custom_call_target="tpu_custom_call" | custom-call | flops 8589934592 | bytes 8388608 | tf_op jit(solution)/shard_map/pallas_call | solution.py:51
  165.4 1.3 constant_dynamic-slice_fusion.8
  166.9 1.6 collective-permute-start.33
  168.4 2.0 collective-permute-start.17
  170.5 1.6 copy-done.2
  172.1 3.9 %shard_map.230 = f32[1024,512]{1,0:T(8,128)} custom-call(f32[1024,512]{1,0:T(8,128)S(1)} %copy-done, f32[1024,512]{1,0:T(8,128)S(1)} %copy-done.2, f32[1024,512]{1,0:T(8,128)S(1)} %copy-done.1, f32[4,512]{1,0:T(4,128)S(1)} %copy-done.4, s32[4,128]{1,0:T(4,128)S(1)} %bitcast.44, bf16[128,512]{1,0:T(8,128)(2,1)S(1)} %collective-permute-done.13.refs_0_, ...), custom_call_target="tpu_custom_call" | custom-call | flops 2147483648 | bytes 8388608 | tf_op jit(solution)/shard_map/pallas_call | solution.py:591
  176.9 2.6 %collective-permute-done.33 = bf16[4,128,512]{2,1,0:T(8,128)(2,1)S(1)} collective-permute-done((bf16[4,128,512]{2,1,0:T(8,128)(2,1)S(1)}, bf16[4,128,512]{2,1,0:T(8,128)(2,1)S(1)}, u32[]{:S(2)}, u32[]{:S(2)}) %collective-permute-start.33) | collective-permute-done | bytes 524320 | tf_op jit(solution)/shard_map/ppermute | solution.py:616
  179.6 2.0 collective-permute-start.34
  181.7 1.6 collective-permute-done.32
  183.8 2.7 %collective-permute-start.20 = (bf16[208,512]{1,0:T(8,128)(2,1)S(1)}, bf16[208,512]{1,0:T(8,128)(2,1)S(1)}, u32[]{:S(2)}, u32[]{:S(2)}) collective-permute-start(bf16[208,512]{1,0:T(8,128)(2,1)S(1)} %get-tuple-element.212), channel_id=1, source_target_pairs={{0,6},{1,7},{2,4},{3,5},{4,2},{5,3},{6,0},{7,1},{8,14},{9,15},{10,... | collective-permute-start | bytes 638984 | tf_op jit(solution)/shard_map/ppermute | solution.py:616
  187.3 9.4 %collective-permute-start.35 = (bf16[7,32,512]{2,1,0:T(8,128)(2,1)S(1)}, bf16[7,32,512]{2,1,0:T(8,128)(2,1)S(1)}, u32[]{:S(2)}, u32[]{:S(2)}) collective-permute-start(bf16[7,32,512]{2,1,0:T(8,128)(2,1)S(1)} %fusion.6), channel_id=1, source_target_pairs={{0,16},{1,17},{2,18},{3,19},{4,20},{5,21},{6,22},{7,23},{8,24},{9,... | collective-permute-start | bytes 688136 | tf_op jit(solution)/shard_map/ppermute | solution.py:616
  196.7 2.0 collective-permute-start.18
  198.7 6.7 %collective-permute-done.19 = bf16[208,512]{1,0:T(8,128)(2,1)S(1)} collective-permute-done((bf16[208,512]{1,0:T(8,128)(2,1)S(1)}, bf16[208,512]{1,0:T(8,128)(2,1)S(1)}, u32[]{:S(2)}, u32[]{:S(2)}) %collective-permute-start.19) | collective-permute-done | bytes 213024 | tf_op jit(solution)/shard_map/ppermute | solution.py:616
  207.0 3.3 %collective-permute-start.23 = (bf16[64,512]{1,0:T(8,128)(2,1)S(1)}, bf16[64,512]{1,0:T(8,128)(2,1)S(1)}, u32[]{:S(2)}, u32[]{:S(2)}) collective-permute-start(bf16[64,512]{1,0:T(8,128)(2,1)S(1)} %get-tuple-element.209), channel_id=1, source_target_pairs={{0,24},{1,25},{2,26},{3,27},{4,28},{5,29},{6,30},{7,31},{8,16},{9,... | collective-permute-start | bytes 196616 | tf_op jit(solution)/shard_map/ppermute | solution.py:616
  210.4 8.6 %collective-permute-done.22 = bf16[64,512]{1,0:T(8,128)(2,1)S(1)} collective-permute-done((bf16[64,512]{1,0:T(8,128)(2,1)S(1)}, bf16[64,512]{1,0:T(8,128)(2,1)S(1)}, u32[]{:S(2)}, u32[]{:S(2)}) %collective-permute-start.22) | collective-permute-done | bytes 65568 | tf_op jit(solution)/shard_map/ppermute | solution.py:616
  219.1 2.4 collective-permute-start.24
  221.5 2.4 collective-permute-start.26
  224.0 1.7 collective-permute-done.24
  225.7 2.0 collective-permute-done.25
  228.9 2.4 collective-permute-start.29
  231.3 1.4 broadcast_multiply_fusion
  235.0 4.4 %collective-permute-done.28 = bf16[3,64,512]{2,1,0:T(8,128)(2,1)S(1)} collective-permute-done((bf16[3,64,512]{2,1,0:T(8,128)(2,1)S(1)}, bf16[3,64,512]{2,1,0:T(8,128)(2,1)S(1)}, u32[]{:S(2)}, u32[]{:S(2)}) %collective-permute-start.28) | collective-permute-done | bytes 196640 | tf_op jit(solution)/shard_map/ppermute | solution.py:616
  240.2 4.9 %collective-permute-done.37 = bf16[4,64,512]{2,1,0:T(8,128)(2,1)S(1)} collective-permute-done((bf16[4,64,512]{2,1,0:T(8,128)(2,1)S(1)}, bf16[4,64,512]{2,1,0:T(8,128)(2,1)S(1)}, u32[]{:S(2)}, u32[]{:S(2)}) %collective-permute-start.37) | collective-permute-done | bytes 262176 | tf_op jit(solution)/shard_map/ppermute | solution.py:616
  245.3 2.1 collective-permute-start.38
  247.7 4.4 %collective-permute-done.41 = bf16[3,128,512]{2,1,0:T(8,128)(2,1)S(1)} collective-permute-done((bf16[3,128,512]{2,1,0:T(8,128)(2,1)S(1)}, bf16[3,128,512]{2,1,0:T(8,128)(2,1)S(1)}, u32[]{:S(2)}, u32[]{:S(2)}) %collective-permute-start.41) | collective-permute-done | bytes 393248 | tf_op jit(solution)/shard_map/ppermute | solution.py:616
  252.4 4.1 %collective-permute-done.38 = bf16[4,128,512]{2,1,0:T(8,128)(2,1)S(1)} collective-permute-done((bf16[4,128,512]{2,1,0:T(8,128)(2,1)S(1)}, bf16[4,128,512]{2,1,0:T(8,128)(2,1)S(1)}, u32[]{:S(2)}, u32[]{:S(2)}) %collective-permute-start.38) | collective-permute-done | bytes 524320 | tf_op jit(solution)/shard_map/ppermute | solution.py:616
  257.3 1.7 fusion.23
  259.5 1.7 slice_bitcast_fusion
  (213 shorter events, 30.2 us)
Async XLA Ops:
  5.1 9.4 %collective-permute-start.1 = (bf16[128,512]{1,0:T(8,128)(2,1)}, bf16[128,512]{1,0:T(8,128)(2,1)S(1)}, u32[]{:S(2)}, u32[]{:S(2)}) collective-permute-start(bf16[128,512]{1,0:T(8,128)(2,1)} %get-tuple-element.100), channel_id=1, source_target_pairs={{31,0},{0,1},{1,2},{2,3},{3,4},{4,5},{5,6},{6,7},{7,8},{8,9},{9,10... | collective-permute-start | bytes 393224 | tf_op jit(solution)/shard_map/ppermute | solution.py:611
  6.1 34.2 %copy-start.35 = (bf16[1536,512]{1,0:T(8,128)(2,1)}, bf16[1536,512]{1,0:T(8,128)(2,1)S(1)}, u32[]{:S(2)}) copy-start(bf16[1536,512]{1,0:T(8,128)(2,1)S(1)} %constant_dynamic-update-slice_fusion.own_in) | copy-start | bytes 4718596
  6.1 62.3 %collective-permute-start = (bf16[1536,512]{1,0:T(8,128)(2,1)S(1)}, bf16[1536,512]{1,0:T(8,128)(2,1)}, u32[]{:S(2)}, u32[]{:S(2)}) collective-permute-start(bf16[1536,512]{1,0:T(8,128)(2,1)S(1)} %constant_dynamic-update-slice_fusion.own_in), channel_id=1, source_target_pairs={{0,2},{1,3},{2,0},{3,1},{4,6},{5,7},{6,4},{7,5},{8,10},{9,11},{10,... | collective-permute-start | bytes 4718600 | tf_op jit(solution)/shard_map/ppermute | solution.py:616
  9.1 59.5 %collective-permute-start.5 = (bf16[1536,512]{1,0:T(8,128)(2,1)S(1)}, bf16[1536,512]{1,0:T(8,128)(2,1)S(1)}, u32[]{:S(2)}, u32[]{:S(2)}) collective-permute-start(bf16[1536,512]{1,0:T(8,128)(2,1)S(1)} %constant_dynamic-update-slice_fusion.own_in), channel_id=1, source_target_pairs={{0,1},{1,0},{2,3},{3,2},{4,5},{5,4},{6,7},{7,6},{8,9},{9,8},{10,11... | collective-permute-start | bytes 4718600 | tf_op jit(solution)/shard_map/ppermute | solution.py:616
  9.6 34.3 %collective-permute-start.2 = (bf16[128,512]{1,0:T(8,128)(2,1)S(1)}, bf16[128,512]{1,0:T(8,128)(2,1)S(1)}, u32[]{:S(2)}, u32[]{:S(2)}) collective-permute-start(bf16[128,512]{1,0:T(8,128)(2,1)S(1)} %copy-done.42), channel_id=1, source_target_pairs={{1,0},{2,1},{3,2},{4,3},{5,4},{6,5},{7,6},{8,7},{9,8},{10,9},{11,1... | collective-permute-start | bytes 393224 | tf_op jit(solution)/shard_map/ppermute | solution.py:611
  13.8 37.2 %collective-permute-start.3 = (bf16[128,512]{1,0:T(8,128)(2,1)S(1)}, bf16[128,512]{1,0:T(8,128)(2,1)S(1)}, u32[]{:S(2)}, u32[]{:S(2)}) collective-permute-start(bf16[128,512]{1,0:T(8,128)(2,1)S(1)} %copy-done.41), channel_id=1, source_target_pairs={{30,0},{31,1},{0,2},{1,3},{2,4},{3,5},{4,6},{5,7},{6,8},{7,9},{8,1... | collective-permute-start | bytes 393224 | tf_op jit(solution)/shard_map/ppermute | solution.py:611
  14.5 38.2 %collective-permute-start.4 = (bf16[128,512]{1,0:T(8,128)(2,1)S(1)}, bf16[128,512]{1,0:T(8,128)(2,1)S(1)}, u32[]{:S(2)}, u32[]{:S(2)}) collective-permute-start(bf16[128,512]{1,0:T(8,128)(2,1)S(1)} %copy-done.40), channel_id=1, source_target_pairs={{2,0},{3,1},{4,2},{5,3},{6,4},{7,5},{8,6},{9,7},{10,8},{11,9},{12,... | collective-permute-start | bytes 393224 | tf_op jit(solution)/shard_map/ppermute | solution.py:611
  19.4 33.3 %copy-start.3 = (f32[4,512]{1,0:T(4,128)S(1)}, f32[4,512]{1,0:T(4,128)}, u32[]{:S(2)}) copy-start(f32[4,512]{1,0:T(4,128)} %get-tuple-element.93.modulation_ref) | copy-start | bytes 24580
  68.5 22.6 %collective-permute-start.6 = (bf16[1536,512]{1,0:T(8,128)(2,1)}, bf16[1536,512]{1,0:T(8,128)(2,1)}, u32[]{:S(2)}, u32[]{:S(2)}) collective-permute-start(bf16[1536,512]{1,0:T(8,128)(2,1)} %collective-permute-done.far_in), channel_id=1, source_target_pairs={{0,1},{1,0},{2,3},{3,2},{4,5},{5,4},{6,7},{7,6},{8,9},{9,8},{10,11... | collective-permute-start | bytes 4718600 | tf_op jit(solution)/shard_map/ppermute | solution.py:616
  86.6 2.7 %collective-permute-start.9 = (bf16[768,512]{1,0:T(8,128)(2,1)}, bf16[768,512]{1,0:T(8,128)(2,1)}, u32[]{:S(2)}, u32[]{:S(2)}) collective-permute-start(bf16[768,512]{1,0:T(8,128)(2,1)} %get-tuple-element.133), channel_id=1, source_target_pairs={{0,1},{1,0},{2,3},{3,2},{4,5},{5,4},{6,7},{7,6},{8,9},{9,8},{10,11... | collective-permute-start | bytes 2359304 | tf_op jit(solution)/shard_map/ppermute | solution.py:616
  87.0 3.9 %collective-permute-start.7 = (bf16[768,512]{1,0:T(8,128)(2,1)}, bf16[768,512]{1,0:T(8,128)(2,1)S(1)}, u32[]{:S(2)}, u32[]{:S(2)}) collective-permute-start(bf16[768,512]{1,0:T(8,128)(2,1)} %get-tuple-element.129), channel_id=1, source_target_pairs={{0,1},{1,0},{2,3},{3,2},{4,5},{5,4},{6,7},{7,6},{8,9},{9,8},{10,11... | collective-permute-start | bytes 2359304 | tf_op jit(solution)/shard_map/ppermute | solution.py:616
  91.1 20.4 %copy-start.16 = (bf16[1024,512]{1,0:T(8,128)(2,1)S(1)}, bf16[1024,512]{1,0:T(8,128)(2,1)}, u32[]{:S(2)}) copy-start(bf16[1024,512]{1,0:T(8,128)(2,1)} %copy-done.15) | copy-start | bytes 3145732
  91.1 20.4 %copy-start.18 = (bf16[1024,512]{1,0:T(8,128)(2,1)S(1)}, bf16[1024,512]{1,0:T(8,128)(2,1)}, u32[]{:S(2)}) copy-start(bf16[1024,512]{1,0:T(8,128)(2,1)} %copy-done.17) | copy-start | bytes 3145732
  110.9 12.9 %collective-permute-start.10 = (bf16[1024,512]{1,0:T(8,128)(2,1)}, bf16[1024,512]{1,0:T(8,128)(2,1)S(1)}, u32[]{:S(2)}, u32[]{:S(2)}) collective-permute-start(bf16[1024,512]{1,0:T(8,128)(2,1)} %get-tuple-element.135), channel_id=1, source_target_pairs={{0,1},{1,0},{2,3},{3,2},{4,5},{5,4},{6,7},{7,6},{8,9},{9,8},{10,11... | collective-permute-start | bytes 3145736 | tf_op jit(solution)/shard_map/ppermute | solution.py:616
  111.3 11.3 %collective-permute-start.8 = (bf16[768,512]{1,0:T(8,128)(2,1)}, bf16[768,512]{1,0:T(8,128)(2,1)S(1)}, u32[]{:S(2)}, u32[]{:S(2)}) collective-permute-start(bf16[768,512]{1,0:T(8,128)(2,1)} %get-tuple-element.131), channel_id=1, source_target_pairs={{0,1},{1,0},{2,3},{3,2},{4,5},{5,4},{6,7},{7,6},{8,9},{9,8},{10,11... | collective-permute-start | bytes 2359304 | tf_op jit(solution)/shard_map/ppermute | solution.py:616
  125.2 27.2 %collective-permute-start.12 = (bf16[7,128,512]{2,1,0:T(8,128)(2,1)S(1)}, bf16[7,128,512]{2,1,0:T(8,128)(2,1)}, u32[]{:S(2)}, u32[]{:S(2)}) collective-permute-start(bf16[7,128,512]{2,1,0:T(8,128)(2,1)S(1)} %pad_maximum_fusion), channel_id=1, source_target_pairs={{0,8},{1,9},{2,10},{3,11},{4,12},{5,13},{6,14},{7,15},{8,0},{9,1},... | collective-permute-start | bytes 2752520 | tf_op jit(solution)/shard_map/ppermute | solution.py:616
  127.3 23.9 %collective-permute-start.11 = (bf16[3,256,512]{2,1,0:T(8,128)(2,1)}, bf16[3,256,512]{2,1,0:T(8,128)(2,1)S(1)}, u32[]{:S(2)}, u32[]{:S(2)}) collective-permute-start(bf16[3,256,512]{2,1,0:T(8,128)(2,1)} %bitcast.4), channel_id=1, source_target_pairs={{0,2},{1,3},{2,0},{3,1},{4,6},{5,7},{6,4},{7,5},{8,10},{9,11},{10,... | collective-permute-start | bytes 2359304 | tf_op jit(solution)/shard_map/ppermute | solution.py:616
  147.4 19.5 %collective-permute-start.13 = (bf16[128,512]{1,0:T(8,128)(2,1)}, bf16[128,512]{1,0:T(8,128)(2,1)S(1)}, u32[]{:S(2)}, u32[]{:S(2)}) collective-permute-start(bf16[128,512]{1,0:T(8,128)(2,1)} %get-tuple-element.166), channel_id=1, source_target_pairs={{1,0},{2,1},{3,2},{4,3},{5,4},{6,5},{7,6},{8,7},{9,8},{10,9},{11,1... | collective-permute-start | bytes 393224 | tf_op jit(solution)/shard_map/ppermute | solution.py:611
  150.1 18.4 %collective-permute-start.14 = (bf16[128,512]{1,0:T(8,128)(2,1)}, bf16[128,512]{1,0:T(8,128)(2,1)S(1)}, u32[]{:S(2)}, u32[]{:S(2)}) collective-permute-start(bf16[128,512]{1,0:T(8,128)(2,1)} %get-tuple-element.167), channel_id=1, source_target_pairs={{31,0},{0,1},{1,2},{2,3},{3,4},{4,5},{5,6},{6,7},{7,8},{8,9},{9,10... | collective-permute-start | bytes 393224 | tf_op jit(solution)/shard_map/ppermute | solution.py:611
  150.1 20.4 %collective-permute-start.15 = (bf16[128,512]{1,0:T(8,128)(2,1)}, bf16[128,512]{1,0:T(8,128)(2,1)S(1)}, u32[]{:S(2)}, u32[]{:S(2)}) collective-permute-start(bf16[128,512]{1,0:T(8,128)(2,1)} %get-tuple-element.168), channel_id=1, source_target_pairs={{2,0},{3,1},{4,2},{5,3},{6,4},{7,5},{8,6},{9,7},{10,8},{11,9},{12,... | collective-permute-start | bytes 393224 | tf_op jit(solution)/shard_map/ppermute | solution.py:611
  151.2 19.2 %collective-permute-start.16 = (bf16[128,512]{1,0:T(8,128)(2,1)}, bf16[128,512]{1,0:T(8,128)(2,1)S(1)}, u32[]{:S(2)}, u32[]{:S(2)}) collective-permute-start(bf16[128,512]{1,0:T(8,128)(2,1)} %get-tuple-element.169), channel_id=1, source_target_pairs={{30,0},{31,1},{0,2},{1,3},{2,4},{3,5},{4,6},{5,7},{6,8},{7,9},{8,1... | collective-permute-start | bytes 393224 | tf_op jit(solution)/shard_map/ppermute | solution.py:611
  154.7 21.3 %collective-permute-start.31 = (bf16[3,128,512]{2,1,0:T(8,128)(2,1)S(1)}, bf16[3,128,512]{2,1,0:T(8,128)(2,1)S(1)}, u32[]{:S(2)}, u32[]{:S(2)}) collective-permute-start(bf16[3,128,512]{2,1,0:T(8,128)(2,1)S(1)} %constant_dynamic-slice_fusion.1), channel_id=1, source_target_pairs={{0,4},{1,5},{2,6},{3,7},{4,0},{5,1},{6,2},{7,3},{8,12},{9,13},{10,... | collective-permute-start | bytes 1179656 | tf_op jit(solution)/shard_map/ppermute | solution.py:616
  166.9 12.6 %collective-permute-start.33 = (bf16[4,128,512]{2,1,0:T(8,128)(2,1)S(1)}, bf16[4,128,512]{2,1,0:T(8,128)(2,1)S(1)}, u32[]{:S(2)}, u32[]{:S(2)}) collective-permute-start(bf16[4,128,512]{2,1,0:T(8,128)(2,1)S(1)} %slice_add_fusion), channel_id=1, source_target_pairs={{0,2},{1,3},{2,0},{3,1},{4,6},{5,7},{6,4},{7,5},{8,10},{9,11},{10,... | collective-permute-start | bytes 1572872 | tf_op jit(solution)/shard_map/ppermute | solution.py:616
  168.4 14.9 %collective-permute-start.17 = (bf16[784,512]{1,0:T(8,128)(2,1)S(1)}, bf16[784,512]{1,0:T(8,128)(2,1)S(1)}, u32[]{:S(2)}, u32[]{:S(2)}) collective-permute-start(bf16[784,512]{1,0:T(8,128)(2,1)S(1)} %pad_maximum_fusion.1), channel_id=1, source_target_pairs={{0,1},{1,0},{2,3},{3,2},{4,5},{5,4},{6,7},{7,6},{8,9},{9,8},{10,11... | collective-permute-start | bytes 2408456 | tf_op jit(solution)/shard_map/ppermute | solution.py:616
  176.2 7.1 %collective-permute-start.32 = (bf16[3,64,512]{2,1,0:T(8,128)(2,1)S(1)}, bf16[3,64,512]{2,1,0:T(8,128)(2,1)S(1)}, u32[]{:S(2)}, u32[]{:S(2)}) collective-permute-start(bf16[3,64,512]{2,1,0:T(8,128)(2,1)S(1)} %constant_dynamic-slice_fusion), channel_id=1, source_target_pairs={{0,8},{1,9},{2,10},{3,11},{4,12},{5,13},{6,14},{7,15},{8,0},{9,1},... | collective-permute-start | bytes 589832 | tf_op jit(solution)/shard_map/ppermute | solution.py:616
  179.6 7.6 %collective-permute-start.34 = (bf16[4,64,512]{2,1,0:T(8,128)(2,1)S(1)}, bf16[4,64,512]{2,1,0:T(8,128)(2,1)S(1)}, u32[]{:S(2)}, u32[]{:S(2)}) collective-permute-start(bf16[4,64,512]{2,1,0:T(8,128)(2,1)S(1)} %fusion.3), channel_id=1, source_target_pairs={{0,4},{1,5},{2,6},{3,7},{4,0},{5,1},{6,2},{7,3},{8,12},{9,13},{10,... | collective-permute-start | bytes 786440 | tf_op jit(solution)/shard_map/ppermute | solution.py:616
  183.8 14.9 %collective-permute-start.20 = (bf16[208,512]{1,0:T(8,128)(2,1)S(1)}, bf16[208,512]{1,0:T(8,128)(2,1)S(1)}, u32[]{:S(2)}, u32[]{:S(2)}) collective-permute-start(bf16[208,512]{1,0:T(8,128)(2,1)S(1)} %get-tuple-element.212), channel_id=1, source_target_pairs={{0,6},{1,7},{2,4},{3,5},{4,2},{5,3},{6,0},{7,1},{8,14},{9,15},{10,... | collective-permute-start | bytes 638984 | tf_op jit(solution)/shard_map/ppermute | solution.py:616
  187.3 22.9 %collective-permute-start.35 = (bf16[7,32,512]{2,1,0:T(8,128)(2,1)S(1)}, bf16[7,32,512]{2,1,0:T(8,128)(2,1)S(1)}, u32[]{:S(2)}, u32[]{:S(2)}) collective-permute-start(bf16[7,32,512]{2,1,0:T(8,128)(2,1)S(1)} %fusion.6), channel_id=1, source_target_pairs={{0,16},{1,17},{2,18},{3,19},{4,20},{5,21},{6,22},{7,23},{8,24},{9,... | collective-permute-start | bytes 688136 | tf_op jit(solution)/shard_map/ppermute | solution.py:616
  196.7 8.7 %collective-permute-start.18 = (bf16[208,512]{1,0:T(8,128)(2,1)S(1)}, bf16[208,512]{1,0:T(8,128)(2,1)S(1)}, u32[]{:S(2)}, u32[]{:S(2)}) collective-permute-start(bf16[208,512]{1,0:T(8,128)(2,1)S(1)} %get-tuple-element.210), channel_id=1, source_target_pairs={{0,2},{1,3},{2,0},{3,1},{4,6},{5,7},{6,4},{7,5},{8,10},{9,11},{10,... | collective-permute-start | bytes 638984 | tf_op jit(solution)/shard_map/ppermute | solution.py:616
  198.7 6.7 %collective-permute-start.19 = (bf16[208,512]{1,0:T(8,128)(2,1)S(1)}, bf16[208,512]{1,0:T(8,128)(2,1)S(1)}, u32[]{:S(2)}, u32[]{:S(2)}) collective-permute-start(bf16[208,512]{1,0:T(8,128)(2,1)S(1)} %get-tuple-element.211), channel_id=1, source_target_pairs={{0,4},{1,5},{2,6},{3,7},{4,0},{5,1},{6,2},{7,3},{8,12},{9,13},{10,... | collective-permute-start | bytes 638984 | tf_op jit(solution)/shard_map/ppermute | solution.py:616
  205.7 25.6 %copy-start.36 = (bf16[16,2048]{1,0:T(8,128)(2,1)S(1)}, bf16[16,2048]{1,0:T(8,128)(2,1)}, u32[]{:S(2)}) copy-start(bf16[16,2048]{1,0:T(8,128)(2,1)} %mod_w_ref.1) | copy-start | bytes 196612
  205.7 25.6 %copy-start.38 = (f32[16]{0:T(128)S(1)}, f32[16]{0:T(128)}, u32[]{:S(2)}) copy-start(f32[16]{0:T(128)} %condition_ref.1) | copy-start | bytes 196
  205.8 4.6 %collective-permute-start.21 = (bf16[64,512]{1,0:T(8,128)(2,1)S(1)}, bf16[64,512]{1,0:T(8,128)(2,1)S(1)}, u32[]{:S(2)}, u32[]{:S(2)}) collective-permute-start(bf16[64,512]{1,0:T(8,128)(2,1)S(1)} %get-tuple-element.207), channel_id=1, source_target_pairs={{0,8},{1,9},{2,10},{3,11},{4,12},{5,13},{6,14},{7,15},{8,0},{9,1},... | collective-permute-start | bytes 196616 | tf_op jit(solution)/shard_map/ppermute | solution.py:616
  205.9 13.2 %collective-permute-start.22 = (bf16[64,512]{1,0:T(8,128)(2,1)S(1)}, bf16[64,512]{1,0:T(8,128)(2,1)S(1)}, u32[]{:S(2)}, u32[]{:S(2)}) collective-permute-start(bf16[64,512]{1,0:T(8,128)(2,1)S(1)} %get-tuple-element.208), channel_id=1, source_target_pairs={{0,16},{1,17},{2,18},{3,19},{4,20},{5,21},{6,22},{7,23},{8,24},{9,... | collective-permute-start | bytes 196616 | tf_op jit(solution)/shard_map/ppermute | solution.py:616
  207.0 12.1 %collective-permute-start.23 = (bf16[64,512]{1,0:T(8,128)(2,1)S(1)}, bf16[64,512]{1,0:T(8,128)(2,1)S(1)}, u32[]{:S(2)}, u32[]{:S(2)}) collective-permute-start(bf16[64,512]{1,0:T(8,128)(2,1)S(1)} %get-tuple-element.209), channel_id=1, source_target_pairs={{0,24},{1,25},{2,26},{3,27},{4,28},{5,29},{6,30},{7,31},{8,16},{9,... | collective-permute-start | bytes 196616 | tf_op jit(solution)/shard_map/ppermute | solution.py:616
  210.3 22.4 %collective-permute-start.36 = (bf16[7,32,512]{2,1,0:T(8,128)(2,1)S(1)}, bf16[7,32,512]{2,1,0:T(8,128)(2,1)S(1)}, u32[]{:S(2)}, u32[]{:S(2)}) collective-permute-start(bf16[7,32,512]{2,1,0:T(8,128)(2,1)S(1)} %fusion.8), channel_id=1, source_target_pairs={{0,16},{1,17},{2,18},{3,19},{4,20},{5,21},{6,22},{7,23},{8,24},{9,... | collective-permute-start | bytes 688136 | tf_op jit(solution)/shard_map/ppermute | solution.py:616
  219.1 6.6 %collective-permute-start.24 = (bf16[3,16,512]{2,1,0:T(8,128)(2,1)S(1)}, bf16[3,16,512]{2,1,0:T(8,128)(2,1)S(1)}, u32[]{:S(2)}, u32[]{:S(2)}) collective-permute-start(bf16[3,16,512]{2,1,0:T(8,128)(2,1)S(1)} %fusion.9), channel_id=1, source_target_pairs={{0,8},{1,9},{2,10},{3,11},{4,12},{5,13},{6,14},{7,15},{8,0},{9,1},... | collective-permute-start | bytes 147464 | tf_op jit(solution)/shard_map/ppermute | solution.py:616
  221.5 6.2 %collective-permute-start.25 = (bf16[3,16,512]{2,1,0:T(8,128)(2,1)S(1)}, bf16[3,16,512]{2,1,0:T(8,128)(2,1)S(1)}, u32[]{:S(2)}, u32[]{:S(2)}) collective-permute-start(bf16[3,16,512]{2,1,0:T(8,128)(2,1)S(1)} %fusion.9), channel_id=1, source_target_pairs={{0,16},{1,17},{2,18},{3,19},{4,20},{5,21},{6,22},{7,23},{8,24},{9,... | collective-permute-start | bytes 147464 | tf_op jit(solution)/shard_map/ppermute | solution.py:616
  221.5 6.2 %collective-permute-start.26 = (bf16[3,16,512]{2,1,0:T(8,128)(2,1)S(1)}, bf16[3,16,512]{2,1,0:T(8,128)(2,1)S(1)}, u32[]{:S(2)}, u32[]{:S(2)}) collective-permute-start(bf16[3,16,512]{2,1,0:T(8,128)(2,1)S(1)} %fusion.9), channel_id=1, source_target_pairs={{0,24},{1,25},{2,26},{3,27},{4,28},{5,29},{6,30},{7,31},{8,16},{9,... | collective-permute-start | bytes 147464 | tf_op jit(solution)/shard_map/ppermute | solution.py:616
  227.8 7.2 %collective-permute-start.27 = (bf16[3,64,512]{2,1,0:T(8,128)(2,1)S(1)}, bf16[3,64,512]{2,1,0:T(8,128)(2,1)S(1)}, u32[]{:S(2)}, u32[]{:S(2)}) collective-permute-start(bf16[3,64,512]{2,1,0:T(8,128)(2,1)S(1)} %pad_maximum_fusion.12), channel_id=1, source_target_pairs={{0,2},{1,3},{2,0},{3,1},{4,6},{5,7},{6,4},{7,5},{8,10},{9,11},{10,... | collective-permute-start | bytes 589832 | tf_op jit(solution)/shard_map/ppermute | solution.py:616
  228.9 10.5 %collective-permute-start.28 = (bf16[3,64,512]{2,1,0:T(8,128)(2,1)S(1)}, bf16[3,64,512]{2,1,0:T(8,128)(2,1)S(1)}, u32[]{:S(2)}, u32[]{:S(2)}) collective-permute-start(bf16[3,64,512]{2,1,0:T(8,128)(2,1)S(1)} %pad_maximum_fusion.12), channel_id=1, source_target_pairs={{0,4},{1,5},{2,6},{3,7},{4,0},{5,1},{6,2},{7,3},{8,12},{9,13},{10,... | collective-permute-start | bytes 589832 | tf_op jit(solution)/shard_map/ppermute | solution.py:616
  228.9 10.5 %collective-permute-start.29 = (bf16[3,64,512]{2,1,0:T(8,128)(2,1)S(1)}, bf16[3,64,512]{2,1,0:T(8,128)(2,1)S(1)}, u32[]{:S(2)}, u32[]{:S(2)}) collective-permute-start(bf16[3,64,512]{2,1,0:T(8,128)(2,1)S(1)} %pad_maximum_fusion.12), channel_id=1, source_target_pairs={{0,6},{1,7},{2,4},{3,5},{4,2},{5,3},{6,0},{7,1},{8,14},{9,15},{10,... | collective-permute-start | bytes 589832 | tf_op jit(solution)/shard_map/ppermute | solution.py:616
  232.9 6.8 %collective-permute-start.40 = (bf16[3,64,512]{2,1,0:T(8,128)(2,1)S(1)}, bf16[3,64,512]{2,1,0:T(8,128)(2,1)S(1)}, u32[]{:S(2)}, u32[]{:S(2)}) collective-permute-start(bf16[3,64,512]{2,1,0:T(8,128)(2,1)S(1)} %slice.185), channel_id=1, source_target_pairs={{0,8},{1,9},{2,10},{3,11},{4,12},{5,13},{6,14},{7,15},{8,0},{9,1},... | collective-permute-start | bytes 589832 | tf_op jit(solution)/shard_map/ppermute | solution.py:616
  234.1 11.0 %collective-permute-start.37 = (bf16[4,64,512]{2,1,0:T(8,128)(2,1)S(1)}, bf16[4,64,512]{2,1,0:T(8,128)(2,1)S(1)}, u32[]{:S(2)}, u32[]{:S(2)}) collective-permute-start(bf16[4,64,512]{2,1,0:T(8,128)(2,1)S(1)} %slice.183), channel_id=1, source_target_pairs={{0,4},{1,5},{2,6},{3,7},{4,0},{5,1},{6,2},{7,3},{8,12},{9,13},{10,... | collective-permute-start | bytes 786440 | tf_op jit(solution)/shard_map/ppermute | solution.py:616
  239.8 12.3 %collective-permute-start.41 = (bf16[3,128,512]{2,1,0:T(8,128)(2,1)S(1)}, bf16[3,128,512]{2,1,0:T(8,128)(2,1)S(1)}, u32[]{:S(2)}, u32[]{:S(2)}) collective-permute-start(bf16[3,128,512]{2,1,0:T(8,128)(2,1)S(1)} %maximum_select_fusion.5), channel_id=1, source_target_pairs={{0,4},{1,5},{2,6},{3,7},{4,0},{5,1},{6,2},{7,3},{8,12},{9,13},{10,... | collective-permute-start | bytes 1179656 | tf_op jit(solution)/shard_map/ppermute | solution.py:616
  245.3 11.2 %collective-permute-start.38 = (bf16[4,128,512]{2,1,0:T(8,128)(2,1)S(1)}, bf16[4,128,512]{2,1,0:T(8,128)(2,1)S(1)}, u32[]{:S(2)}, u32[]{:S(2)}) collective-permute-start(bf16[4,128,512]{2,1,0:T(8,128)(2,1)S(1)} %maximum_select_fusion.2), channel_id=1, source_target_pairs={{0,8},{1,9},{2,10},{3,11},{4,12},{5,13},{6,14},{7,15},{8,0},{9,1},... | collective-permute-start | bytes 1572872 | tf_op jit(solution)/shard_map/ppermute | solution.py:616
  247.6 11.4 %collective-permute-start.30 = (bf16[3,256,512]{2,1,0:T(8,128)(2,1)S(1)}, bf16[3,256,512]{2,1,0:T(8,128)(2,1)S(1)}, u32[]{:S(2)}, u32[]{:S(2)}) collective-permute-start(bf16[3,256,512]{2,1,0:T(8,128)(2,1)S(1)} %pad_maximum_fusion.2), channel_id=1, source_target_pairs={{0,1},{1,0},{2,3},{3,2},{4,5},{5,4},{6,7},{7,6},{8,9},{9,8},{10,11... | collective-permute-start | bytes 2359304 | tf_op jit(solution)/shard_map/ppermute | solution.py:616
  257.0 4.2 %collective-permute-start.39 = (bf16[1,256,512]{2,1,0:T(8,128)(2,1)S(1)}, bf16[1,256,512]{2,1,0:T(8,128)(2,1)S(1)}, u32[]{:S(2)}, u32[]{:S(2)}) collective-permute-start(bf16[1,256,512]{2,1,0:T(8,128)(2,1)S(1)} %get-tuple-element.194), channel_id=1, source_target_pairs={{0,1},{1,0},{2,3},{3,2},{4,5},{5,4},{6,7},{7,6},{8,9},{9,8},{10,11... | collective-permute-start | bytes 786440 | tf_op jit(solution)/shard_map/ppermute | solution.py:616
  (37 other events, 191.8 us)
